TPU v7x, 512 devices: a whole 4x8x8 slice. The times are simulated.
512 devices in a mesh: gx: 32 (over y_hi, z, core), gy: 16 (over y_lo, x).
Axes of the slice: x: 4, y: 8 (y_hi: 2, y_lo: 4; y = y_hi * 4 + y_lo), z: 8, core: 2. Of those that a mesh axis runs over, the one named last changes fastest.
Arguments:
- positions: float32 [32, 16, 3, 128], P('gx', 'gy'), may hold values from 0 to 1
- species: int32 [32, 16, 128], P('gx', 'gy'), may hold values from 0 to 1
- neighbours: int32 [32, 16, 128, 8], P('gx', 'gy'), may hold values from 0 to 383, as said below
- counts: int32 [32, 16, 128], P('gx', 'gy'), may hold values from 1 to 8, as said below
- image_z: int32 [32, 16, 128, 8], P('gx', 'gy'), may hold values from -1 to 1
- send_lists: int32 [32, 16, 256], P('gx', 'gy'), may hold values from 0 to 127, as said below
- w_basis: float32 [8, 128], replicated, may hold values from -2 to 2
- w_center: float32 [2, 128], replicated, may hold values from -3 to 3
- w_neigh: float32 [2, 128], replicated, may hold values from -3 to 3
- w_env: float32 [128, 32], replicated, may hold values from -0.5 to 0.5
- w_latent: float32 [128, 128], replicated, may hold values from -0.5 to 0.5
- w_tensor: float32 [2, 32, 128], replicated, may hold values from -0.75 to 0.75
- w_out: float32 [128], replicated, may hold values from -0.5 to 0.5
Outputs:
- forces: float32 [32, 16, 3, 128], P('gx', 'gy')
- atom_energy: float32 [32, 16, 128], P('gx', 'gy')
Inputs may be any that keep to these rules, and one draw needn't show every extreme that they name: `neighbours`: slots below 128 name another own atom of the box, never the atom itself; slots from 128 name ghost slots in the order of the ghost blocks. Padded slots hold indices of the same kind. `counts`: in every box some atom has all 8 slots live. `send_lists`: each of the four blocks (128, 64, 32, 32 entries) lists distinct atoms of the sending box.
All inputs are finite; a program needn't handle non-finite values.
Results may differ from a plain program's by a relative error of at most 0.00011.
Values sent between devices are 32-bit elements; how exact they have to be, the bound alone decides.
No kernel may reach another device: no remote copies, remote signals or barrier semaphores. Data moves between devices by JAX's collectives and lax.ppermute only.
A program may use at most 64 MiB of HBM per device.

v0:
```python
import jax
import jax.numpy as jnp
from jax import lax
from jax.sharding import PartitionSpec as P

PRECISE = lax.Precision.HIGHEST
SOFTEN = 0.25
ENV_SCALE = 0.25


def from_behind(block, axis, distance):
    devices = range(lax.axis_size(axis))
    route = [((i - distance) % len(devices), i) for i in devices]
    return lax.ppermute(block, axis, route)


def product(left, right):
    return jnp.dot(left, right, precision=PRECISE, preferred_element_type=jnp.float32)


def first_layer(
    pos_table, spec_table, neigh_idx, live_mask, image_lift, w_basis, w_center, w_neigh, w_env
):
    atom_count, slot_count = neigh_idx.shape
    flat_idx = neigh_idx.reshape(-1)
    centre = jnp.broadcast_to(
        pos_table[:atom_count][:, None, :], (atom_count, slot_count, 3)
    ).reshape(-1, 3)
    lift_z = image_lift.reshape(-1).astype(jnp.float32)
    zero_col = jnp.zeros_like(lift_z)
    displace = pos_table[flat_idx] - centre + jnp.stack([zero_col, zero_col, lift_z], axis=1)
    radius_sq = jnp.sum(displace * displace, axis=1) + SOFTEN
    radius = jnp.sqrt(radius_sq)
    unit_vec = displace / radius[:, None]
    envelope = live_mask * jnp.exp(-0.25 * radius_sq)
    nbasis = w_basis.shape[0]
    centres = 0.5 + 2.5 * jnp.arange(nbasis).astype(jnp.float32) / (nbasis - 1)
    basis_val = jnp.exp(-jnp.square((radius[:, None] - centres[None, :]) / 0.5))
    spec_c = jnp.broadcast_to(spec_table[:atom_count][:, None], (atom_count, slot_count)).reshape(
        -1
    )
    spec_n = spec_table[flat_idx]
    pre_act = (
        product(basis_val, w_basis) + w_center[0] + spec_c[:, None] * (w_center[1] - w_center[0])
    )
    pre_act = pre_act + w_neigh[0] + spec_n[:, None] * (w_neigh[1] - w_neigh[0])
    latent = jax.nn.silu(pre_act)
    weight_env = product(latent, w_env) * envelope[:, None]
    to_centre = jnp.concatenate(
        [weight_env] + [weight_env * unit_vec[:, comp : comp + 1] for comp in range(3)], axis=1
    )
    to_neigh = jnp.concatenate(
        [weight_env] + [-weight_env * unit_vec[:, comp : comp + 1] for comp in range(3)], axis=1
    )
    own_part = to_centre.reshape(atom_count, slot_count, -1).sum(axis=1)
    env_part = jax.ops.segment_sum(to_neigh, flat_idx, num_segments=pos_table.shape[0])
    env_part = env_part.at[:atom_count].add(own_part)
    return (ENV_SCALE * env_part, latent, unit_vec, envelope)


def second_layer(latent, unit_vec, envelope, env_all, neigh_idx, w_latent, w_tensor, w_out):
    atom_count, slot_count = neigh_idx.shape
    flat_idx = neigh_idx.reshape(-1)
    env_width = env_all.shape[1]
    channels = env_width // 4
    env_c = jnp.broadcast_to(
        env_all[:atom_count][:, None, :], (atom_count, slot_count, env_width)
    ).reshape(-1, env_width)
    env_n = env_all[flat_idx]
    proj_c = env_c[:, :channels]
    proj_n = env_n[:, :channels]
    for comp in range(3):
        lower = (comp + 1) * channels
        proj_c = proj_c + env_c[:, lower : lower + channels] * unit_vec[:, comp : comp + 1]
        proj_n = proj_n - env_n[:, lower : lower + channels] * unit_vec[:, comp : comp + 1]
    hidden = jax.nn.silu(
        product(latent, w_latent) + product(proj_c, w_tensor[0]) + product(proj_n, w_tensor[1])
    )
    return envelope * product(latent + hidden, w_out)


def energy_split(edge_energy, neigh_idx, total_slots):
    atom_count, slot_count = neigh_idx.shape
    half_edge = 0.5 * edge_energy
    shares = jax.ops.segment_sum(half_edge, neigh_idx.reshape(-1), num_segments=total_slots)
    return shares.at[:atom_count].add(half_edge.reshape(atom_count, slot_count).sum(axis=1))


def move_x_direct(values, steps):
    return from_behind(values, "gx", steps)


def move_y_direct(values, steps):
    return from_behind(values, "gy", steps)


def direct_out(packet, block_cuts):
    cut_one, cut_two, cut_three = block_cuts
    face_x = move_x_direct(packet[:cut_one], -1)
    face_y = move_y_direct(packet[cut_one:cut_two], -1)
    corner_up = move_y_direct(move_x_direct(packet[cut_two:cut_three], -1), -1)
    corner_down = move_y_direct(move_x_direct(packet[cut_three:], -1), 1)
    return jnp.concatenate([face_x, face_y, corner_up, corner_down], axis=0)


def direct_in(ghost, block_cuts):
    cut_one, cut_two, cut_three = block_cuts
    face_x = move_x_direct(ghost[:cut_one], 1)
    face_y = move_y_direct(ghost[cut_one:cut_two], 1)
    corner_up = move_x_direct(move_y_direct(ghost[cut_two:cut_three], 1), 1)
    corner_down = move_x_direct(move_y_direct(ghost[cut_three:], -1), 1)
    return jnp.concatenate([face_x, face_y, corner_up, corner_down], axis=0)


def gather_back(values, sends, atom_count):
    return jnp.zeros((atom_count, values.shape[1]), jnp.float32).at[sends].add(values)


def ghost_offsets(block_cuts, total_ghosts):
    cut_one, cut_two, cut_three = block_cuts
    rows = [
        (cut_one, (1.0, 0.0, 0.0)),
        (cut_two - cut_one, (0.0, 1.0, 0.0)),
        (cut_three - cut_two, (1.0, 1.0, 0.0)),
        (total_ghosts - cut_three, (1.0, -1.0, 0.0)),
    ]
    return jnp.concatenate(
        [
            jnp.broadcast_to(jnp.array(shift_vec, jnp.float32)[None, :], (length, 3))
            for length, shift_vec in rows
        ],
        axis=0,
    )


def local(
    positions,
    species,
    neighbours,
    counts,
    image_z,
    send_lists,
    w_basis,
    w_center,
    w_neigh,
    w_env,
    w_latent,
    w_tensor,
    w_out,
):
    atom_count = positions.shape[3]
    slot_count = neighbours.shape[3]
    total_ghosts = send_lists.shape[2]
    block_cuts = (
        atom_count,
        atom_count + atom_count // 2,
        atom_count + atom_count // 2 + atom_count // 4,
    )
    pos_rows = positions[0, 0].T
    spec_rows = species[0, 0].astype(jnp.float32)
    neigh_idx = neighbours[0, 0]
    image_lift = image_z[0, 0]
    sends = send_lists[0, 0]
    live_mask = (
        (jnp.arange(slot_count)[None, :] < counts[0, 0][:, None]).astype(jnp.float32).reshape(-1)
    )
    own_table = jnp.concatenate([pos_rows, spec_rows[:, None]], axis=1)
    ghost_table = direct_out(own_table[sends], block_cuts)
    table_pos = jnp.concatenate(
        [pos_rows, ghost_table[:, :3] + ghost_offsets(block_cuts, total_ghosts)], axis=0
    )
    table_species = jnp.concatenate([spec_rows, ghost_table[:, 3]], axis=0)

    def layer_pos(pos_table):
        return first_layer(
            pos_table,
            table_species,
            neigh_idx,
            live_mask,
            image_lift,
            w_basis,
            w_center,
            w_neigh,
            w_env,
        )

    outputs, pull_first = jax.vjp(layer_pos, table_pos)
    env_part, latent, unit_vec, envelope = outputs
    env_own = env_part[:atom_count] + gather_back(
        direct_in(env_part[atom_count:], block_cuts), sends, atom_count
    )
    env_all = jnp.concatenate([env_own, direct_out(env_own[sends], block_cuts)], axis=0)

    def energy_fn(latent_in, unit_in, envelope_in, env_in):
        return second_layer(
            latent_in, unit_in, envelope_in, env_in, neigh_idx, w_latent, w_tensor, w_out
        )

    edge_energy, pull_second = jax.vjp(energy_fn, latent, unit_vec, envelope, env_all)
    grad_latent, grad_unit, grad_envelope, grad_env = pull_second(jnp.ones_like(edge_energy))
    energy_part = energy_split(edge_energy, neigh_idx, atom_count + total_ghosts)
    grad_own = grad_env[:atom_count] + gather_back(
        direct_in(grad_env[atom_count:], block_cuts), sends, atom_count
    )
    grad_all = jnp.concatenate([grad_own, direct_out(grad_own[sends], block_cuts)], axis=0)
    grad_pos = pull_first((grad_all, grad_latent, grad_unit, grad_envelope))[0]
    returned = jnp.concatenate([grad_pos[atom_count:], energy_part[atom_count:, None]], axis=1)
    settled = gather_back(direct_in(returned, block_cuts), sends, atom_count)
    forces = -(grad_pos[:atom_count] + settled[:, :3])
    atom_energy = energy_part[:atom_count] + settled[:, 3]
    return (forces.T[None, None], atom_energy[None, None])


def solution(mesh):
    return jax.shard_map(
        local,
        mesh=mesh,
        in_specs=(
            P("gx", "gy", None, None),
            P("gx", "gy", None),
            P("gx", "gy", None, None),
            P("gx", "gy", None),
            P("gx", "gy", None, None),
            P("gx", "gy", None),
            P(),
            P(),
            P(),
            P(),
            P(),
            P(),
            P(),
        ),
        out_specs=(P("gx", "gy", None, None), P("gx", "gy", None)),
        check_vma=False,
    )
```

profile of v0, /device:TPU:30, one launch (start us, length us, event | category | flops | bytes accessed | tf_op | source)
XLA Modules:
  0.0 281.1 jit_solution(4304300009670202908)
XLA Ops:
  3.1 13.0 %collective-permute-start.2 = (f32[32,4]{1,0:T(8,128)S(1)}, f32[32,4]{1,0:T(8,128)S(1)}, u32[]{:S(2)}, u32[]{:S(2)}) collective-permute-start(f32[32,4]{1,0:T(8,128)S(1)} %get-tuple-element.98), channel_id=1, source_target_pairs={{16,0},{32,16},{48,32},{64,48},{80,64},{96,80},{112,96},{128,112},... | collective-permute-start | bytes 1544 | tf_op jit(solution)/shard_map/ppermute | solution.py:14
  16.1 2.6 collective-permute-start.4
  18.7 2.7 collective-permute-start.1
  21.4 1.9 collective-permute-start
  25.6 2.4 collective-permute-start.3
  28.1 7.3 %collective-permute-start.5 = (f32[32,4]{1,0:T(8,128)S(1)}, f32[32,4]{1,0:T(8,128)S(1)}, u32[]{:S(2)}, u32[]{:S(2)}) collective-permute-start(f32[32,4]{1,0:T(8,128)S(1)} %collective-permute-done.4), channel_id=1, source_target_pairs={{15,0},{0,1},{1,2},{2,3},{3,4},{4,5},{5,6},{6,7},{7,8},{8,9},{9,10... | collective-permute-start | bytes 1544 | tf_op jit(solution)/shard_map/ppermute | solution.py:14
  40.1 6.9 %gather_fusion.2 = f32[1024]{0:T(1024)S(1)} fusion(f32[384]{0:T(512)S(1)} %pad_maximum_fusion.7, s32[1024]{0:T(1024)S(1)} %get-tuple-element.119), kind=kCustom, calls=%fused_computation.2 | custom fusion | bytes 12288 | tf_op jit(solution)/shard_map/jvp()/gather | solution.py:42
  47.0 2.8 gather_fusion.1
  56.5 6.1 %scatter_custom_fusion = f32[384,128]{1,0:T(8,128)S(1)} fusion(s32[1024]{0:T(1024)S(1)} %reshape.337, f32[1024,128]{1,0:T(8,128)S(1)} %copy.115, f32[]{:T(128)} %constant.93.clone.1), kind=kCustom, calls=%fused_computation.120 | custom fusion | flops 131072 | bytes 196612 | tf_op jit(solution)/shard_map/jvp()/scatter-add | solution.py:56
  62.6 8.1 %collective-permute-start.8 = (f32[32,128]{1,0:T(8,128)S(1)}, f32[32,128]{1,0:T(8,128)S(1)}, u32[]{:S(2)}, u32[]{:S(2)}) collective-permute-start(f32[32,128]{1,0:T(8,128)S(1)} %get-tuple-element.77), channel_id=1, source_target_pairs={{15,0},{0,1},{1,2},{2,3},{3,4},{4,5},{5,6},{6,7},{7,8},{8,9},{9,10... | collective-permute-start | bytes 49160 | tf_op jit(solution)/shard_map/ppermute | solution.py:14
  70.7 1.9 collective-permute-start.10
  72.7 7.8 %collective-permute-start.7 = (f32[64,128]{1,0:T(8,128)S(1)}, f32[64,128]{1,0:T(8,128)S(1)}, u32[]{:S(2)}, u32[]{:S(2)}) collective-permute-start(f32[64,128]{1,0:T(8,128)S(1)} %slice.282), channel_id=1, source_target_pairs={{15,0},{0,1},{1,2},{2,3},{3,4},{4,5},{5,6},{6,7},{7,8},{8,9},{9,10... | collective-permute-start | bytes 98312 | tf_op jit(solution)/shard_map/ppermute | solution.py:14
  82.5 3.2 %collective-permute-start.9 = (f32[32,128]{1,0:T(8,128)S(1)}, f32[32,128]{1,0:T(8,128)S(1)}, u32[]{:S(2)}, u32[]{:S(2)}) collective-permute-start(f32[32,128]{1,0:T(8,128)S(1)} %collective-permute-done.8), channel_id=1, source_target_pairs={{496,0},{0,16},{16,32},{32,48},{48,64},{64,80},{80,96},{96,112},{1... | collective-permute-start | bytes 49160 | tf_op jit(solution)/shard_map/ppermute | solution.py:14
  85.7 1.9 collective-permute-start.11
  88.3 5.3 %collective-permute-done.9 = f32[32,128]{1,0:T(8,128)S(1)} collective-permute-done((f32[32,128]{1,0:T(8,128)S(1)}, f32[32,128]{1,0:T(8,128)S(1)}, u32[]{:S(2)}, u32[]{:S(2)}) %collective-permute-start.9) | collective-permute-done | bytes 16416 | tf_op jit(solution)/shard_map/ppermute | solution.py:14
  93.5 3.2 %collective-permute-done.11 = f32[32,128]{1,0:T(8,128)S(1)} collective-permute-done((f32[32,128]{1,0:T(8,128)S(1)}, f32[32,128]{1,0:T(8,128)S(1)}, u32[]{:S(2)}, u32[]{:S(2)}) %collective-permute-start.11) | collective-permute-done | bytes 16416 | tf_op jit(solution)/shard_map/ppermute | solution.py:14
  96.8 2.0 scatter_custom_fusion.1
  100.8 1.9 collective-permute-start.16
  102.7 2.9 %collective-permute-start.14 = (f32[32,128]{1,0:T(8,128)}, f32[32,128]{1,0:T(8,128)}, u32[]{:S(2)}, u32[]{:S(2)}) collective-permute-start(f32[32,128]{1,0:T(8,128)} %get-tuple-element.92), channel_id=1, source_target_pairs={{16,0},{32,16},{48,32},{64,48},{80,64},{96,80},{112,96},{128,112},... | collective-permute-start | bytes 49160 | tf_op jit(solution)/shard_map/ppermute | solution.py:14
  105.6 1.9 collective-permute-start.13
  107.5 1.9 collective-permute-start.12
  113.0 8.0 %collective-permute-start.17 = (f32[32,128]{1,0:T(8,128)}, f32[32,128]{1,0:T(8,128)S(1)}, u32[]{:S(2)}, u32[]{:S(2)}) collective-permute-start(f32[32,128]{1,0:T(8,128)} %collective-permute-done.16), channel_id=1, source_target_pairs={{15,0},{0,1},{1,2},{2,3},{3,4},{4,5},{5,6},{6,7},{7,8},{8,9},{9,10... | collective-permute-start | bytes 49160 | tf_op jit(solution)/shard_map/ppermute | solution.py:14
  124.6 6.2 %collective-permute-done.15 = f32[32,128]{1,0:T(8,128)S(1)} collective-permute-done((f32[32,128]{1,0:T(8,128)}, f32[32,128]{1,0:T(8,128)S(1)}, u32[]{:S(2)}, u32[]{:S(2)}) %collective-permute-start.15) | collective-permute-done | bytes 16416 | tf_op jit(solution)/shard_map/ppermute | solution.py:14
  130.8 2.8 gather_fusion.4
  140.4 6.1 %scatter_fusion = f32[384,128]{1,0:T(8,128)S(1)} fusion(f32[384,128]{1,0:T(8,128)S(1)} %pad.81, s32[1024]{0:T(1024)S(1)} %bitcast.95, f32[1024,128]{1,0:T(8,128)S(1)} %copy.133), kind=kCustom, calls=%fused_computation.9 | custom fusion | flops 131072 | bytes 1576960 | tf_op jit(solution)/shard_map/transpose(jvp())/scatter-add | solution.py:69
  146.6 1.9 collective-permute-start.20
  148.5 3.9 %collective-permute-start.22 = (f32[32,128]{1,0:T(8,128)S(1)}, f32[32,128]{1,0:T(8,128)}, u32[]{:S(2)}, u32[]{:S(2)}) collective-permute-start(f32[32,128]{1,0:T(8,128)S(1)} %get-tuple-element.74), channel_id=1, source_target_pairs={{1,0},{2,1},{3,2},{4,3},{5,4},{6,5},{7,6},{8,7},{9,8},{10,9},{11,1... | collective-permute-start | bytes 49160 | tf_op jit(solution)/shard_map/ppermute | solution.py:14
  152.5 5.8 %collective-permute-start.19 = (f32[64,128]{1,0:T(8,128)S(1)}, f32[64,128]{1,0:T(8,128)S(1)}, u32[]{:S(2)}, u32[]{:S(2)}) collective-permute-start(f32[64,128]{1,0:T(8,128)S(1)} %slice.299), channel_id=1, source_target_pairs={{15,0},{0,1},{1,2},{2,3},{3,4},{4,5},{5,6},{6,7},{7,8},{8,9},{9,10... | collective-permute-start | bytes 98312 | tf_op jit(solution)/shard_map/ppermute | solution.py:14
  160.2 3.2 %collective-permute-start.21 = (f32[32,128]{1,0:T(8,128)}, f32[32,128]{1,0:T(8,128)S(1)}, u32[]{:S(2)}, u32[]{:S(2)}) collective-permute-start(f32[32,128]{1,0:T(8,128)} %collective-permute-done.20), channel_id=1, source_target_pairs={{496,0},{0,16},{16,32},{32,48},{48,64},{64,80},{80,96},{96,112},{1... | collective-permute-start | bytes 49160 | tf_op jit(solution)/shard_map/ppermute | solution.py:14
  169.0 2.6 collective-permute-done.21
  171.5 3.2 %collective-permute-done.23 = f32[32,128]{1,0:T(8,128)S(1)} collective-permute-done((f32[32,128]{1,0:T(8,128)}, f32[32,128]{1,0:T(8,128)S(1)}, u32[]{:S(2)}, u32[]{:S(2)}) %collective-permute-start.23) | collective-permute-done | bytes 16416 | tf_op jit(solution)/shard_map/ppermute | solution.py:14
  174.7 2.1 scatter_custom_fusion.3
  177.8 3.9 %collective-permute-start.28 = (f32[32,128]{1,0:T(8,128)S(1)}, f32[32,128]{1,0:T(8,128)S(1)}, u32[]{:S(2)}, u32[]{:S(2)}) collective-permute-start(f32[32,128]{1,0:T(8,128)S(1)} %get-tuple-element.89), channel_id=1, source_target_pairs={{16,0},{32,16},{48,32},{64,48},{80,64},{96,80},{112,96},{128,112},... | collective-permute-start | bytes 49160 | tf_op jit(solution)/shard_map/ppermute | solution.py:14
  183.6 2.9 %collective-permute-start.24 = (f32[128,128]{1,0:T(8,128)S(1)}, f32[128,128]{1,0:T(8,128)S(1)}, u32[]{:S(2)}, u32[]{:S(2)}) collective-permute-start(f32[128,128]{1,0:T(8,128)S(1)} %slice.302), channel_id=1, source_target_pairs={{16,0},{32,16},{48,32},{64,48},{80,64},{96,80},{112,96},{128,112},... | collective-permute-start | bytes 196616 | tf_op jit(solution)/shard_map/ppermute | solution.py:14
  188.4 7.8 %collective-permute-start.29 = (f32[32,128]{1,0:T(8,128)S(1)}, f32[32,128]{1,0:T(8,128)S(1)}, u32[]{:S(2)}, u32[]{:S(2)}) collective-permute-start(f32[32,128]{1,0:T(8,128)S(1)} %collective-permute-done.28), channel_id=1, source_target_pairs={{15,0},{0,1},{1,2},{2,3},{3,4},{4,5},{5,6},{6,7},{7,8},{8,9},{9,10... | collective-permute-start | bytes 49160 | tf_op jit(solution)/shard_map/ppermute | solution.py:14
  196.3 2.1 collective-permute-start.27
  198.5 7.3 %collective-permute-done.27 = f32[32,128]{1,0:T(8,128)S(1)} collective-permute-done((f32[32,128]{1,0:T(8,128)S(1)}, f32[32,128]{1,0:T(8,128)S(1)}, u32[]{:S(2)}, u32[]{:S(2)}) %collective-permute-start.27) | collective-permute-done | bytes 16416 | tf_op jit(solution)/shard_map/ppermute | solution.py:14
  206.5 4.0 %gather_fusion.6 = f32[1024,128]{1,0:T(8,128)} fusion(f32[384,128]{1,0:T(8,128)S(1)} %broadcast_multiply_fusion, s32[1024]{0:T(1024)S(1)} %copy-done.27), kind=kCustom, calls=%fused_computation.6 | custom fusion | bytes 1052672 | tf_op jit(solution)/shard_map/transpose(jvp())/gather | solution.py:56
  210.6 2.1 copy.134
  231.3 3.6 %multiply_reduce_fusion = (f32[1024]{0:T(1024)S(1)}, f32[1024,3]{1,0:T(8,128)S(1)}) fusion(f32[1024,3]{1,0:T(8,128)S(1)} %get-tuple-element.56, f32[1024]{0:T(1024)S(1)} %copy-done.23, f32[1024,1]{1,0:T(8,128)} %copy.143, f32[1024,1]{1,0:T(8,128)} %copy.141, f32[1024,1]{1,0:T(8,128)} %copy.139, f32[1024,1]{1,0:T(8,128)} %copy.137, f32[1024,1]{1,0:T(8,128)} %copy.136, ...), kind=kLoop, calls=%fused_computation.50 | loop fusion | flops 41984 | bytes 81920 | tf_op jit(solution)/shard_map/transpose(jvp())/reduce_sum | solution.py:34
  235.7 7.7 %scatter_custom_fusion.5 = f32[384]{0:T(512)S(1)} fusion(s32[1024]{0:T(1024)} %copy-done.26, f32[1024]{0:T(1024)S(1)} %get-tuple-element.103, f32[]{:T(128)} %constant.93.clone.1), kind=kCustom, calls=%fused_computation.209 | custom fusion | flops 1024 | bytes 2048 | tf_op jit(solution)/shard_map/scatter-add | solution.py:85
  244.1 6.1 %scatter_fusion.1 = f32[384,3]{1,0:T(8,128)S(1)} fusion(f32[384,3]{1,0:T(8,128)S(1)} %pad.92, s32[1024]{0:T(1024)S(1)} %bitcast.96, f32[1024,3]{1,0:T(8,128)S(1)} %get-tuple-element.48), kind=kCustom, calls=%fused_computation.11 | custom fusion | flops 3072 | bytes 40960 | tf_op jit(solution)/shard_map/transpose(jvp())/scatter-add | solution.py:31
  252.3 3.9 %collective-permute-start.34 = (f32[32,4]{0,1:T(4,128)S(1)}, f32[32,4]{0,1:T(4,128)S(1)}, u32[]{:S(2)}, u32[]{:S(2)}) collective-permute-start(f32[32,4]{0,1:T(4,128)S(1)} %get-tuple-element.101), channel_id=1, source_target_pairs={{1,0},{2,1},{3,2},{4,3},{5,4},{6,5},{7,6},{8,7},{9,8},{10,9},{11,1... | collective-permute-start | bytes 1544 | tf_op jit(solution)/shard_map/ppermute | solution.py:14
  258.2 5.8 %collective-permute-start.31 = (f32[64,4]{0,1:T(4,128)S(1)}, f32[64,4]{0,1:T(4,128)S(1)}, u32[]{:S(2)}, u32[]{:S(2)}) collective-permute-start(f32[64,4]{0,1:T(4,128)S(1)} %fusion.94), channel_id=1, source_target_pairs={{15,0},{0,1},{1,2},{2,3},{3,4},{4,5},{5,6},{6,7},{7,8},{8,9},{9,10... | collective-permute-start | bytes 3080 | tf_op jit(solution)/shard_map/ppermute | solution.py:14
  264.1 2.9 %collective-permute-start.33 = (f32[32,4]{0,1:T(4,128)S(1)}, f32[32,4]{0,1:T(4,128)S(1)}, u32[]{:S(2)}, u32[]{:S(2)}) collective-permute-start(f32[32,4]{0,1:T(4,128)S(1)} %collective-permute-done.32), channel_id=1, source_target_pairs={{496,0},{0,16},{16,32},{32,48},{48,64},{64,80},{80,96},{96,112},{1... | collective-permute-start | bytes 1544 | tf_op jit(solution)/shard_map/ppermute | solution.py:14
  267.0 2.2 collective-permute-start.35
  269.4 5.6 %collective-permute-done.33 = f32[32,4]{0,1:T(4,128)S(1)} collective-permute-done((f32[32,4]{0,1:T(4,128)S(1)}, f32[32,4]{0,1:T(4,128)S(1)}, u32[]{:S(2)}, u32[]{:S(2)}) %collective-permute-start.33) | collective-permute-done | bytes 544 | tf_op jit(solution)/shard_map/ppermute | solution.py:14
  275.0 2.9 %collective-permute-done.35 = f32[32,4]{0,1:T(4,128)S(1)} collective-permute-done((f32[32,4]{0,1:T(4,128)S(1)}, f32[32,4]{0,1:T(4,128)S(1)}, u32[]{:S(2)}, u32[]{:S(2)}) %collective-permute-start.35) | collective-permute-done | bytes 544 | tf_op jit(solution)/shard_map/ppermute | solution.py:14
  (285 shorter events, 74.4 us)
Async XLA Ops:
  0.6 87.0 %copy-start = (f32[128,128]{1,0:T(8,128)S(1)}, f32[128,128]{1,0:T(8,128)}, u32[]{:S(2)}) copy-start(f32[128,128]{1,0:T(8,128)} %param.31) | copy-start | bytes 196612
  1.4 95.4 %copy-start.34 = (s32[256,1]{0,1:T(1,128)}, s32[256,1]{0,1:T(1,128)S(1)}, u32[]{:S(2)}) copy-start(s32[256,1]{0,1:T(1,128)S(1)} %compare_select_fusion.1) | copy-start | bytes 3076
  2.3 138.1 %copy-start.15 = (s32[1024,1]{0,1:T(1,128)}, s32[1024,1]{0,1:T(1,128)S(1)}, u32[]{:S(2)}) copy-start(s32[1024,1]{0,1:T(1,128)S(1)} %compare_select_fusion) | copy-start | bytes 12292
  2.4 96.4 %copy-start.28 = (s32[1024]{0:T(1024)}, s32[1024]{0:T(1024)S(1)}, u32[]{:S(2)}) copy-start(s32[1024]{0:T(1024)S(1)} %get-tuple-element.118) | copy-start | bytes 12292
  3.1 22.5 %collective-permute-start.2 = (f32[32,4]{1,0:T(8,128)S(1)}, f32[32,4]{1,0:T(8,128)S(1)}, u32[]{:S(2)}, u32[]{:S(2)}) collective-permute-start(f32[32,4]{1,0:T(8,128)S(1)} %get-tuple-element.98), channel_id=1, source_target_pairs={{16,0},{32,16},{48,32},{64,48},{80,64},{96,80},{112,96},{128,112},... | collective-permute-start | bytes 1544 | tf_op jit(solution)/shard_map/ppermute | solution.py:14
  16.1 12.0 %collective-permute-start.4 = (f32[32,4]{1,0:T(8,128)S(1)}, f32[32,4]{1,0:T(8,128)S(1)}, u32[]{:S(2)}, u32[]{:S(2)}) collective-permute-start(f32[32,4]{1,0:T(8,128)S(1)} %get-tuple-element.99), channel_id=1, source_target_pairs={{16,0},{32,16},{48,32},{64,48},{80,64},{96,80},{112,96},{128,112},... | collective-permute-start | bytes 1544 | tf_op jit(solution)/shard_map/ppermute | solution.py:14
  18.7 18.3 %collective-permute-start.1 = (f32[64,4]{1,0:T(8,128)S(1)}, f32[64,4]{1,0:T(8,128)S(1)}, u32[]{:S(2)}, u32[]{:S(2)}) collective-permute-start(f32[64,4]{1,0:T(8,128)S(1)} %slice.272), channel_id=1, source_target_pairs={{1,0},{2,1},{3,2},{4,3},{5,4},{6,5},{7,6},{8,7},{9,8},{10,9},{11,1... | collective-permute-start | bytes 3080 | tf_op jit(solution)/shard_map/ppermute | solution.py:14
  21.4 15.6 %collective-permute-start = (f32[128,4]{1,0:T(8,128)S(1)}, f32[128,4]{1,0:T(8,128)S(1)}, u32[]{:S(2)}, u32[]{:S(2)}) collective-permute-start(f32[128,4]{1,0:T(8,128)S(1)} %slice.271), channel_id=1, source_target_pairs={{16,0},{32,16},{48,32},{64,48},{80,64},{96,80},{112,96},{128,112},... | collective-permute-start | bytes 6152 | tf_op jit(solution)/shard_map/ppermute | solution.py:14
  23.5 33.0 %copy-start.26 = (s32[1024]{0:T(1024)}, s32[1024]{0:T(1024)S(1)}, u32[]{:S(2)}) copy-start(s32[1024]{0:T(1024)S(1)} %reshape.337) | copy-start | bytes 12292
  24.9 26.9 %copy-start.47 = (f32[8]{0:T(128)}, f32[8]{0:T(128)S(1)}, u32[]{:S(2)}) copy-start(f32[8]{0:T(128)S(1)} %multiply_add_fusion.1) | copy-start | bytes 100
  25.6 11.1 %collective-permute-start.3 = (f32[32,4]{1,0:T(8,128)S(1)}, f32[32,4]{1,0:T(8,128)S(1)}, u32[]{:S(2)}, u32[]{:S(2)}) collective-permute-start(f32[32,4]{1,0:T(8,128)S(1)} %collective-permute-done.2), channel_id=1, source_target_pairs={{1,0},{2,1},{3,2},{4,3},{5,4},{6,5},{7,6},{8,7},{9,8},{10,9},{11,1... | collective-permute-start | bytes 1544 | tf_op jit(solution)/shard_map/ppermute | solution.py:14
  28.1 8.8 %collective-permute-start.5 = (f32[32,4]{1,0:T(8,128)S(1)}, f32[32,4]{1,0:T(8,128)S(1)}, u32[]{:S(2)}, u32[]{:S(2)}) collective-permute-start(f32[32,4]{1,0:T(8,128)S(1)} %collective-permute-done.4), channel_id=1, source_target_pairs={{15,0},{0,1},{1,2},{2,3},{3,4},{4,5},{5,6},{6,7},{7,8},{8,9},{9,10... | collective-permute-start | bytes 1544 | tf_op jit(solution)/shard_map/ppermute | solution.py:14
  36.3 13.9 %copy-start.29 = (pred[1024]{0:T(1024)(128)(4,1)}, pred[1024]{0:T(1024)(128)(4,1)S(1)}, u32[]{:S(2)}) copy-start(pred[1024]{0:T(1024)(128)(4,1)S(1)} %lt.56) | copy-start | bytes 3076
  53.8 33.8 %copy-start.49 = (f32[1024,128]{1,0:T(8,128)}, f32[1024,128]{1,0:T(8,128)S(1)}, u32[]{:S(2)}) copy-start(f32[1024,128]{1,0:T(8,128)S(1)} %fusion.2) | copy-start | bytes 1572868
  62.6 19.8 %collective-permute-start.8 = (f32[32,128]{1,0:T(8,128)S(1)}, f32[32,128]{1,0:T(8,128)S(1)}, u32[]{:S(2)}, u32[]{:S(2)}) collective-permute-start(f32[32,128]{1,0:T(8,128)S(1)} %get-tuple-element.77), channel_id=1, source_target_pairs={{15,0},{0,1},{1,2},{2,3},{3,4},{4,5},{5,6},{6,7},{7,8},{8,9},{9,10... | collective-permute-start | bytes 49160 | tf_op jit(solution)/shard_map/ppermute | solution.py:14
  70.7 14.9 %collective-permute-start.10 = (f32[32,128]{1,0:T(8,128)S(1)}, f32[32,128]{1,0:T(8,128)S(1)}, u32[]{:S(2)}, u32[]{:S(2)}) collective-permute-start(f32[32,128]{1,0:T(8,128)S(1)} %get-tuple-element.78), channel_id=1, source_target_pairs={{1,0},{2,1},{3,2},{4,3},{5,4},{6,5},{7,6},{8,7},{9,8},{10,9},{11,1... | collective-permute-start | bytes 49160 | tf_op jit(solution)/shard_map/ppermute | solution.py:14
  72.7 24.1 %collective-permute-start.7 = (f32[64,128]{1,0:T(8,128)S(1)}, f32[64,128]{1,0:T(8,128)S(1)}, u32[]{:S(2)}, u32[]{:S(2)}) collective-permute-start(f32[64,128]{1,0:T(8,128)S(1)} %slice.282), channel_id=1, source_target_pairs={{15,0},{0,1},{1,2},{2,3},{3,4},{4,5},{5,6},{6,7},{7,8},{8,9},{9,10... | collective-permute-start | bytes 98312 | tf_op jit(solution)/shard_map/ppermute | solution.py:14
  80.5 16.2 %collective-permute-start.6 = (f32[128,128]{1,0:T(8,128)S(1)}, f32[128,128]{1,0:T(8,128)S(1)}, u32[]{:S(2)}, u32[]{:S(2)}) collective-permute-start(f32[128,128]{1,0:T(8,128)S(1)} %get-tuple-element.75), channel_id=1, source_target_pairs={{496,0},{0,16},{16,32},{32,48},{48,64},{64,80},{80,96},{96,112},{1... | collective-permute-start | bytes 196616 | tf_op jit(solution)/shard_map/ppermute | solution.py:14
  82.5 11.1 %collective-permute-start.9 = (f32[32,128]{1,0:T(8,128)S(1)}, f32[32,128]{1,0:T(8,128)S(1)}, u32[]{:S(2)}, u32[]{:S(2)}) collective-permute-start(f32[32,128]{1,0:T(8,128)S(1)} %collective-permute-done.8), channel_id=1, source_target_pairs={{496,0},{0,16},{16,32},{32,48},{48,64},{64,80},{80,96},{96,112},{1... | collective-permute-start | bytes 49160 | tf_op jit(solution)/shard_map/ppermute | solution.py:14
  85.7 11.1 %collective-permute-start.11 = (f32[32,128]{1,0:T(8,128)S(1)}, f32[32,128]{1,0:T(8,128)S(1)}, u32[]{:S(2)}, u32[]{:S(2)}) collective-permute-start(f32[32,128]{1,0:T(8,128)S(1)} %collective-permute-done.10), channel_id=1, source_target_pairs={{496,0},{0,16},{16,32},{32,48},{48,64},{64,80},{80,96},{96,112},{1... | collective-permute-start | bytes 49160 | tf_op jit(solution)/shard_map/ppermute | solution.py:14
  100.8 12.2 %collective-permute-start.16 = (f32[32,128]{1,0:T(8,128)S(1)}, f32[32,128]{1,0:T(8,128)}, u32[]{:S(2)}, u32[]{:S(2)}) collective-permute-start(f32[32,128]{1,0:T(8,128)S(1)} %get-tuple-element.91), channel_id=1, source_target_pairs={{16,0},{32,16},{48,32},{64,48},{80,64},{96,80},{112,96},{128,112},... | collective-permute-start | bytes 49160 | tf_op jit(solution)/shard_map/ppermute | solution.py:14
  102.7 18.3 %collective-permute-start.14 = (f32[32,128]{1,0:T(8,128)}, f32[32,128]{1,0:T(8,128)}, u32[]{:S(2)}, u32[]{:S(2)}) collective-permute-start(f32[32,128]{1,0:T(8,128)} %get-tuple-element.92), channel_id=1, source_target_pairs={{16,0},{32,16},{48,32},{64,48},{80,64},{96,80},{112,96},{128,112},... | collective-permute-start | bytes 49160 | tf_op jit(solution)/shard_map/ppermute | solution.py:14
  105.6 18.3 %collective-permute-start.13 = (f32[64,128]{1,0:T(8,128)}, f32[64,128]{1,0:T(8,128)}, u32[]{:S(2)}, u32[]{:S(2)}) collective-permute-start(f32[64,128]{1,0:T(8,128)} %slice.286), channel_id=1, source_target_pairs={{1,0},{2,1},{3,2},{4,3},{5,4},{6,5},{7,6},{8,7},{9,8},{10,9},{11,1... | collective-permute-start | bytes 98312 | tf_op jit(solution)/shard_map/ppermute | solution.py:14
  107.5 15.5 %collective-permute-start.12 = (f32[128,128]{1,0:T(8,128)S(1)}, f32[128,128]{1,0:T(8,128)}, u32[]{:S(2)}, u32[]{:S(2)}) collective-permute-start(f32[128,128]{1,0:T(8,128)S(1)} %slice.285), channel_id=1, source_target_pairs={{16,0},{32,16},{48,32},{64,48},{80,64},{96,80},{112,96},{128,112},... | collective-permute-start | bytes 196616 | tf_op jit(solution)/shard_map/ppermute | solution.py:14
  113.0 17.8 %collective-permute-start.17 = (f32[32,128]{1,0:T(8,128)}, f32[32,128]{1,0:T(8,128)S(1)}, u32[]{:S(2)}, u32[]{:S(2)}) collective-permute-start(f32[32,128]{1,0:T(8,128)} %collective-permute-done.16), channel_id=1, source_target_pairs={{15,0},{0,1},{1,2},{2,3},{3,4},{4,5},{5,6},{6,7},{7,8},{8,9},{9,10... | collective-permute-start | bytes 49160 | tf_op jit(solution)/shard_map/ppermute | solution.py:14
  121.0 9.8 %collective-permute-start.15 = (f32[32,128]{1,0:T(8,128)}, f32[32,128]{1,0:T(8,128)S(1)}, u32[]{:S(2)}, u32[]{:S(2)}) collective-permute-start(f32[32,128]{1,0:T(8,128)} %collective-permute-done.14), channel_id=1, source_target_pairs={{1,0},{2,1},{3,2},{4,3},{5,4},{6,5},{7,6},{8,7},{9,8},{10,9},{11,1... | collective-permute-start | bytes 49160 | tf_op jit(solution)/shard_map/ppermute | solution.py:14
  146.6 13.7 %collective-permute-start.20 = (f32[32,128]{1,0:T(8,128)S(1)}, f32[32,128]{1,0:T(8,128)}, u32[]{:S(2)}, u32[]{:S(2)}) collective-permute-start(f32[32,128]{1,0:T(8,128)S(1)} %get-tuple-element.73), channel_id=1, source_target_pairs={{15,0},{0,1},{1,2},{2,3},{3,4},{4,5},{5,6},{6,7},{7,8},{8,9},{9,10... | collective-permute-start | bytes 49160 | tf_op jit(solution)/shard_map/ppermute | solution.py:14
  148.5 14.9 %collective-permute-start.22 = (f32[32,128]{1,0:T(8,128)S(1)}, f32[32,128]{1,0:T(8,128)}, u32[]{:S(2)}, u32[]{:S(2)}) collective-permute-start(f32[32,128]{1,0:T(8,128)S(1)} %get-tuple-element.74), channel_id=1, source_target_pairs={{1,0},{2,1},{3,2},{4,3},{5,4},{6,5},{7,6},{8,7},{9,8},{10,9},{11,1... | collective-permute-start | bytes 49160 | tf_op jit(solution)/shard_map/ppermute | solution.py:14
  152.5 22.3 %collective-permute-start.19 = (f32[64,128]{1,0:T(8,128)S(1)}, f32[64,128]{1,0:T(8,128)S(1)}, u32[]{:S(2)}, u32[]{:S(2)}) collective-permute-start(f32[64,128]{1,0:T(8,128)S(1)} %slice.299), channel_id=1, source_target_pairs={{15,0},{0,1},{1,2},{2,3},{3,4},{4,5},{5,6},{6,7},{7,8},{8,9},{9,10... | collective-permute-start | bytes 98312 | tf_op jit(solution)/shard_map/ppermute | solution.py:14
  158.3 16.4 %collective-permute-start.18 = (f32[128,128]{1,0:T(8,128)S(1)}, f32[128,128]{1,0:T(8,128)S(1)}, u32[]{:S(2)}, u32[]{:S(2)}) collective-permute-start(f32[128,128]{1,0:T(8,128)S(1)} %get-tuple-element.71), channel_id=1, source_target_pairs={{496,0},{0,16},{16,32},{32,48},{48,64},{64,80},{80,96},{96,112},{1... | collective-permute-start | bytes 196616 | tf_op jit(solution)/shard_map/ppermute | solution.py:14
  160.2 11.3 %collective-permute-start.21 = (f32[32,128]{1,0:T(8,128)}, f32[32,128]{1,0:T(8,128)S(1)}, u32[]{:S(2)}, u32[]{:S(2)}) collective-permute-start(f32[32,128]{1,0:T(8,128)} %collective-permute-done.20), channel_id=1, source_target_pairs={{496,0},{0,16},{16,32},{32,48},{48,64},{64,80},{80,96},{96,112},{1... | collective-permute-start | bytes 49160 | tf_op jit(solution)/shard_map/ppermute | solution.py:14
  163.4 11.3 %collective-permute-start.23 = (f32[32,128]{1,0:T(8,128)}, f32[32,128]{1,0:T(8,128)S(1)}, u32[]{:S(2)}, u32[]{:S(2)}) collective-permute-start(f32[32,128]{1,0:T(8,128)} %collective-permute-done.22), channel_id=1, source_target_pairs={{496,0},{0,16},{16,32},{32,48},{48,64},{64,80},{80,96},{96,112},{1... | collective-permute-start | bytes 49160 | tf_op jit(solution)/shard_map/ppermute | solution.py:14
  177.8 10.7 %collective-permute-start.28 = (f32[32,128]{1,0:T(8,128)S(1)}, f32[32,128]{1,0:T(8,128)S(1)}, u32[]{:S(2)}, u32[]{:S(2)}) collective-permute-start(f32[32,128]{1,0:T(8,128)S(1)} %get-tuple-element.89), channel_id=1, source_target_pairs={{16,0},{32,16},{48,32},{64,48},{80,64},{96,80},{112,96},{128,112},... | collective-permute-start | bytes 49160 | tf_op jit(solution)/shard_map/ppermute | solution.py:14
  181.7 14.6 %collective-permute-start.26 = (f32[32,128]{1,0:T(8,128)S(1)}, f32[32,128]{1,0:T(8,128)S(1)}, u32[]{:S(2)}, u32[]{:S(2)}) collective-permute-start(f32[32,128]{1,0:T(8,128)S(1)} %get-tuple-element.90), channel_id=1, source_target_pairs={{16,0},{32,16},{48,32},{64,48},{80,64},{96,80},{112,96},{128,112},... | collective-permute-start | bytes 49160 | tf_op jit(solution)/shard_map/ppermute | solution.py:14
  183.6 14.8 %collective-permute-start.24 = (f32[128,128]{1,0:T(8,128)S(1)}, f32[128,128]{1,0:T(8,128)S(1)}, u32[]{:S(2)}, u32[]{:S(2)}) collective-permute-start(f32[128,128]{1,0:T(8,128)S(1)} %slice.302), channel_id=1, source_target_pairs={{16,0},{32,16},{48,32},{64,48},{80,64},{96,80},{112,96},{128,112},... | collective-permute-start | bytes 196616 | tf_op jit(solution)/shard_map/ppermute | solution.py:14
  186.5 12.0 %collective-permute-start.25 = (f32[64,128]{1,0:T(8,128)S(1)}, f32[64,128]{1,0:T(8,128)S(1)}, u32[]{:S(2)}, u32[]{:S(2)}) collective-permute-start(f32[64,128]{1,0:T(8,128)S(1)} %slice.303), channel_id=1, source_target_pairs={{1,0},{2,1},{3,2},{4,3},{5,4},{6,5},{7,6},{8,7},{9,8},{10,9},{11,1... | collective-permute-start | bytes 98312 | tf_op jit(solution)/shard_map/ppermute | solution.py:14
  188.4 17.4 %collective-permute-start.29 = (f32[32,128]{1,0:T(8,128)S(1)}, f32[32,128]{1,0:T(8,128)S(1)}, u32[]{:S(2)}, u32[]{:S(2)}) collective-permute-start(f32[32,128]{1,0:T(8,128)S(1)} %collective-permute-done.28), channel_id=1, source_target_pairs={{15,0},{0,1},{1,2},{2,3},{3,4},{4,5},{5,6},{6,7},{7,8},{8,9},{9,10... | collective-permute-start | bytes 49160 | tf_op jit(solution)/shard_map/ppermute | solution.py:14
  196.3 9.5 %collective-permute-start.27 = (f32[32,128]{1,0:T(8,128)S(1)}, f32[32,128]{1,0:T(8,128)S(1)}, u32[]{:S(2)}, u32[]{:S(2)}) collective-permute-start(f32[32,128]{1,0:T(8,128)S(1)} %collective-permute-done.26), channel_id=1, source_target_pairs={{1,0},{2,1},{3,2},{4,3},{5,4},{6,5},{7,6},{8,7},{9,8},{10,9},{11,1... | collective-permute-start | bytes 49160 | tf_op jit(solution)/shard_map/ppermute | solution.py:14
  219.3 1.9 copy-start.31
  229.3 2.1 copy-start.23
  231.3 3.6 %copy-start.24 = (f32[1024]{0:T(1024)S(1)}, f32[1024]{0:T(1024)}, u32[]{:S(2)}) copy-start(f32[1024]{0:T(1024)} %get-tuple-element.57) | copy-start | bytes 12292
  231.3 3.6 %copy-start.32 = (f32[1,1024]{1,0:T(1,128)S(1)}, f32[1,1024]{1,0:T(1,128)}, u32[]{:S(2)}) copy-start(f32[1,1024]{1,0:T(1,128)} %fusion.19) | copy-start | bytes 12292
  250.4 13.6 %collective-permute-start.32 = (f32[32,4]{0,1:T(4,128)S(1)}, f32[32,4]{0,1:T(4,128)S(1)}, u32[]{:S(2)}, u32[]{:S(2)}) collective-permute-start(f32[32,4]{0,1:T(4,128)S(1)} %get-tuple-element.100), channel_id=1, source_target_pairs={{15,0},{0,1},{1,2},{2,3},{3,4},{4,5},{5,6},{6,7},{7,8},{8,9},{9,10... | collective-permute-start | bytes 1544 | tf_op jit(solution)/shard_map/ppermute | solution.py:14
  252.3 14.6 %collective-permute-start.34 = (f32[32,4]{0,1:T(4,128)S(1)}, f32[32,4]{0,1:T(4,128)S(1)}, u32[]{:S(2)}, u32[]{:S(2)}) collective-permute-start(f32[32,4]{0,1:T(4,128)S(1)} %get-tuple-element.101), channel_id=1, source_target_pairs={{1,0},{2,1},{3,2},{4,3},{5,4},{6,5},{7,6},{8,7},{9,8},{10,9},{11,1... | collective-permute-start | bytes 1544 | tf_op jit(solution)/shard_map/ppermute | solution.py:14
  256.3 21.6 %collective-permute-start.30 = (f32[128,4]{0,1:T(4,128)S(1)}, f32[128,4]{0,1:T(4,128)S(1)}, u32[]{:S(2)}, u32[]{:S(2)}) collective-permute-start(f32[128,4]{0,1:T(4,128)S(1)} %fusion.93), channel_id=1, source_target_pairs={{496,0},{0,16},{16,32},{32,48},{48,64},{64,80},{80,96},{96,112},{1... | collective-permute-start | bytes 6152 | tf_op jit(solution)/shard_map/ppermute | solution.py:14
  258.2 19.7 %collective-permute-start.31 = (f32[64,4]{0,1:T(4,128)S(1)}, f32[64,4]{0,1:T(4,128)S(1)}, u32[]{:S(2)}, u32[]{:S(2)}) collective-permute-start(f32[64,4]{0,1:T(4,128)S(1)} %fusion.94), channel_id=1, source_target_pairs={{15,0},{0,1},{1,2},{2,3},{3,4},{4,5},{5,6},{6,7},{7,8},{8,9},{9,10... | collective-permute-start | bytes 3080 | tf_op jit(solution)/shard_map/ppermute | solution.py:14
  264.1 10.9 %collective-permute-start.33 = (f32[32,4]{0,1:T(4,128)S(1)}, f32[32,4]{0,1:T(4,128)S(1)}, u32[]{:S(2)}, u32[]{:S(2)}) collective-permute-start(f32[32,4]{0,1:T(4,128)S(1)} %collective-permute-done.32), channel_id=1, source_target_pairs={{496,0},{0,16},{16,32},{32,48},{48,64},{64,80},{80,96},{96,112},{1... | collective-permute-start | bytes 1544 | tf_op jit(solution)/shard_map/ppermute | solution.py:14
  267.0 10.9 %collective-permute-start.35 = (f32[32,4]{0,1:T(4,128)S(1)}, f32[32,4]{0,1:T(4,128)S(1)}, u32[]{:S(2)}, u32[]{:S(2)}) collective-permute-start(f32[32,4]{0,1:T(4,128)S(1)} %collective-permute-done.34), channel_id=1, source_target_pairs={{496,0},{0,16},{16,32},{32,48},{48,64},{64,80},{80,96},{96,112},{1... | collective-permute-start | bytes 1544 | tf_op jit(solution)/shard_map/ppermute | solution.py:14
  (40 other events, 34.8 us)
where the time goes:
time: 283 us; the launch traced here: 281 us
  starting transfers between devices  131 us (46%)
  local copies, waits for them, and re-layouts  58.1 us (21%)
  other arithmetic  41.9 us (15%)
  waiting for transfers between devices  36.4 us (13%)
  matrix products  11.3 us (4%)
    ppermute x36, starting transfers between devices, from_behind(): return lax.ppermute(block, axis, route)  131 us
    ppermute x36, waiting for transfers between devices, from_behind(): return lax.ppermute(block, axis, route)  36.4 us
    unnamed x127, local copies, waits for them, and re-layouts  19.6 us
    dot_general x11, matrix products, product(): jnp.dot(left, right, precision=PRECISE, preferred_element_type=jnp.float32)  11.3 us
    scatter-add x1, other arithmetic, energy_split(): jax.ops.segment_sum(half_edge, neigh_idx.reshape(-1), num_segments=total_...  7.75 us
    gather x1, local copies, waits for them, and re-layouts, first_layer(): spec_n = spec_table[flat_idx]  6.87 us
    scatter-add x1, other arithmetic, second_layer(): env_n = env_all[flat_idx]  6.13 us
    scatter-add x1, other arithmetic, first_layer(): pos_table[flat_idx] - centre  6.11 us
  transfers between devices with their start and end apart: 36, of which 8 were waited for; matrix products, arithmetic and copies ran while one was open for 4% of the time, Pallas kernels for 0%

commit v1 on v0

v1 whole, which is shorter than its diff:
```python
import jax
import jax.numpy as jnp
from jax import lax
from jax.experimental import pallas as pl
from jax.experimental.pallas import tpu as pltpu
from jax.sharding import PartitionSpec as P

F32 = jnp.float32
BF16 = jnp.bfloat16
ATOMS = 128
SLOTS = 8
EDGES = ATOMS * SLOTS
WIDE = 256
LONE = 128
TC = 32
VMEM_LIMIT = 48 * 1024 * 1024


def halves(x):
    high = x.astype(BF16)
    return high, (x - high.astype(F32)).astype(BF16)


def dot_nn(a, b):
    return lax.dot_general(a, b, (((1,), (0,)), ((), ())), preferred_element_type=F32)


def dot_nt(a, b):
    return lax.dot_general(a, b, (((1,), (1,)), ((), ())), preferred_element_type=F32)


def product(left, right):
    a, b = halves(left)
    c, d = halves(right)
    return dot_nn(a, c) + (dot_nn(a, d) + dot_nn(b, c))


def one_hot(index_row, rows):
    lines = lax.broadcasted_iota(jnp.int32, (rows, index_row.shape[1]), 0)
    return jnp.where(lines == index_row, 1.0, 0.0).astype(BF16)


def gather(high, low, hot):
    return dot_nn(high, hot) + dot_nn(low, hot)


def scatter(values, hot):
    high, low = halves(values)
    return dot_nt(high, hot) + dot_nt(low, hot)


def lanes(table, index):
    return jnp.take_along_axis(table, index, axis=1, mode="promise_in_bounds")


def spread(row):
    return jnp.broadcast_to(row, (8, row.shape[1]))


def sigmoid_parts(pre):
    gate = 1.0 / (1.0 + jnp.exp(-pre))
    value = pre * gate
    return value, gate + value * (1.0 - gate)


def four(weight, unit, sign):
    parts = [weight]
    for comp in range(3):
        parts.append((sign * weight) * unit[comp])
    return jnp.concatenate(parts, axis=0)


def basis_of(radius):
    step = lax.broadcasted_iota(jnp.int32, (8, radius.shape[1]), 0).astype(F32)
    gap = radius - (0.5 + 2.5 * step / 7.0)
    return jnp.exp(-4.0 * gap * gap), gap


def unit_rows(geo):
    return [geo[0:1], geo[1:2], geo[2:3]]


def geometry(dx, dy, dz, live):
    radius_sq = dx * dx + dy * dy + dz * dz + 0.25
    radius = jnp.sqrt(radius_sq)
    inverse = 1.0 / radius
    envelope = live * jnp.exp(-0.25 * radius_sq)
    return dx * inverse, dy * inverse, dz * inverse, envelope, radius


def first_kernel(
    own_ref, x_ref, yc_ref, wfeat_ref, wenv_ref, xc_ref, oy_ref, lat_ref, dlat_ref, wl_ref, geo_ref, count_ref, rank_ref
):
    sub = lax.broadcasted_iota(jnp.int32, (SLOTS, ATOMS), 0)
    lane = lax.broadcasted_iota(jnp.int32, (SLOTS, ATOMS), 1)
    x_send = x_ref[5:6]
    list_low = spread(x_ref[4:5])
    list_high = jnp.where(lane < 64, spread(yc_ref[5:6]), jnp.where(lane < 96, spread(yc_ref[29:30]), spread(x_send)))

    neigh = own_ref[8:16].astype(jnp.int32)
    live = sub < spread(own_ref[6:7]).astype(jnp.int32)
    ghost = neigh - ATOMS
    low = lanes(list_low, jnp.clip(ghost, 0, ATOMS - 1)).astype(jnp.int32)
    high = lanes(list_high, jnp.clip(ghost - ATOMS, 0, ATOMS - 1)).astype(jnp.int32)
    atom = jnp.where(ghost < 0, neigh, jnp.where(ghost < ATOMS, low, high))
    in_x = (ghost >= 0) & (ghost < 128)
    in_y = (ghost >= 128) & (ghost < 192)
    in_c = ghost >= 192
    live = live & (ghost < 224)

    def pick(line):
        values = lanes(spread(own_ref[line : line + 1]), atom)
        values = jnp.where(in_x, lanes(spread(x_ref[line : line + 1]), atom), values)
        values = jnp.where(in_y, lanes(spread(yc_ref[line : line + 1]), atom), values)
        return jnp.where(in_c, lanes(spread(yc_ref[24 + line : 25 + line]), atom), values)

    shift_x = jnp.where(in_x | in_c, 1.0, 0.0)
    shift_y = jnp.where(in_y | in_c, 1.0, 0.0)
    dx = pick(0) + shift_x - own_ref[0:1]
    dy = pick(1) + shift_y - own_ref[1:2]
    dz = pick(2) - own_ref[2:3] + own_ref[16:24]
    rows = list(geometry(dx, dy, dz, jnp.where(live, 1.0, 0.0)))
    rows.append(spread(own_ref[3:4]))
    rows.append(pick(3))
    box = jnp.where(in_x, 128, 0) + jnp.where(in_y, 256, 0) + jnp.where(in_c, 384, 0)
    rows.append((box + atom).astype(F32))
    for line, values in enumerate(rows):
        for k in range(SLOTS):
            geo_ref[line : line + 1, k * ATOMS : (k + 1) * ATOMS] = values[k : k + 1]
    geo_ref[8:16, 0:EDGES] = jnp.zeros((8, EDGES), F32)

    y_neigh = yc_ref[8:16].astype(jnp.int32)
    wanted = (sub < spread(yc_ref[6:7]).astype(jnp.int32)) & (y_neigh >= 352)
    wanted_f = jnp.where(wanted, 1.0, 0.0)
    y_atom = lanes(spread(x_send), jnp.clip(y_neigh - 256, 0, ATOMS - 1))
    before = jnp.where(
        lax.broadcasted_iota(jnp.int32, (ATOMS, ATOMS), 0) <= lax.broadcasted_iota(jnp.int32, (ATOMS, ATOMS), 1), 1.0, 0.0
    ).astype(BF16)
    upto = dot_nn(wanted_f.astype(BF16), before)
    totals = jnp.sum(wanted_f, axis=1, keepdims=True)
    running = jnp.zeros((1, 1), F32)
    starts = []
    for k in range(SLOTS):
        starts.append(running)
        running = running + totals[k : k + 1]
    rank = jnp.where(wanted, upto - 1.0 + jnp.concatenate(starts, axis=0), -1.0)
    rank_ref[0:8] = rank
    rank_ref[8:16] = y_atom
    count = jnp.sum(wanted_f).astype(jnp.int32)
    count_ref[0] = count
    blocks = (count + (LONE - 1)) // LONE

    def compact(block, carry):
        base = (block * LONE).astype(F32)
        line = lax.broadcasted_iota(jnp.int32, (LONE, ATOMS), 0).astype(F32) + base
        packed = jnp.zeros((8, LONE), F32)
        for k in range(SLOTS):
            hot = jnp.where(line == rank_ref[k : k + 1], 1.0, 0.0).astype(BF16)
            feats = jnp.where(sub == 0, lane.astype(F32), 0.0)
            feats = jnp.where(sub == 1, rank_ref[8 + k : 9 + k], feats)
            feats = jnp.where(sub == 2, yc_ref[16 + k : 17 + k], feats)
            feats = jnp.where(sub == 3, 1.0, feats)
            packed = packed + dot_nt(feats.astype(BF16), hot)
        centre = lanes(yc_ref[0:8], spread(packed[0:1]).astype(jnp.int32))
        other = lanes(x_ref[0:8], spread(packed[1:2]).astype(jnp.int32))
        ex = other[0:1] + 1.0 - centre[0:1]
        ey = other[1:2] - 1.0 - centre[1:2]
        ez = other[2:3] - centre[2:3] + packed[2:3]
        found = list(geometry(ex, ey, ez, packed[3:4])) + [centre[3:4], other[3:4], packed[1:2], packed[0:1]]
        spot = pl.ds(pl.multiple_of(EDGES + block * LONE, LONE), LONE)
        for number, values in enumerate(found):
            geo_ref[number : number + 1, spot] = values
        return carry

    lax.fori_loop(0, blocks, compact, 0)

    wfeat = wfeat_ref[...]
    wenv = wenv_ref[...]
    xc_ref[...] = jnp.zeros_like(xc_ref)
    oy_ref[...] = jnp.zeros_like(oy_ref)

    def edge_block(spot):
        geo = geo_ref[:, spot]
        basis, _ = basis_of(geo[4:5])
        line = lax.broadcasted_iota(jnp.int32, basis.shape, 0)
        extra = jnp.where(line == 0, 1.0, jnp.where(line == 1, geo[5:6], jnp.where(line == 2, geo[6:7], 0.0)))
        pre = product(wfeat, jnp.concatenate([basis, extra], axis=0))
        latent, slope = sigmoid_parts(pre)
        lat_ref[:, spot] = latent
        dlat_ref[:, spot] = slope
        plain = product(wenv, latent)
        wl_ref[:, spot] = plain
        weight = plain * (0.25 * geo[3:4])
        unit = unit_rows(geo)
        return geo, four(weight, unit, 1.0), four(weight, unit, -1.0)

    def main(block, carry):
        spot = pl.ds(pl.multiple_of(block * WIDE, WIDE), WIDE)
        geo, centre, other = edge_block(spot)
        sums = scatter(other, one_hot(geo[7:8].astype(jnp.int32), 512))
        oy_ref[0:128] += sums[:, 0:128] + (centre[:, 0:128] + centre[:, 128:256])
        xc_ref[0:128] += sums[:, 128:256]
        oy_ref[128:256] += sums[:, 256:384]
        xc_ref[128:256] += sums[:, 384:512]
        return carry

    lax.fori_loop(0, EDGES // WIDE, main, 0)

    def lone(block, carry):
        spot = pl.ds(pl.multiple_of(EDGES + block * LONE, LONE), LONE)
        geo, centre, other = edge_block(spot)
        xc_ref[0:128] += scatter(other, one_hot(geo[7:8].astype(jnp.int32), 128))
        oy_ref[128:256] += scatter(centre, one_hot(geo[8:9].astype(jnp.int32), 128))
        return carry

    lax.fori_loop(0, blocks, lone, 0)


def fill_tables(up_ref, down_ref, from_below_ref, from_above_ref, table_ref):
    own = down_ref[0:128] + from_below_ref[0:128]
    in_x = down_ref[128:256] + from_below_ref[128:256]
    in_y = up_ref[0:128] + from_above_ref[0:128]
    in_c = up_ref[128:256] + from_above_ref[128:256]
    for place, values in enumerate((own, in_x, in_y, in_c)):
        high, low = halves(values)
        table_ref[0:128, place * 128 : (place + 1) * 128] = high
        table_ref[128:256, place * 128 : (place + 1) * 128] = low
    return own


def fetch(table_ref, spot, hot):
    both = dot_nn(table_ref[:, spot], hot)
    return both[0:128] + both[128:256]


def project(rows, unit, sign):
    total = rows[0:TC]
    for comp in range(3):
        total = total + (sign * unit[comp]) * rows[(comp + 1) * TC : (comp + 2) * TC]
    return total


def second_kernel(
    count_ref, up_ref, down_ref, below_ref, above_ref, lat_ref, geo_ref, wlat_t_ref, wlat_ref, wten_t_ref, wten_ref, wout_ref,
    xc_ref, oy_ref, glat_ref, rows_ref, table_ref,
):
    own = fill_tables(up_ref, down_ref, below_ref, above_ref, table_ref)
    blocks = (count_ref[0] + (LONE - 1)) // LONE
    wout = wout_ref[...]
    xc_ref[...] = jnp.zeros_like(xc_ref)
    oy_ref[...] = jnp.zeros_like(oy_ref)

    def edge_block(spot, geo, env_c, env_n):
        unit = unit_rows(geo)
        envelope = geo[3:4]
        latent = lat_ref[:, spot]
        both = jnp.concatenate([project(env_c, unit, 1.0), project(env_n, unit, -1.0)], axis=0)
        pre = product(wlat_t_ref[...], latent) + product(wten_t_ref[...], both)
        hidden, slope = sigmoid_parts(pre)
        read = jnp.sum(wout * (latent + hidden), axis=0, keepdims=True)
        direct = wout * envelope
        grad_pre = direct * slope
        glat_ref[:, spot] = direct + product(wlat_ref[...], grad_pre)
        grad_both = product(wten_ref[...], grad_pre)
        grad_c, grad_n = grad_both[0:TC], grad_both[TC : 2 * TC]
        found = [read, 0.5 * envelope * read]
        for comp in range(3):
            lines = slice((comp + 1) * TC, (comp + 2) * TC)
            found.append(jnp.sum(env_c[lines] * grad_c - env_n[lines] * grad_n, axis=0, keepdims=True))
        for number, values in enumerate(found):
            rows_ref[number : number + 1, spot] = values
        return four(grad_c, unit, 1.0), four(grad_n, unit, -1.0)

    def main(block, carry):
        spot = pl.ds(pl.multiple_of(block * WIDE, WIDE), WIDE)
        geo = geo_ref[:, spot]
        hot = one_hot(geo[7:8].astype(jnp.int32), 512)
        env_n = fetch(table_ref, slice(0, 512), hot)
        centre, other = edge_block(spot, geo, jnp.concatenate([own, own], axis=1), env_n)
        sums = scatter(other, hot)
        oy_ref[0:128] += sums[:, 0:128] + (centre[:, 0:128] + centre[:, 128:256])
        xc_ref[0:128] += sums[:, 128:256]
        oy_ref[128:256] += sums[:, 256:384]
        xc_ref[128:256] += sums[:, 384:512]
        return carry

    lax.fori_loop(0, EDGES // WIDE, main, 0)

    def lone(block, carry):
        spot = pl.ds(pl.multiple_of(EDGES + block * LONE, LONE), LONE)
        geo = geo_ref[:, spot]
        hot_n = one_hot(geo[7:8].astype(jnp.int32), 128)
        hot_c = one_hot(geo[8:9].astype(jnp.int32), 128)
        env_n = fetch(table_ref, slice(128, 256), hot_n)
        env_c = fetch(table_ref, slice(256, 384), hot_c)
        centre, other = edge_block(spot, geo, env_c, env_n)
        xc_ref[0:128] += scatter(other, hot_n)
        oy_ref[128:256] += scatter(centre, hot_c)
        return carry

    lax.fori_loop(0, blocks, lone, 0)


def third_kernel(
    count_ref, up_ref, down_ref, below_ref, above_ref, dlat_ref, wl_ref, glat_ref, geo_ref, rows_ref, wenv_ref, wbasis_ref,
    yc_ref, ox_ref, table_ref,
):
    own = fill_tables(up_ref, down_ref, below_ref, above_ref, table_ref)
    blocks = (count_ref[0] + (LONE - 1)) // LONE
    yc_ref[...] = jnp.zeros_like(yc_ref)
    ox_ref[...] = jnp.zeros_like(ox_ref)

    def edge_block(spot, geo, grad_c, grad_n):
        unit = unit_rows(geo)
        envelope, radius = geo[3:4], geo[4:5]
        rows = rows_ref[:, spot]
        plain = wl_ref[:, spot]
        grad_w = 0.25 * (project(grad_c, unit, 1.0) + project(grad_n, unit, -1.0))
        weight = plain * (0.25 * envelope)
        grad_env = rows[0:1] + jnp.sum(grad_w * plain, axis=0, keepdims=True)
        grad_lat = glat_ref[:, spot] + product(wenv_ref[...], grad_w * envelope)
        grad_pre = grad_lat * dlat_ref[:, spot]
        grad_basis = product(wbasis_ref[...], grad_pre)
        basis, gap = basis_of(radius)
        grad_r = jnp.sum(grad_basis * (-8.0 * gap * basis), axis=0, keepdims=True)
        inverse = 1.0 / radius
        along = []
        for comp in range(3):
            lines = slice((comp + 1) * TC, (comp + 2) * TC)
            along.append(rows[2 + comp : 3 + comp] + jnp.sum(weight * (grad_c[lines] - grad_n[lines]), axis=0, keepdims=True))
            grad_r = grad_r - along[comp] * unit[comp] * inverse
        grad_sq = grad_r * (0.5 * inverse) - 0.25 * envelope * grad_env
        force = [-(along[comp] * inverse + 2.0 * radius * unit[comp] * grad_sq) for comp in range(3)]
        line = lax.broadcasted_iota(jnp.int32, (8, envelope.shape[1]), 0)
        packed = jnp.where(line == 3, rows[1:2], 0.0)
        for comp in range(3):
            packed = jnp.where(line == comp, force[comp], packed)
        return packed, jnp.where(line == 3, packed, -packed)

    def main(block, carry):
        spot = pl.ds(pl.multiple_of(block * WIDE, WIDE), WIDE)
        geo = geo_ref[:, spot]
        hot = one_hot(geo[7:8].astype(jnp.int32), 512)
        grad_n = fetch(table_ref, slice(0, 512), hot)
        other, centre = edge_block(spot, geo, jnp.concatenate([own, own], axis=1), grad_n)
        sums = scatter(other, hot)
        ox_ref[0:8] += sums[:, 0:128] + (centre[:, 0:128] + centre[:, 128:256])
        ox_ref[8:16] += sums[:, 128:256]
        yc_ref[0:8] += sums[:, 256:384]
        yc_ref[8:16] += sums[:, 384:512]
        return carry

    lax.fori_loop(0, EDGES // WIDE, main, 0)

    def lone(block, carry):
        spot = pl.ds(pl.multiple_of(EDGES + block * LONE, LONE), LONE)
        geo = geo_ref[:, spot]
        hot_n = one_hot(geo[7:8].astype(jnp.int32), 128)
        hot_c = one_hot(geo[8:9].astype(jnp.int32), 128)
        grad_n = fetch(table_ref, slice(128, 256), hot_n)
        grad_c = fetch(table_ref, slice(256, 384), hot_c)
        other, centre = edge_block(spot, geo, grad_c, grad_n)
        ox_ref[8:16] += scatter(other, hot_n)
        yc_ref[0:8] += scatter(centre, hot_c)
        return carry

    lax.fori_loop(0, blocks, lone, 0)


def call(kernel, out_shape, in_specs, out_specs, scratch, cost):
    return pl.pallas_call(
        kernel,
        out_shape=out_shape,
        in_specs=in_specs,
        out_specs=out_specs,
        scratch_shapes=scratch,
        compiler_params=pltpu.CompilerParams(vmem_limit_bytes=VMEM_LIMIT),
        cost_estimate=pl.CostEstimate(flops=cost, bytes_accessed=1 << 20, transcendentals=1 << 18),
    )


def shape(*dims):
    return jax.ShapeDtypeStruct(dims, F32)


IN_VMEM = pl.BlockSpec(memory_space=pltpu.VMEM)
IN_SMEM = pl.BlockSpec(memory_space=pltpu.SMEM)


def step(block, axis, distance):
    size = lax.axis_size(axis)
    return lax.ppermute(block, axis, [(i, (i + distance) % size) for i in range(size)])


def butterfly(xc, oy):
    from_left = step(xc, "gx", 1)
    from_right = step(oy, "gx", -1)
    here = oy + from_left
    beside = xc + from_right
    up = jnp.concatenate([here[128:256], beside[128:256]], axis=0)
    down = jnp.concatenate([here[0:128], beside[0:128]], axis=0)
    return up, down, step(up, "gy", 1), step(down, "gy", -1)


def local(
    positions, species, neighbours, counts, image_z, send_lists, w_basis, w_center, w_neigh, w_env, w_latent, w_tensor, w_out
):
    base = jnp.concatenate(
        [
            positions[0, 0],
            species[0].astype(F32),
            send_lists[0, 0].reshape(2, ATOMS).astype(F32),
            counts[0].astype(F32),
            jnp.zeros((1, ATOMS), F32),
        ],
        axis=0,
    )
    in_x = step(base, "gx", -1)
    own = jnp.concatenate([base, neighbours[0, 0].T.astype(F32), image_z[0, 0].T.astype(F32)], axis=0)
    in_yc = step(jnp.concatenate([own, in_x], axis=0), "gy", -1)

    wfeat = jnp.concatenate(
        [w_basis, (w_center[0] + w_neigh[0])[None], (w_center[1] - w_center[0])[None], (w_neigh[1] - w_neigh[0])[None],
         jnp.zeros((5, 128), F32)], axis=0
    ).T
    xc, oy, lat, dlat, wl, geo, count = call(
        first_kernel,
        (shape(256, 128), shape(256, 128), shape(128, 2 * EDGES), shape(128, 2 * EDGES), shape(32, 2 * EDGES),
         shape(16, 2 * EDGES), jax.ShapeDtypeStruct((1,), jnp.int32)),
        [IN_VMEM] * 5,
        (IN_VMEM,) * 6 + (IN_SMEM,),
        [pltpu.VMEM((16, ATOMS), F32)],
        500_000_000,
    )(own, in_x, in_yc, wfeat, w_env.T)
    up, down, below, above = butterfly(xc, oy)
    wten = w_tensor.reshape(2 * TC, 128)
    xc, oy, glat, rows = call(
        second_kernel,
        (shape(256, 128), shape(256, 128), shape(128, 2 * EDGES), shape(8, 2 * EDGES)),
        [IN_SMEM] + [IN_VMEM] * 11,
        (IN_VMEM,) * 4,
        [pltpu.VMEM((256, 512), BF16)],
        1_000_000_000,
    )(count, up, down, below, above, lat, geo, w_latent.T, w_latent, wten.T, wten, w_out[:, None])
    up, down, below, above = butterfly(xc, oy)
    yc, ox = call(
        third_kernel,
        (shape(16, 128), shape(16, 128)),
        [IN_SMEM] + [IN_VMEM] * 11,
        (IN_VMEM,) * 2,
        [pltpu.VMEM((256, 512), BF16)],
        500_000_000,
    )(count, up, down, below, above, dlat, wl, glat, geo, rows, w_env, w_basis)
    yc = step(yc, "gy", 1)
    ox = ox + yc
    total = ox[0:8] + step(ox[8:16], "gx", 1)
    return (total[0:3][None, None], total[3][None, None])


def solution(mesh):
    part = P("gx", "gy", None)
    wide = P("gx", "gy", None, None)
    return jax.shard_map(
        local,
        mesh=mesh,
        in_specs=(wide, part, wide, part, wide, part) + (P(),) * 7,
        out_specs=(wide, part),
        check_vma=False,
    )
```

time: 283 us -> 122 us (0.43)
  the two profiles are of different devices: /device:TPU:30 before, /device:TPU:32 now
where the time goes in v1:
time: 122 us
  starting transfers between devices  60.5 us (50%)
  waiting for transfers between devices  39.7 us (33%)
  Pallas kernels  14.6 us (12%)
  local copies, waits for them, and re-layouts  5.73 us (5%)
    ppermute x12, starting transfers between devices, step(): lax.ppermute(block, axis, [(i, (i + distance) % size) for i in range(size)])  60.5 us
    ppermute x12, waiting for transfers between devices, step(): lax.ppermute(block, axis, [(i, (i + distance) % size) for i in range(size)])  39.7 us
    pallas_call x1, Pallas kernels, local(): call(second_kernel, (shape(256, 128), shape(256, 128), shape(128, 2 * EDG...  5.48 us
    pallas_call x1, Pallas kernels, local(): call(third_kernel, (shape(16, 128), shape(16, 128)), [IN_SMEM] + [IN_VMEM...  4.89 us
    unnamed x32, local copies, waits for them, and re-layouts  4.76 us
    pallas_call x1, Pallas kernels, local(): call(first_kernel, (shape(256, 128), shape(256, 128), shape(128, 2 * EDGE...  4.24 us
  transfers between devices with their start and end apart: 12, of which 11 were waited for; matrix products, arithmetic and copies ran while one was open for 1% of the time, Pallas kernels for 0%

profile of v1, /device:TPU:32, one launch (start us, length us, event | category | flops | bytes accessed | tf_op | source)
XLA Modules:
  0.0 121.6 jit_solution(8419446862411726507)
XLA Ops:
  0.6 0.0 copy-start.10
  0.6 0.7 copy.35
  1.3 0.0 copy-done.10
  1.3 0.6 copy-done.12
  2.0 0.0 copy-done.13
  2.0 0.0 copy-start.7
  2.0 9.9 %collective-permute-start = (f32[8,128]{1,0:T(8,128)S(1)}, f32[8,128]{1,0:T(8,128)S(1)}, u32[]{:S(2)}, u32[]{:S(2)}) collective-permute-start(f32[8,128]{1,0:T(8,128)S(1)} %concatenate.27), channel_id=1, source_target_pairs={{0,496},{16,0},{32,16},{48,32},{64,48},{80,64},{96,80},{112,96},{1... | collective-permute-start | bytes 12296 | tf_op jit(solution)/shard_map/ppermute | solution.py:392
  12.0 1.3 %collective-permute-done.x_ref = f32[8,128]{1,0:T(8,128)S(1)} collective-permute-done((f32[8,128]{1,0:T(8,128)S(1)}, f32[8,128]{1,0:T(8,128)S(1)}, u32[]{:S(2)}, u32[]{:S(2)}) %collective-permute-start) | collective-permute-done | bytes 4128 | tf_op jit(solution)/shard_map/ppermute | solution.py:392
  13.3 7.7 %collective-permute-start.1 = (f32[32,128]{1,0:T(8,128)S(1)}, f32[32,128]{1,0:T(8,128)S(1)}, u32[]{:S(2)}, u32[]{:S(2)}) collective-permute-start(f32[32,128]{1,0:T(8,128)S(1)} %concatenate.28), channel_id=1, source_target_pairs={{0,15},{1,0},{2,1},{3,2},{4,3},{5,4},{6,5},{7,6},{8,7},{9,8},{10,9... | collective-permute-start | bytes 49160 | tf_op jit(solution)/shard_map/ppermute | solution.py:392
  21.1 0.0 copy-start.2
  21.1 0.7 copy-done.2
  21.8 0.1 copy.27
  21.9 0.5 collective-permute-done.1.yc_ref
  22.4 0.1 copy-done.3
  22.5 4.2 %shard_map.140 = (f32[256,128]{1,0:T(8,128)S(1)}, f32[256,128]{1,0:T(8,128)S(1)}, f32[128,2048]{1,0:T(8,128)S(1)}, f32[128,2048]{1,0:T(8,128)S(1)}, f32[32,2048]...) custom-call(f32[24,128]{1,0:T(8,128)S(1)} %concatenate.26.own_ref, f32[8,128]{1,0:T(8,128)S(1)} %collective-permute-done.x_ref, ...), custom_call_target="tpu_custom_call" | custom-call | flops 500000000 | bytes 1048576 | tf_op jit(solution)/shard_map/pallas_call | solution.py:426
  26.8 1.9 %collective-permute-start.2 = (f32[256,128]{1,0:T(8,128)S(1)}, f32[256,128]{1,0:T(8,128)S(1)}, u32[]{:S(2)}, u32[]{:S(2)}) collective-permute-start(f32[256,128]{1,0:T(8,128)S(1)} %get-tuple-element.17), channel_id=1, source_target_pairs={{0,16},{16,32},{32,48},{48,64},{64,80},{80,96},{96,112},{112,128},... | collective-permute-start | bytes 393224 | tf_op jit(solution)/shard_map/ppermute | solution.py:392
  28.7 9.7 %collective-permute-start.3 = (f32[256,128]{1,0:T(8,128)S(1)}, f32[256,128]{1,0:T(8,128)S(1)}, u32[]{:S(2)}, u32[]{:S(2)}) collective-permute-start(f32[256,128]{1,0:T(8,128)S(1)} %get-tuple-element.16), channel_id=1, source_target_pairs={{0,496},{16,0},{32,16},{48,32},{64,48},{80,64},{96,80},{112,96},{1... | collective-permute-start | bytes 393224 | tf_op jit(solution)/shard_map/ppermute | solution.py:392
  38.4 0.7 collective-permute-done.2
  39.1 3.5 %collective-permute-done.3 = f32[256,128]{1,0:T(8,128)S(1)} collective-permute-done((f32[256,128]{1,0:T(8,128)S(1)}, f32[256,128]{1,0:T(8,128)S(1)}, u32[]{:S(2)}, u32[]{:S(2)}) %collective-permute-start.3) | collective-permute-done | bytes 131104 | tf_op jit(solution)/shard_map/ppermute | solution.py:392
  42.7 8.0 %collective-permute-start.5 = (f32[256,128]{1,0:T(8,128)S(1)}, f32[256,128]{1,0:T(8,128)S(1)}, u32[]{:S(2)}, u32[]{:S(2)}) collective-permute-start(f32[256,128]{1,0:T(8,128)S(1)} %pad_maximum_fusion.1.down_ref), channel_id=1, source_target_pairs={{0,15},{1,0},{2,1},{3,2},{4,3},{5,4},{6,5},{7,6},{8,7},{9,8},{10,9... | collective-permute-start | bytes 393224 | tf_op jit(solution)/shard_map/ppermute | solution.py:392
  50.7 0.0 copy-start
  50.8 0.0 copy-start.1
  50.8 1.9 %collective-permute-start.4 = (f32[256,128]{1,0:T(8,128)S(1)}, f32[256,128]{1,0:T(8,128)S(1)}, u32[]{:S(2)}, u32[]{:S(2)}) collective-permute-start(f32[256,128]{1,0:T(8,128)S(1)} %pad_maximum_fusion.up_ref), channel_id=1, source_target_pairs={{0,1},{1,2},{2,3},{3,4},{4,5},{5,6},{6,7},{7,8},{8,9},{9,10},{10,1... | collective-permute-start | bytes 393224 | tf_op jit(solution)/shard_map/ppermute | solution.py:392
  52.7 0.1 copy.28
  52.8 0.1 copy.29.wten_t_ref
  52.9 0.0 copy-start.11
  52.9 0.7 copy-done.11
  53.6 0.1 copy.30.wout_ref
  53.7 0.0 collective-permute-done.5.above_ref
  53.7 7.8 %collective-permute-done.4.below_ref = f32[256,128]{1,0:T(8,128)S(1)} collective-permute-done((f32[256,128]{1,0:T(8,128)S(1)}, f32[256,128]{1,0:T(8,128)S(1)}, u32[]{:S(2)}, u32[]{:S(2)}) %collective-permute-start.4) | collective-permute-done | bytes 131104 | tf_op jit(solution)/shard_map/ppermute | solution.py:392
  61.6 1.2 %copy-done.5 = f32[128,2048]{1,0:T(8,128)S(1)} copy-done((f32[128,2048]{1,0:T(8,128)S(1)}, f32[128,2048]{1,0:T(8,128)}, u32[]{:S(2)}) %copy-start.5) | copy-done | bytes 1048600
  62.8 5.5 %shard_map.141 = (f32[256,128]{1,0:T(8,128)S(1)}, f32[256,128]{1,0:T(8,128)S(1)}, f32[128,2048]{1,0:T(8,128)S(1)}, f32[8,2048]{1,0:T(8,128)S(1)}) custom-call(s32[1]{0:T(128)} %get-tuple-element.15.count_ref, f32[256,128]{1,0:T(8,128)S(1)} %pad_maximum_fusion.up_ref, f32[256,128]{1,0:T(8,128)S(1)} %pad_maximum_fusion.1.down_ref, ...), custom_call_target="tpu_custom_call" | custom-call | flops 1000000000 | bytes 1048576 | tf_op jit(solution)/shard_map/pallas_call | solution.py:437
  68.3 1.9 %collective-permute-start.6 = (f32[256,128]{1,0:T(8,128)S(1)}, f32[256,128]{1,0:T(8,128)S(1)}, u32[]{:S(2)}, u32[]{:S(2)}) collective-permute-start(f32[256,128]{1,0:T(8,128)S(1)} %get-tuple-element.21), channel_id=1, source_target_pairs={{0,16},{16,32},{32,48},{48,64},{64,80},{80,96},{96,112},{112,128},... | collective-permute-start | bytes 393224 | tf_op jit(solution)/shard_map/ppermute | solution.py:392
  70.2 9.7 %collective-permute-start.7 = (f32[256,128]{1,0:T(8,128)S(1)}, f32[256,128]{1,0:T(8,128)S(1)}, u32[]{:S(2)}, u32[]{:S(2)}) collective-permute-start(f32[256,128]{1,0:T(8,128)S(1)} %get-tuple-element.20), channel_id=1, source_target_pairs={{0,496},{16,0},{32,16},{48,32},{64,48},{80,64},{96,80},{112,96},{1... | collective-permute-start | bytes 393224 | tf_op jit(solution)/shard_map/ppermute | solution.py:392
  79.9 0.7 collective-permute-done.6
  80.6 1.8 %collective-permute-done.7 = f32[256,128]{1,0:T(8,128)S(1)} collective-permute-done((f32[256,128]{1,0:T(8,128)S(1)}, f32[256,128]{1,0:T(8,128)S(1)}, u32[]{:S(2)}, u32[]{:S(2)}) %collective-permute-start.7) | collective-permute-done | bytes 131104 | tf_op jit(solution)/shard_map/ppermute | solution.py:392
  82.4 1.9 %collective-permute-start.9 = (f32[256,128]{1,0:T(8,128)S(1)}, f32[256,128]{1,0:T(8,128)S(1)}, u32[]{:S(2)}, u32[]{:S(2)}) collective-permute-start(f32[256,128]{1,0:T(8,128)S(1)} %pad_maximum_fusion.3.down_ref), channel_id=1, source_target_pairs={{0,15},{1,0},{2,1},{3,2},{4,3},{5,4},{6,5},{7,6},{8,7},{9,8},{10,9... | collective-permute-start | bytes 393224 | tf_op jit(solution)/shard_map/ppermute | solution.py:392
  84.4 3.9 %collective-permute-start.8 = (f32[256,128]{1,0:T(8,128)S(1)}, f32[256,128]{1,0:T(8,128)S(1)}, u32[]{:S(2)}, u32[]{:S(2)}) collective-permute-start(f32[256,128]{1,0:T(8,128)S(1)} %pad_maximum_fusion.2.up_ref), channel_id=1, source_target_pairs={{0,1},{1,2},{2,3},{3,4},{4,5},{5,6},{6,7},{7,8},{8,9},{9,10},{10,1... | collective-permute-start | bytes 393224 | tf_op jit(solution)/shard_map/ppermute | solution.py:392
  88.3 0.1 copy.31.wenv_ref
  88.4 0.9 collective-permute-done.9.above_ref
  89.3 5.9 %collective-permute-done.8.below_ref = f32[256,128]{1,0:T(8,128)S(1)} collective-permute-done((f32[256,128]{1,0:T(8,128)S(1)}, f32[256,128]{1,0:T(8,128)S(1)}, u32[]{:S(2)}, u32[]{:S(2)}) %collective-permute-start.8) | collective-permute-done | bytes 131104 | tf_op jit(solution)/shard_map/ppermute | solution.py:392
  95.1 4.9 %shard_map.142 = (f32[16,128]{1,0:T(8,128)S(1)}, f32[16,128]{1,0:T(8,128)S(1)}) custom-call(s32[1]{0:T(128)} %get-tuple-element.15.count_ref, f32[256,128]{1,0:T(8,128)S(1)} %pad_maximum_fusion.2.up_ref, f32[256,128]{1,0:T(8,128)S(1)} %pad_maximum_fusion.3.down_ref, f32[256,128]{1,0:T(8,128)S(1)} %collective-permute-done.8.below_ref, ...), custom_call_target="tpu_custom_call" | custom-call | flops 500000000 | bytes 1048576 | tf_op jit(solution)/shard_map/pallas_call | solution.py:446
  100.0 2.0 %collective-permute-start.10 = (f32[16,128]{1,0:T(8,128)S(1)}, f32[16,128]{1,0:T(8,128)S(1)}, u32[]{:S(2)}, u32[]{:S(2)}) collective-permute-start(f32[16,128]{1,0:T(8,128)S(1)} %get-tuple-element.27), channel_id=1, source_target_pairs={{0,1},{1,2},{2,3},{3,4},{4,5},{5,6},{6,7},{7,8},{8,9},{9,10},{10,1... | collective-permute-start | bytes 24584 | tf_op jit(solution)/shard_map/ppermute | solution.py:392
  102.0 7.5 %collective-permute-done.10 = f32[16,128]{1,0:T(8,128)S(1)} collective-permute-done((f32[16,128]{1,0:T(8,128)S(1)}, f32[16,128]{1,0:T(8,128)S(1)}, u32[]{:S(2)}, u32[]{:S(2)}) %collective-permute-start.10) | collective-permute-done | bytes 8224 | tf_op jit(solution)/shard_map/ppermute | solution.py:392
  109.6 1.9 %collective-permute-start.11 = (f32[8,128]{1,0:T(8,128)S(1)}, f32[8,128]{1,0:T(8,128)S(1)}, u32[]{:S(2)}, u32[]{:S(2)}) collective-permute-start(f32[8,128]{1,0:T(8,128)S(1)} %slice.75), channel_id=1, source_target_pairs={{0,16},{16,32},{32,48},{48,64},{64,80},{80,96},{96,112},{112,128},... | collective-permute-start | bytes 12296 | tf_op jit(solution)/shard_map/ppermute | solution.py:392
  111.5 9.0 %collective-permute-done.11 = f32[8,128]{1,0:T(8,128)S(1)} collective-permute-done((f32[8,128]{1,0:T(8,128)S(1)}, f32[8,128]{1,0:T(8,128)S(1)}, u32[]{:S(2)}, u32[]{:S(2)}) %collective-permute-start.11) | collective-permute-done | bytes 4128 | tf_op jit(solution)/shard_map/ppermute | solution.py:392
  120.5 0.5 slice_bitcast_fusion.1
  121.0 0.6 copy.32
  (41 shorter events, 0.3 us)
Async XLA Ops:
  0.6 0.7 copy-start.10
  1.3 0.7 copy-start.12
  1.3 0.7 copy-start.13
  2.0 10.0 %copy-start.6 = (s32[1,1,128,8]{2,3,1,0:T(8,128)S(1)}, s32[1,1,128,8]{2,3,1,0:T(8,128)}, u32[]{:S(2)}) copy-start(s32[1,1,128,8]{2,3,1,0:T(8,128)} %param.17) | copy-start | bytes 12292
  2.0 10.0 %copy-start.7 = (s32[1,1,128,8]{2,3,1,0:T(8,128)S(1)}, s32[1,1,128,8]{2,3,1,0:T(8,128)}, u32[]{:S(2)}) copy-start(s32[1,1,128,8]{2,3,1,0:T(8,128)} %param.15) | copy-start | bytes 12292
  2.0 11.2 %collective-permute-start = (f32[8,128]{1,0:T(8,128)S(1)}, f32[8,128]{1,0:T(8,128)S(1)}, u32[]{:S(2)}, u32[]{:S(2)}) collective-permute-start(f32[8,128]{1,0:T(8,128)S(1)} %concatenate.27), channel_id=1, source_target_pairs={{0,496},{16,0},{32,16},{48,32},{64,48},{80,64},{96,80},{112,96},{1... | collective-permute-start | bytes 12296 | tf_op jit(solution)/shard_map/ppermute | solution.py:392
  13.3 7.7 %copy-start.8 = (f32[2,128]{1,0:T(2,128)S(1)}, f32[2,128]{1,0:T(2,128)}, u32[]{:S(2)}) copy-start(f32[2,128]{1,0:T(2,128)} %param.21) | copy-start | bytes 3076
  13.3 7.7 %copy-start.9 = (f32[2,128]{1,0:T(2,128)S(1)}, f32[2,128]{1,0:T(2,128)}, u32[]{:S(2)}) copy-start(f32[2,128]{1,0:T(2,128)} %param.20) | copy-start | bytes 3076
  13.3 9.1 %collective-permute-start.1 = (f32[32,128]{1,0:T(8,128)S(1)}, f32[32,128]{1,0:T(8,128)S(1)}, u32[]{:S(2)}, u32[]{:S(2)}) collective-permute-start(f32[32,128]{1,0:T(8,128)S(1)} %concatenate.28), channel_id=1, source_target_pairs={{0,15},{1,0},{2,1},{3,2},{4,3},{5,4},{6,5},{7,6},{8,7},{9,8},{10,9... | collective-permute-start | bytes 49160 | tf_op jit(solution)/shard_map/ppermute | solution.py:392
  21.1 0.7 copy-start.2
  21.8 0.7 copy-start.3
  26.8 26.9 %copy-start.4 = (f32[128,2048]{1,0:T(8,128)}, f32[128,2048]{1,0:T(8,128)S(1)}, u32[]{:S(2)}) copy-start(f32[128,2048]{1,0:T(8,128)S(1)} %get-tuple-element.18.lat_ref) | copy-start | bytes 3145732
  26.8 12.3 %collective-permute-start.2 = (f32[256,128]{1,0:T(8,128)S(1)}, f32[256,128]{1,0:T(8,128)S(1)}, u32[]{:S(2)}, u32[]{:S(2)}) collective-permute-start(f32[256,128]{1,0:T(8,128)S(1)} %get-tuple-element.17), channel_id=1, source_target_pairs={{0,16},{16,32},{32,48},{48,64},{64,80},{80,96},{96,112},{112,128},... | collective-permute-start | bytes 393224 | tf_op jit(solution)/shard_map/ppermute | solution.py:392
  28.7 14.0 %collective-permute-start.3 = (f32[256,128]{1,0:T(8,128)S(1)}, f32[256,128]{1,0:T(8,128)S(1)}, u32[]{:S(2)}, u32[]{:S(2)}) collective-permute-start(f32[256,128]{1,0:T(8,128)S(1)} %get-tuple-element.16), channel_id=1, source_target_pairs={{0,496},{16,0},{32,16},{48,32},{64,48},{80,64},{96,80},{112,96},{1... | collective-permute-start | bytes 393224 | tf_op jit(solution)/shard_map/ppermute | solution.py:392
  42.7 11.0 %collective-permute-start.5 = (f32[256,128]{1,0:T(8,128)S(1)}, f32[256,128]{1,0:T(8,128)S(1)}, u32[]{:S(2)}, u32[]{:S(2)}) collective-permute-start(f32[256,128]{1,0:T(8,128)S(1)} %pad_maximum_fusion.1.down_ref), channel_id=1, source_target_pairs={{0,15},{1,0},{2,1},{3,2},{4,3},{5,4},{6,5},{7,6},{8,7},{9,8},{10,9... | collective-permute-start | bytes 393224 | tf_op jit(solution)/shard_map/ppermute | solution.py:392
  50.7 2.0 %copy-start = (f32[128,128]{1,0:T(8,128)S(1)}, f32[128,128]{1,0:T(8,128)}, u32[]{:S(2)}) copy-start(f32[128,128]{1,0:T(8,128)} %wlat_ref.1) | copy-start | bytes 196612
  50.8 2.0 %copy-start.1 = (f32[2,32,128]{2,1,0:T(8,128)S(1)}, f32[2,32,128]{2,1,0:T(8,128)}, u32[]{:S(2)}) copy-start(f32[2,32,128]{2,1,0:T(8,128)} %param.24) | copy-start | bytes 98308
  50.8 10.8 %collective-permute-start.4 = (f32[256,128]{1,0:T(8,128)S(1)}, f32[256,128]{1,0:T(8,128)S(1)}, u32[]{:S(2)}, u32[]{:S(2)}) collective-permute-start(f32[256,128]{1,0:T(8,128)S(1)} %pad_maximum_fusion.up_ref), channel_id=1, source_target_pairs={{0,1},{1,2},{2,3},{3,4},{4,5},{5,6},{6,7},{7,8},{8,9},{9,10},{10,1... | collective-permute-start | bytes 393224 | tf_op jit(solution)/shard_map/ppermute | solution.py:392
  52.9 0.7 copy-start.11
  61.6 1.2 %copy-start.5 = (f32[128,2048]{1,0:T(8,128)S(1)}, f32[128,2048]{1,0:T(8,128)}, u32[]{:S(2)}) copy-start(f32[128,2048]{1,0:T(8,128)} %copy-done.4) | copy-start | bytes 3145732
  68.3 12.3 %collective-permute-start.6 = (f32[256,128]{1,0:T(8,128)S(1)}, f32[256,128]{1,0:T(8,128)S(1)}, u32[]{:S(2)}, u32[]{:S(2)}) collective-permute-start(f32[256,128]{1,0:T(8,128)S(1)} %get-tuple-element.21), channel_id=1, source_target_pairs={{0,16},{16,32},{32,48},{48,64},{64,80},{80,96},{96,112},{112,128},... | collective-permute-start | bytes 393224 | tf_op jit(solution)/shard_map/ppermute | solution.py:392
  70.2 12.2 %collective-permute-start.7 = (f32[256,128]{1,0:T(8,128)S(1)}, f32[256,128]{1,0:T(8,128)S(1)}, u32[]{:S(2)}, u32[]{:S(2)}) collective-permute-start(f32[256,128]{1,0:T(8,128)S(1)} %get-tuple-element.20), channel_id=1, source_target_pairs={{0,496},{16,0},{32,16},{48,32},{64,48},{80,64},{96,80},{112,96},{1... | collective-permute-start | bytes 393224 | tf_op jit(solution)/shard_map/ppermute | solution.py:392
  82.4 6.9 %collective-permute-start.9 = (f32[256,128]{1,0:T(8,128)S(1)}, f32[256,128]{1,0:T(8,128)S(1)}, u32[]{:S(2)}, u32[]{:S(2)}) collective-permute-start(f32[256,128]{1,0:T(8,128)S(1)} %pad_maximum_fusion.3.down_ref), channel_id=1, source_target_pairs={{0,15},{1,0},{2,1},{3,2},{4,3},{5,4},{6,5},{7,6},{8,7},{9,8},{10,9... | collective-permute-start | bytes 393224 | tf_op jit(solution)/shard_map/ppermute | solution.py:392
  84.4 10.8 %collective-permute-start.8 = (f32[256,128]{1,0:T(8,128)S(1)}, f32[256,128]{1,0:T(8,128)S(1)}, u32[]{:S(2)}, u32[]{:S(2)}) collective-permute-start(f32[256,128]{1,0:T(8,128)S(1)} %pad_maximum_fusion.2.up_ref), channel_id=1, source_target_pairs={{0,1},{1,2},{2,3},{3,4},{4,5},{5,6},{6,7},{7,8},{8,9},{9,10},{10,1... | collective-permute-start | bytes 393224 | tf_op jit(solution)/shard_map/ppermute | solution.py:392
  100.0 9.5 %collective-permute-start.10 = (f32[16,128]{1,0:T(8,128)S(1)}, f32[16,128]{1,0:T(8,128)S(1)}, u32[]{:S(2)}, u32[]{:S(2)}) collective-permute-start(f32[16,128]{1,0:T(8,128)S(1)} %get-tuple-element.27), channel_id=1, source_target_pairs={{0,1},{1,2},{2,3},{3,4},{4,5},{5,6},{6,7},{7,8},{8,9},{9,10},{10,1... | collective-permute-start | bytes 24584 | tf_op jit(solution)/shard_map/ppermute | solution.py:392
  109.6 10.9 %collective-permute-start.11 = (f32[8,128]{1,0:T(8,128)S(1)}, f32[8,128]{1,0:T(8,128)S(1)}, u32[]{:S(2)}, u32[]{:S(2)}) collective-permute-start(f32[8,128]{1,0:T(8,128)S(1)} %slice.75), channel_id=1, source_target_pairs={{0,16},{16,32},{32,48},{48,64},{64,80},{80,96},{96,112},{112,128},... | collective-permute-start | bytes 12296 | tf_op jit(solution)/shard_map/ppermute | solution.py:392

commit v2 on v1

--- a/solution.py
+++ b/solution.py
@@ -216,12 +216,14 @@
     lax.fori_loop(0, blocks, lone, 0)
 
 
-def fill_tables(up_ref, down_ref, from_below_ref, from_above_ref, table_ref):
-    own = down_ref[0:128] + from_below_ref[0:128]
-    in_x = down_ref[128:256] + from_below_ref[128:256]
-    in_y = up_ref[0:128] + from_above_ref[0:128]
-    in_c = up_ref[128:256] + from_above_ref[128:256]
-    for place, values in enumerate((own, in_x, in_y, in_c)):
+def fill_tables(odd_ref, one_ref, two_ref, one_in_ref, two_in_ref, table_ref):
+    odd = odd_ref[0] == 1
+    one = one_ref[...] + one_in_ref[...]
+    two = two_ref[...] + two_in_ref[...]
+    down = jnp.where(odd, two, one)
+    up = jnp.where(odd, one, two)
+    own = down[0:128]
+    for place, values in enumerate((own, down[128:256], up[0:128], up[128:256])):
         high, low = halves(values)
         table_ref[0:128, place * 128 : (place + 1) * 128] = high
         table_ref[128:256, place * 128 : (place + 1) * 128] = low
@@ -241,10 +243,10 @@
 
 
 def second_kernel(
-    count_ref, up_ref, down_ref, below_ref, above_ref, lat_ref, geo_ref, wlat_t_ref, wlat_ref, wten_t_ref, wten_ref, wout_ref,
+    count_ref, odd_ref, one_ref, two_ref, one_in_ref, two_in_ref, lat_ref, geo_ref, wlat_t_ref, wlat_ref, wten_t_ref, wten_ref, wout_ref,
     xc_ref, oy_ref, glat_ref, rows_ref, table_ref,
 ):
-    own = fill_tables(up_ref, down_ref, below_ref, above_ref, table_ref)
+    own = fill_tables(odd_ref, one_ref, two_ref, one_in_ref, two_in_ref, table_ref)
     blocks = (count_ref[0] + (LONE - 1)) // LONE
     wout = wout_ref[...]
     xc_ref[...] = jnp.zeros_like(xc_ref)
@@ -302,10 +304,10 @@
 
 
 def third_kernel(
-    count_ref, up_ref, down_ref, below_ref, above_ref, dlat_ref, wl_ref, glat_ref, geo_ref, rows_ref, wenv_ref, wbasis_ref,
+    count_ref, odd_ref, one_ref, two_ref, one_in_ref, two_in_ref, dlat_ref, wl_ref, glat_ref, geo_ref, rows_ref, wenv_ref, wbasis_ref,
     yc_ref, ox_ref, table_ref,
 ):
-    own = fill_tables(up_ref, down_ref, below_ref, above_ref, table_ref)
+    own = fill_tables(odd_ref, one_ref, two_ref, one_in_ref, two_in_ref, table_ref)
     blocks = (count_ref[0] + (LONE - 1)) // LONE
     yc_ref[...] = jnp.zeros_like(yc_ref)
     ox_ref[...] = jnp.zeros_like(ox_ref)
@@ -387,19 +389,60 @@
 IN_SMEM = pl.BlockSpec(memory_space=pltpu.SMEM)
 
 
-def step(block, axis, distance):
-    size = lax.axis_size(axis)
-    return lax.ppermute(block, axis, [(i, (i + distance) % size) for i in range(size)])
-
-
-def butterfly(xc, oy):
-    from_left = step(xc, "gx", 1)
-    from_right = step(oy, "gx", -1)
-    here = oy + from_left
-    beside = xc + from_right
+BOXES_X, BOXES_Y = 32, 16
+RUNGS = [(y, half if y % 2 == 0 else 1 - half) for y in range(8) for half in range(2)]
+RUNGS = RUNGS[4:] + RUNGS[:4]
+AROUND = {(0, 0): 0, (0, 1): 1, (1, 1): 2, (1, 0): 3}
+
+
+def at_home(p, q):
+    return (p % BOXES_X) * BOXES_Y + q % BOXES_Y
+
+
+def at_work(p, q):
+    chip, core = (p % BOXES_X) // 2, p % 2
+    z, left = (chip, 0) if chip < 8 else (15 - chip, 1)
+    y, right = RUNGS[q % BOXES_Y]
+    x = AROUND[(left, right)]
+    return (((y // 4) * 8 + z) * 2 + core) * BOXES_Y + (y % 4) * 4 + x
+
+
+def odd_box():
+    gx, gy = lax.axis_index("gx"), lax.axis_index("gy")
+    y = (gx // 16) * 4 + gy // 4
+    right = (gy % 4 + 1) // 2
+    return gx % 2 == 1, (y + right) % 2 == 1
+
+
+def move(block, source, target, shift):
+    pairs = [
+        (source(p + shift[0], q + shift[1]), target(p, q)) for p in range(BOXES_X) for q in range(BOXES_Y)
+    ]
+    return lax.ppermute(block, ("gx", "gy"), pairs)
+
+
+def trade(block, axis, first):
+    pairs = []
+    for p in range(BOXES_X):
+        for q in range(BOXES_Y):
+            away = 1 if (p, q)[axis] % 2 == first else -1
+            pairs.append((at_work(p + away * (axis == 0), q + away * (axis == 1)), at_work(p, q)))
+    return lax.ppermute(block, ("gx", "gy"), pairs)
+
+
+def butterfly(xc, oy, odd_p, odd_q):
+    far = jnp.where(odd_p, xc, oy)
+    near = jnp.where(odd_p, oy, xc)
+    far_in = trade(far, 0, 1)
+    near_in = trade(near, 0, 0)
+    far, near = far + far_in, near + near_in
+    here = jnp.where(odd_p, near, far)
+    beside = jnp.where(odd_p, far, near)
     up = jnp.concatenate([here[128:256], beside[128:256]], axis=0)
     down = jnp.concatenate([here[0:128], beside[0:128]], axis=0)
-    return up, down, step(up, "gy", 1), step(down, "gy", -1)
+    one = jnp.where(odd_q, up, down)
+    two = jnp.where(odd_q, down, up)
+    return one, two, trade(one, 1, 1), trade(two, 1, 0)
 
 
 def local(
@@ -415,9 +458,12 @@
         ],
         axis=0,
     )
-    in_x = step(base, "gx", -1)
+    odd_p, odd_q = odd_box()
+    odd = odd_q.astype(jnp.int32).reshape(1)
+    in_x = move(base, at_home, at_work, (1, 0))
     own = jnp.concatenate([base, neighbours[0, 0].T.astype(F32), image_z[0, 0].T.astype(F32)], axis=0)
-    in_yc = step(jnp.concatenate([own, in_x], axis=0), "gy", -1)
+    own = move(own, at_home, at_work, (0, 0))
+    in_yc = move(jnp.concatenate([own, in_x], axis=0), at_work, at_work, (0, 1))
 
     wfeat = jnp.concatenate(
         [w_basis, (w_center[0] + w_neigh[0])[None], (w_center[1] - w_center[0])[None], (w_neigh[1] - w_neigh[0])[None],
@@ -432,28 +478,27 @@
         [pltpu.VMEM((16, ATOMS), F32)],
         500_000_000,
     )(own, in_x, in_yc, wfeat, w_env.T)
-    up, down, below, above = butterfly(xc, oy)
+    one, two, one_in, two_in = butterfly(xc, oy, odd_p, odd_q)
     wten = w_tensor.reshape(2 * TC, 128)
     xc, oy, glat, rows = call(
         second_kernel,
         (shape(256, 128), shape(256, 128), shape(128, 2 * EDGES), shape(8, 2 * EDGES)),
-        [IN_SMEM] + [IN_VMEM] * 11,
+        [IN_SMEM] * 2 + [IN_VMEM] * 11,
         (IN_VMEM,) * 4,
         [pltpu.VMEM((256, 512), BF16)],
         1_000_000_000,
-    )(count, up, down, below, above, lat, geo, w_latent.T, w_latent, wten.T, wten, w_out[:, None])
-    up, down, below, above = butterfly(xc, oy)
+    )(count, odd, one, two, one_in, two_in, lat, geo, w_latent.T, w_latent, wten.T, wten, w_out[:, None])
+    one, two, one_in, two_in = butterfly(xc, oy, odd_p, odd_q)
     yc, ox = call(
         third_kernel,
         (shape(16, 128), shape(16, 128)),
-        [IN_SMEM] + [IN_VMEM] * 11,
+        [IN_SMEM] * 2 + [IN_VMEM] * 11,
         (IN_VMEM,) * 2,
         [pltpu.VMEM((256, 512), BF16)],
         500_000_000,
-    )(count, up, down, below, above, dlat, wl, glat, geo, rows, w_env, w_basis)
-    yc = step(yc, "gy", 1)
-    ox = ox + yc
-    total = ox[0:8] + step(ox[8:16], "gx", 1)
+    )(count, odd, one, two, one_in, two_in, dlat, wl, glat, geo, rows, w_env, w_basis)
+    ox = ox + move(yc, at_work, at_work, (0, -1))
+    total = move(ox[8:16], at_work, at_home, (-1, 0)) + move(ox[0:8], at_work, at_home, (0, 0))
     return (total[0:3][None, None], total[3][None, None])
 
 

time: 122 us -> 111 us (0.910)
  the two profiles are of different devices: /device:TPU:32 before, /device:TPU:96 now
where the time goes in v2:
time: 111 us; the launch traced here: 110 us
  starting transfers between devices  48 us (43%)
  waiting for transfers between devices  38.4 us (35%)
  Pallas kernels  14.6 us (13%)
  local copies, waits for them, and re-layouts  6.28 us (6%)
  other arithmetic  1.54 us (1%)
    ppermute x6, starting transfers between devices, move(): return lax.ppermute(block, ('gx', 'gy'), pairs)  24.9 us
    ppermute x8, starting transfers between devices, trade(): return lax.ppermute(block, ('gx', 'gy'), pairs)  23.1 us
    ppermute x6, waiting for transfers between devices, move(): return lax.ppermute(block, ('gx', 'gy'), pairs)  22.1 us
    ppermute x8, waiting for transfers between devices, trade(): return lax.ppermute(block, ('gx', 'gy'), pairs)  16.2 us
    pallas_call x1, Pallas kernels, local(): call(second_kernel, (shape(256, 128), shape(256, 128), shape(128, 2 * EDG...  5.5 us
    unnamed x28, local copies, waits for them, and re-layouts  5.33 us
    pallas_call x1, Pallas kernels, local(): call(third_kernel, (shape(16, 128), shape(16, 128)), [IN_SMEM] * 2 + [IN_...  4.9 us
    pallas_call x1, Pallas kernels, local(): call(first_kernel, (shape(256, 128), shape(256, 128), shape(128, 2 * EDGE...  4.24 us
  transfers between devices with their start and end apart: 14, of which 10 were waited for; matrix products, arithmetic and copies ran while one was open for 0% of the time, Pallas kernels for 0%

profile of v2, /device:TPU:96, one launch (start us, length us, event | category | flops | bytes accessed | tf_op | source)
XLA Modules:
  0.0 109.8 jit_solution(3090098572449829117)
XLA Ops:
  0.6 0.7 copy.35
  1.4 0.7 copy-done.11
  2.0 0.7 convert_bitcast_fusion.2
  2.7 0.7 convert_bitcast_fusion
  3.4 12.0 %collective-permute-start = (f32[24,128]{1,0:T(8,128)S(1)}, f32[24,128]{1,0:T(8,128)S(1)}, u32[]{:S(2)}, u32[]{:S(2)}) collective-permute-start(f32[24,128]{1,0:T(8,128)S(1)} %concatenate.25), channel_id=1, source_target_pairs={{0,8},{1,9},{2,13},{3,12},{4,256},{5,257},{6,261},{7,260},{8,264},... | collective-permute-start | bytes 36872 | tf_op jit(solution)/shard_map/ppermute | solution.py:421
  15.4 0.0 copy-start.8
  15.4 4.2 %collective-permute-start.1 = (f32[8,128]{1,0:T(8,128)S(1)}, f32[8,128]{1,0:T(8,128)S(1)}, u32[]{:S(2)}, u32[]{:S(2)}) collective-permute-start(f32[8,128]{1,0:T(8,128)S(1)} %concatenate.26), channel_id=1, source_target_pairs={{16,8},{17,9},{18,13},{19,12},{20,256},{21,257},{22,261},{23,260},... | collective-permute-start | bytes 12296 | tf_op jit(solution)/shard_map/ppermute | solution.py:421
  19.7 3.7 %collective-permute-done.1.x_ref = f32[8,128]{1,0:T(8,128)S(1)} collective-permute-done((f32[8,128]{1,0:T(8,128)S(1)}, f32[8,128]{1,0:T(8,128)S(1)}, u32[]{:S(2)}, u32[]{:S(2)}) %collective-permute-start.1) | collective-permute-done | bytes 4128 | tf_op jit(solution)/shard_map/ppermute | solution.py:421
  23.4 0.0 collective-permute-done.own_ref
  23.4 1.9 %collective-permute-start.2 = (f32[32,128]{1,0:T(8,128)S(1)}, f32[32,128]{1,0:T(8,128)S(1)}, u32[]{:S(2)}, u32[]{:S(2)}) collective-permute-start(f32[32,128]{1,0:T(8,128)S(1)} %pad_maximum_fusion.4), channel_id=1, source_target_pairs={{9,8},{13,9},{12,13},{256,12},{257,256},{261,257},{260,261},{264,2... | collective-permute-start | bytes 49160 | tf_op jit(solution)/shard_map/ppermute | solution.py:421
  25.3 0.0 copy-start.2
  25.4 0.7 copy-done.2
  26.0 0.1 copy.27
  26.1 2.8 %collective-permute-done.2.yc_ref = f32[32,128]{1,0:T(8,128)S(1)} collective-permute-done((f32[32,128]{1,0:T(8,128)S(1)}, f32[32,128]{1,0:T(8,128)S(1)}, u32[]{:S(2)}, u32[]{:S(2)}) %collective-permute-start.2) | collective-permute-done | bytes 16416 | tf_op jit(solution)/shard_map/ppermute | solution.py:421
  29.0 4.2 %shard_map.140 = (f32[256,128]{1,0:T(8,128)S(1)}, f32[256,128]{1,0:T(8,128)S(1)}, f32[128,2048]{1,0:T(8,128)S(1)}, f32[128,2048]{1,0:T(8,128)S(1)}, f32[32,2048]...) custom-call(f32[24,128]{1,0:T(8,128)S(1)} %collective-permute-done.own_ref, ...), custom_call_target="tpu_custom_call" | custom-call | flops 500000000 | bytes 1048576 | tf_op jit(solution)/shard_map/pallas_call | solution.py:472
  33.3 1.9 %collective-permute-start.3 = (f32[256,128]{1,0:T(8,128)S(1)}, f32[256,128]{1,0:T(8,128)S(1)}, u32[]{:S(2)}, u32[]{:S(2)}) collective-permute-start(f32[256,128]{1,0:T(8,128)S(1)} %get-tuple-element.42), channel_id=1, source_target_pairs={{24,8},{25,9},{29,13},{28,12},{272,256},{273,257},{277,261},{276,2... | collective-permute-start | bytes 393224 | tf_op jit(solution)/shard_map/ppermute | solution.py:430
  35.2 2.6 %collective-permute-start.4 = (f32[256,128]{1,0:T(8,128)S(1)}, f32[256,128]{1,0:T(8,128)S(1)}, u32[]{:S(2)}, u32[]{:S(2)}) collective-permute-start(f32[256,128]{1,0:T(8,128)S(1)} %get-tuple-element.43), channel_id=1, source_target_pairs={{27,8},{26,9},{30,13},{31,12},{275,256},{274,257},{278,261},{279,2... | collective-permute-start | bytes 393224 | tf_op jit(solution)/shard_map/ppermute | solution.py:430
  37.9 3.6 %collective-permute-done.4 = f32[256,128]{1,0:T(8,128)S(1)} collective-permute-done((f32[256,128]{1,0:T(8,128)S(1)}, f32[256,128]{1,0:T(8,128)S(1)}, u32[]{:S(2)}, u32[]{:S(2)}) %collective-permute-start.4) | collective-permute-done | bytes 131104 | tf_op jit(solution)/shard_map/ppermute | solution.py:430
  41.6 0.0 copy-start
  41.6 3.1 %collective-permute-start.5 = (f32[256,128]{1,0:T(8,128)S(1)}, f32[256,128]{1,0:T(8,128)S(1)}, u32[]{:S(2)}, u32[]{:S(2)}) collective-permute-start(f32[256,128]{1,0:T(8,128)S(1)} %get-tuple-element.41.one_ref), channel_id=1, source_target_pairs={{4,8},{13,9},{9,13},{256,12},{12,256},{261,257},{257,261},{264,260... | collective-permute-start | bytes 393224 | tf_op jit(solution)/shard_map/ppermute | solution.py:430
  44.8 5.4 %collective-permute-start.6 = (f32[256,128]{1,0:T(8,128)S(1)}, f32[256,128]{1,0:T(8,128)S(1)}, u32[]{:S(2)}, u32[]{:S(2)}) collective-permute-start(f32[256,128]{1,0:T(8,128)S(1)} %get-tuple-element.40.two_ref), channel_id=1, source_target_pairs={{9,8},{8,9},{12,13},{13,12},{257,256},{256,257},{260,261},{261,260... | collective-permute-start | bytes 393224 | tf_op jit(solution)/shard_map/ppermute | solution.py:430
  50.2 0.0 copy-start.1
  50.2 0.1 copy.28
  50.3 0.7 copy-done.1
  50.9 0.1 copy.29.wten_t_ref
  51.0 0.0 copy-start.10
  51.0 0.7 copy-done.10
  51.7 0.1 copy.30.wout_ref
  51.8 2.2 %collective-permute-done.6.two_in_ref = f32[256,128]{1,0:T(8,128)S(1)} collective-permute-done((f32[256,128]{1,0:T(8,128)S(1)}, f32[256,128]{1,0:T(8,128)S(1)}, u32[]{:S(2)}, u32[]{:S(2)}) %collective-permute-start.6) | collective-permute-done | bytes 131104 | tf_op jit(solution)/shard_map/ppermute | solution.py:430
  54.0 1.2 %copy-done.5 = f32[128,2048]{1,0:T(8,128)S(1)} copy-done((f32[128,2048]{1,0:T(8,128)S(1)}, f32[128,2048]{1,0:T(8,128)}, u32[]{:S(2)}) %copy-start.5) | copy-done | bytes 1048600
  55.3 5.5 %shard_map.141 = (f32[256,128]{1,0:T(8,128)S(1)}, f32[256,128]{1,0:T(8,128)S(1)}, f32[128,2048]{1,0:T(8,128)S(1)}, f32[8,2048]{1,0:T(8,128)S(1)}) custom-call(s32[1]{0:T(128)} %get-tuple-element.15.count_ref, s32[1]{0:T(128)} %bitcast.9.odd_ref, f32[256,128]{1,0:T(8,128)S(1)} %get-tuple-element.41.one_ref, f32[256,128]{1,0:T(8,128)S(1)} %get-tuple-element.40.two_ref, ...), custom_call_target="tpu_custom_call" | custom-call | flops 1000000000 | bytes 1048576 | tf_op jit(solution)/shard_map/pallas_call | solution.py:483
  60.8 1.9 %collective-permute-start.7 = (f32[256,128]{1,0:T(8,128)S(1)}, f32[256,128]{1,0:T(8,128)S(1)}, u32[]{:S(2)}, u32[]{:S(2)}) collective-permute-start(f32[256,128]{1,0:T(8,128)S(1)} %get-tuple-element.38), channel_id=1, source_target_pairs={{24,8},{25,9},{29,13},{28,12},{272,256},{273,257},{277,261},{276,2... | collective-permute-start | bytes 393224 | tf_op jit(solution)/shard_map/ppermute | solution.py:430
  62.7 2.6 %collective-permute-start.8 = (f32[256,128]{1,0:T(8,128)S(1)}, f32[256,128]{1,0:T(8,128)S(1)}, u32[]{:S(2)}, u32[]{:S(2)}) collective-permute-start(f32[256,128]{1,0:T(8,128)S(1)} %get-tuple-element.39), channel_id=1, source_target_pairs={{27,8},{26,9},{30,13},{31,12},{275,256},{274,257},{278,261},{279,2... | collective-permute-start | bytes 393224 | tf_op jit(solution)/shard_map/ppermute | solution.py:430
  65.3 3.7 %collective-permute-done.8 = f32[256,128]{1,0:T(8,128)S(1)} collective-permute-done((f32[256,128]{1,0:T(8,128)S(1)}, f32[256,128]{1,0:T(8,128)S(1)}, u32[]{:S(2)}, u32[]{:S(2)}) %collective-permute-start.8) | collective-permute-done | bytes 131104 | tf_op jit(solution)/shard_map/ppermute | solution.py:430
  69.1 3.6 %collective-permute-start.10 = (f32[256,128]{1,0:T(8,128)S(1)}, f32[256,128]{1,0:T(8,128)S(1)}, u32[]{:S(2)}, u32[]{:S(2)}) collective-permute-start(f32[256,128]{1,0:T(8,128)S(1)} %get-tuple-element.36.two_ref), channel_id=1, source_target_pairs={{9,8},{8,9},{12,13},{13,12},{257,256},{256,257},{260,261},{261,260... | collective-permute-start | bytes 393224 | tf_op jit(solution)/shard_map/ppermute | solution.py:430
  72.8 1.9 %collective-permute-start.9 = (f32[256,128]{1,0:T(8,128)S(1)}, f32[256,128]{1,0:T(8,128)S(1)}, u32[]{:S(2)}, u32[]{:S(2)}) collective-permute-start(f32[256,128]{1,0:T(8,128)S(1)} %get-tuple-element.37.one_ref), channel_id=1, source_target_pairs={{4,8},{13,9},{9,13},{256,12},{12,256},{261,257},{257,261},{264,260... | collective-permute-start | bytes 393224 | tf_op jit(solution)/shard_map/ppermute | solution.py:430
  74.7 0.1 copy.31.wenv_ref
  74.8 2.1 %collective-permute-done.10.two_in_ref = f32[256,128]{1,0:T(8,128)S(1)} collective-permute-done((f32[256,128]{1,0:T(8,128)S(1)}, f32[256,128]{1,0:T(8,128)S(1)}, u32[]{:S(2)}, u32[]{:S(2)}) %collective-permute-start.10) | collective-permute-done | bytes 131104 | tf_op jit(solution)/shard_map/ppermute | solution.py:430
  76.9 4.6 %collective-permute-done.9.one_in_ref = f32[256,128]{1,0:T(8,128)S(1)} collective-permute-done((f32[256,128]{1,0:T(8,128)S(1)}, f32[256,128]{1,0:T(8,128)S(1)}, u32[]{:S(2)}, u32[]{:S(2)}) %collective-permute-start.9) | collective-permute-done | bytes 131104 | tf_op jit(solution)/shard_map/ppermute | solution.py:430
  81.5 4.9 %shard_map.142 = (f32[16,128]{1,0:T(8,128)S(1)}, f32[16,128]{1,0:T(8,128)S(1)}) custom-call(s32[1]{0:T(128)} %get-tuple-element.15.count_ref, s32[1]{0:T(128)} %bitcast.9.odd_ref, f32[256,128]{1,0:T(8,128)S(1)} %get-tuple-element.37.one_ref, f32[256,128]{1,0:T(8,128)S(1)} %get-tuple-element.36.two_ref, f32[256,128]{1,0:T(8,128)S(1)} %collective-permute-done.9.one_in_ref, ...), custom_call_target="tpu_custom_call" | custom-call | flops 500000000 | bytes 1048576 | tf_op jit(solution)/shard_map/pallas_call | solution.py:492
  86.4 2.0 %collective-permute-start.11 = (f32[16,128]{1,0:T(8,128)S(1)}, f32[16,128]{1,0:T(8,128)S(1)}, u32[]{:S(2)}, u32[]{:S(2)}) collective-permute-start(f32[16,128]{1,0:T(8,128)S(1)} %get-tuple-element.27), channel_id=1, source_target_pairs={{4,8},{8,9},{9,13},{13,12},{12,256},{256,257},{257,261},{261,260},... | collective-permute-start | bytes 24584 | tf_op jit(solution)/shard_map/ppermute | solution.py:421
  88.4 4.8 %collective-permute-done.11 = f32[16,128]{1,0:T(8,128)S(1)} collective-permute-done((f32[16,128]{1,0:T(8,128)S(1)}, f32[16,128]{1,0:T(8,128)S(1)}, u32[]{:S(2)}, u32[]{:S(2)}) %collective-permute-start.11) | collective-permute-done | bytes 8224 | tf_op jit(solution)/shard_map/ppermute | solution.py:421
  93.2 1.9 %collective-permute-start.12 = (f32[8,128]{1,0:T(8,128)S(1)}, f32[8,128]{1,0:T(8,128)S(1)}, u32[]{:S(2)}, u32[]{:S(2)}) collective-permute-start(f32[8,128]{1,0:T(8,128)S(1)} %get-tuple-element.53), channel_id=1, source_target_pairs={{27,0},{26,1},{30,2},{31,3},{275,4},{274,5},{278,6},{279,7},{283,8... | collective-permute-start | bytes 12296 | tf_op jit(solution)/shard_map/ppermute | solution.py:421
  95.1 2.8 %collective-permute-start.13 = (f32[8,128]{1,0:T(8,128)S(1)}, f32[8,128]{1,0:T(8,128)S(1)}, u32[]{:S(2)}, u32[]{:S(2)}) collective-permute-start(f32[8,128]{1,0:T(8,128)S(1)} %get-tuple-element.52), channel_id=1, source_target_pairs={{8,0},{9,1},{13,2},{12,3},{256,4},{257,5},{261,6},{260,7},{264,8},... | collective-permute-start | bytes 12296 | tf_op jit(solution)/shard_map/ppermute | solution.py:421
  98.0 7.4 %collective-permute-done.12 = f32[8,128]{1,0:T(8,128)S(1)} collective-permute-done((f32[8,128]{1,0:T(8,128)S(1)}, f32[8,128]{1,0:T(8,128)S(1)}, u32[]{:S(2)}, u32[]{:S(2)}) %collective-permute-start.12) | collective-permute-done | bytes 4128 | tf_op jit(solution)/shard_map/ppermute | solution.py:421
  105.4 3.4 %collective-permute-done.13 = f32[8,128]{1,0:T(8,128)S(1)} collective-permute-done((f32[8,128]{1,0:T(8,128)S(1)}, f32[8,128]{1,0:T(8,128)S(1)}, u32[]{:S(2)}, u32[]{:S(2)}) %collective-permute-start.13) | collective-permute-done | bytes 4128 | tf_op jit(solution)/shard_map/ppermute | solution.py:421
  108.8 0.5 slice_bitcast_fusion.1
  109.3 0.6 copy.32
  (39 shorter events, 0.4 us)
Async XLA Ops:
  0.6 0.7 copy-start.9
  0.6 2.0 %copy-start.6 = (s32[1,1,128,8]{2,3,1,0:T(8,128)S(1)}, s32[1,1,128,8]{2,3,1,0:T(8,128)}, u32[]{:S(2)}) copy-start(s32[1,1,128,8]{2,3,1,0:T(8,128)} %param.17) | copy-start | bytes 12292
  1.3 0.7 copy-start.11
  3.4 20.0 %collective-permute-start = (f32[24,128]{1,0:T(8,128)S(1)}, f32[24,128]{1,0:T(8,128)S(1)}, u32[]{:S(2)}, u32[]{:S(2)}) collective-permute-start(f32[24,128]{1,0:T(8,128)S(1)} %concatenate.25), channel_id=1, source_target_pairs={{0,8},{1,9},{2,13},{3,12},{4,256},{5,257},{6,261},{7,260},{8,264},... | collective-permute-start | bytes 36872 | tf_op jit(solution)/shard_map/ppermute | solution.py:421
  15.4 9.9 %copy-start.7 = (f32[2,128]{1,0:T(2,128)S(1)}, f32[2,128]{1,0:T(2,128)}, u32[]{:S(2)}) copy-start(f32[2,128]{1,0:T(2,128)} %param.21) | copy-start | bytes 3076
  15.4 9.9 %copy-start.8 = (f32[2,128]{1,0:T(2,128)S(1)}, f32[2,128]{1,0:T(2,128)}, u32[]{:S(2)}) copy-start(f32[2,128]{1,0:T(2,128)} %param.20) | copy-start | bytes 3076
  15.4 7.9 %collective-permute-start.1 = (f32[8,128]{1,0:T(8,128)S(1)}, f32[8,128]{1,0:T(8,128)S(1)}, u32[]{:S(2)}, u32[]{:S(2)}) collective-permute-start(f32[8,128]{1,0:T(8,128)S(1)} %concatenate.26), channel_id=1, source_target_pairs={{16,8},{17,9},{18,13},{19,12},{20,256},{21,257},{22,261},{23,260},... | collective-permute-start | bytes 12296 | tf_op jit(solution)/shard_map/ppermute | solution.py:421
  23.4 5.6 %collective-permute-start.2 = (f32[32,128]{1,0:T(8,128)S(1)}, f32[32,128]{1,0:T(8,128)S(1)}, u32[]{:S(2)}, u32[]{:S(2)}) collective-permute-start(f32[32,128]{1,0:T(8,128)S(1)} %pad_maximum_fusion.4), channel_id=1, source_target_pairs={{9,8},{13,9},{12,13},{256,12},{257,256},{261,257},{260,261},{264,2... | collective-permute-start | bytes 49160 | tf_op jit(solution)/shard_map/ppermute | solution.py:421
  25.3 0.7 copy-start.2
  26.0 2.9 %copy-start.3 = (f32[128,32]{0,1:T(8,128)S(1)}, f32[128,32]{0,1:T(8,128)}, u32[]{:S(2)}) copy-start(f32[128,32]{0,1:T(8,128)} %param.22) | copy-start | bytes 49156
  33.2 8.4 %copy-start.4 = (f32[128,2048]{1,0:T(8,128)}, f32[128,2048]{1,0:T(8,128)S(1)}, u32[]{:S(2)}) copy-start(f32[128,2048]{1,0:T(8,128)S(1)} %get-tuple-element.18.lat_ref) | copy-start | bytes 3145732
  33.3 4.6 %collective-permute-start.3 = (f32[256,128]{1,0:T(8,128)S(1)}, f32[256,128]{1,0:T(8,128)S(1)}, u32[]{:S(2)}, u32[]{:S(2)}) collective-permute-start(f32[256,128]{1,0:T(8,128)S(1)} %get-tuple-element.42), channel_id=1, source_target_pairs={{24,8},{25,9},{29,13},{28,12},{272,256},{273,257},{277,261},{276,2... | collective-permute-start | bytes 393224 | tf_op jit(solution)/shard_map/ppermute | solution.py:430
  35.2 6.3 %collective-permute-start.4 = (f32[256,128]{1,0:T(8,128)S(1)}, f32[256,128]{1,0:T(8,128)S(1)}, u32[]{:S(2)}, u32[]{:S(2)}) collective-permute-start(f32[256,128]{1,0:T(8,128)S(1)} %get-tuple-element.43), channel_id=1, source_target_pairs={{27,8},{26,9},{30,13},{31,12},{275,256},{274,257},{278,261},{279,2... | collective-permute-start | bytes 393224 | tf_op jit(solution)/shard_map/ppermute | solution.py:430
  41.6 8.6 %copy-start = (f32[128,128]{1,0:T(8,128)S(1)}, f32[128,128]{1,0:T(8,128)}, u32[]{:S(2)}) copy-start(f32[128,128]{1,0:T(8,128)} %wlat_ref.1) | copy-start | bytes 196612
  41.6 10.2 %collective-permute-start.5 = (f32[256,128]{1,0:T(8,128)S(1)}, f32[256,128]{1,0:T(8,128)S(1)}, u32[]{:S(2)}, u32[]{:S(2)}) collective-permute-start(f32[256,128]{1,0:T(8,128)S(1)} %get-tuple-element.41.one_ref), channel_id=1, source_target_pairs={{4,8},{13,9},{9,13},{256,12},{12,256},{261,257},{257,261},{264,260... | collective-permute-start | bytes 393224 | tf_op jit(solution)/shard_map/ppermute | solution.py:430
  44.8 9.3 %collective-permute-start.6 = (f32[256,128]{1,0:T(8,128)S(1)}, f32[256,128]{1,0:T(8,128)S(1)}, u32[]{:S(2)}, u32[]{:S(2)}) collective-permute-start(f32[256,128]{1,0:T(8,128)S(1)} %get-tuple-element.40.two_ref), channel_id=1, source_target_pairs={{9,8},{8,9},{12,13},{13,12},{257,256},{256,257},{260,261},{261,260... | collective-permute-start | bytes 393224 | tf_op jit(solution)/shard_map/ppermute | solution.py:430
  50.2 0.8 copy-start.1
  51.0 0.7 copy-start.10
  54.0 1.2 %copy-start.5 = (f32[128,2048]{1,0:T(8,128)S(1)}, f32[128,2048]{1,0:T(8,128)}, u32[]{:S(2)}) copy-start(f32[128,2048]{1,0:T(8,128)} %copy-done.4) | copy-start | bytes 3145732
  60.8 4.5 %collective-permute-start.7 = (f32[256,128]{1,0:T(8,128)S(1)}, f32[256,128]{1,0:T(8,128)S(1)}, u32[]{:S(2)}, u32[]{:S(2)}) collective-permute-start(f32[256,128]{1,0:T(8,128)S(1)} %get-tuple-element.38), channel_id=1, source_target_pairs={{24,8},{25,9},{29,13},{28,12},{272,256},{273,257},{277,261},{276,2... | collective-permute-start | bytes 393224 | tf_op jit(solution)/shard_map/ppermute | solution.py:430
  62.7 6.3 %collective-permute-start.8 = (f32[256,128]{1,0:T(8,128)S(1)}, f32[256,128]{1,0:T(8,128)S(1)}, u32[]{:S(2)}, u32[]{:S(2)}) collective-permute-start(f32[256,128]{1,0:T(8,128)S(1)} %get-tuple-element.39), channel_id=1, source_target_pairs={{27,8},{26,9},{30,13},{31,12},{275,256},{274,257},{278,261},{279,2... | collective-permute-start | bytes 393224 | tf_op jit(solution)/shard_map/ppermute | solution.py:430
  69.1 7.8 %collective-permute-start.10 = (f32[256,128]{1,0:T(8,128)S(1)}, f32[256,128]{1,0:T(8,128)S(1)}, u32[]{:S(2)}, u32[]{:S(2)}) collective-permute-start(f32[256,128]{1,0:T(8,128)S(1)} %get-tuple-element.36.two_ref), channel_id=1, source_target_pairs={{9,8},{8,9},{12,13},{13,12},{257,256},{256,257},{260,261},{261,260... | collective-permute-start | bytes 393224 | tf_op jit(solution)/shard_map/ppermute | solution.py:430
  72.8 8.7 %collective-permute-start.9 = (f32[256,128]{1,0:T(8,128)S(1)}, f32[256,128]{1,0:T(8,128)S(1)}, u32[]{:S(2)}, u32[]{:S(2)}) collective-permute-start(f32[256,128]{1,0:T(8,128)S(1)} %get-tuple-element.37.one_ref), channel_id=1, source_target_pairs={{4,8},{13,9},{9,13},{256,12},{12,256},{261,257},{257,261},{264,260... | collective-permute-start | bytes 393224 | tf_op jit(solution)/shard_map/ppermute | solution.py:430
  86.4 6.8 %collective-permute-start.11 = (f32[16,128]{1,0:T(8,128)S(1)}, f32[16,128]{1,0:T(8,128)S(1)}, u32[]{:S(2)}, u32[]{:S(2)}) collective-permute-start(f32[16,128]{1,0:T(8,128)S(1)} %get-tuple-element.27), channel_id=1, source_target_pairs={{4,8},{8,9},{9,13},{13,12},{12,256},{256,257},{257,261},{261,260},... | collective-permute-start | bytes 24584 | tf_op jit(solution)/shard_map/ppermute | solution.py:421
  93.2 12.1 %collective-permute-start.12 = (f32[8,128]{1,0:T(8,128)S(1)}, f32[8,128]{1,0:T(8,128)S(1)}, u32[]{:S(2)}, u32[]{:S(2)}) collective-permute-start(f32[8,128]{1,0:T(8,128)S(1)} %get-tuple-element.53), channel_id=1, source_target_pairs={{27,0},{26,1},{30,2},{31,3},{275,4},{274,5},{278,6},{279,7},{283,8... | collective-permute-start | bytes 12296 | tf_op jit(solution)/shard_map/ppermute | solution.py:421
  95.1 13.6 %collective-permute-start.13 = (f32[8,128]{1,0:T(8,128)S(1)}, f32[8,128]{1,0:T(8,128)S(1)}, u32[]{:S(2)}, u32[]{:S(2)}) collective-permute-start(f32[8,128]{1,0:T(8,128)S(1)} %get-tuple-element.52), channel_id=1, source_target_pairs={{8,0},{9,1},{13,2},{12,3},{256,4},{257,5},{261,6},{260,7},{264,8},... | collective-permute-start | bytes 12296 | tf_op jit(solution)/shard_map/ppermute | solution.py:421

commit v3 on v2

--- a/solution.py
+++ b/solution.py
@@ -10,10 +10,10 @@
 ATOMS = 128
 SLOTS = 8
 EDGES = ATOMS * SLOTS
-WIDE = 256
+WIDE = 1024
 LONE = 128
 TC = 32
-VMEM_LIMIT = 48 * 1024 * 1024
+VMEM_LIMIT = 24 * 1024 * 1024
 
 
 def halves(x):
@@ -47,6 +47,10 @@
 def scatter(values, hot):
     high, low = halves(values)
     return dot_nt(high, hot) + dot_nt(low, hot)
+
+
+def fold(values):
+    return sum(values[:, k * ATOMS : (k + 1) * ATOMS] for k in range(WIDE // ATOMS))
 
 
 def lanes(table, index):
@@ -86,6 +90,24 @@
     inverse = 1.0 / radius
     envelope = live * jnp.exp(-0.25 * radius_sq)
     return dx * inverse, dy * inverse, dz * inverse, envelope, radius
+
+
+def pack_kernel(*refs):
+    sources, (base_ref, own_ref), held, sems = refs[:6], refs[6:8], refs[8:14], refs[14]
+    copies = [pltpu.make_async_copy(source, place, sems.at[i]) for i, (source, place) in enumerate(zip(sources, held))]
+    for copy in copies:
+        copy.start()
+    for copy in copies:
+        copy.wait()
+    positions, species, counts, sends, neighbours, images = held
+    lists = sends[0].astype(F32)
+    rows = [positions[0], positions[1], positions[2], species[0].astype(F32), lists[:, 0:ATOMS], lists[:, ATOMS:]]
+    rows += [counts[0].astype(F32), jnp.zeros((1, ATOMS), F32)]
+    for line, values in enumerate(rows):
+        base_ref[line : line + 1] = values
+        own_ref[line : line + 1] = values
+    own_ref[8:16] = neighbours[...].astype(F32)
+    own_ref[16:24] = images[...].astype(F32)
 
 
 def first_kernel(
@@ -195,16 +217,17 @@
         return geo, four(weight, unit, 1.0), four(weight, unit, -1.0)
 
     def main(block, carry):
-        spot = pl.ds(pl.multiple_of(block * WIDE, WIDE), WIDE)
+        spot = pl.ds(block * WIDE, WIDE)
         geo, centre, other = edge_block(spot)
         sums = scatter(other, one_hot(geo[7:8].astype(jnp.int32), 512))
-        oy_ref[0:128] += sums[:, 0:128] + (centre[:, 0:128] + centre[:, 128:256])
+        oy_ref[0:128] += sums[:, 0:128] + fold(centre)
         xc_ref[0:128] += sums[:, 128:256]
         oy_ref[128:256] += sums[:, 256:384]
         xc_ref[128:256] += sums[:, 384:512]
         return carry
 
-    lax.fori_loop(0, EDGES // WIDE, main, 0)
+    for block in range(EDGES // WIDE):
+        main(block, 0)
 
     def lone(block, carry):
         spot = pl.ds(pl.multiple_of(EDGES + block * LONE, LONE), LONE)
@@ -242,9 +265,42 @@
     return total
 
 
+def early_kernel(count_ref, lat_ref, wlat_t_ref, wout_ref, pre_ref, read_ref):
+    blocks = (count_ref[0] + (LONE - 1)) // LONE
+    wout = wout_ref[...]
+
+    def edge_block(spot):
+        latent = lat_ref[:, spot]
+        pre_ref[:, spot] = product(wlat_t_ref[...], latent)
+        read_ref[0:1, spot] = jnp.sum(wout * latent, axis=0, keepdims=True)
+
+    edge_block(pl.ds(0, EDGES))
+
+    def lone(block, carry):
+        edge_block(pl.ds(pl.multiple_of(EDGES + block * LONE, LONE), LONE))
+        return carry
+
+    lax.fori_loop(0, blocks, lone, 0)
+
+
+def late_kernel(count_ref, gpre_ref, geo_ref, wlat_ref, wout_ref, glat_ref):
+    blocks = (count_ref[0] + (LONE - 1)) // LONE
+
+    def edge_block(spot):
+        glat_ref[:, spot] = wout_ref[...] * geo_ref[3:4, spot] + product(wlat_ref[...], gpre_ref[:, spot])
+
+    edge_block(pl.ds(0, EDGES))
+
+    def lone(block, carry):
+        edge_block(pl.ds(pl.multiple_of(EDGES + block * LONE, LONE), LONE))
+        return carry
+
+    lax.fori_loop(0, blocks, lone, 0)
+
+
 def second_kernel(
-    count_ref, odd_ref, one_ref, two_ref, one_in_ref, two_in_ref, lat_ref, geo_ref, wlat_t_ref, wlat_ref, wten_t_ref, wten_ref, wout_ref,
-    xc_ref, oy_ref, glat_ref, rows_ref, table_ref,
+    count_ref, odd_ref, one_ref, two_ref, one_in_ref, two_in_ref, early_ref, first_read_ref, geo_ref, wten_t_ref, wten_ref, wout_ref,
+    xc_ref, oy_ref, gpre_ref, rows_ref, table_ref,
 ):
     own = fill_tables(odd_ref, one_ref, two_ref, one_in_ref, two_in_ref, table_ref)
     blocks = (count_ref[0] + (LONE - 1)) // LONE
@@ -255,14 +311,12 @@
     def edge_block(spot, geo, env_c, env_n):
         unit = unit_rows(geo)
         envelope = geo[3:4]
-        latent = lat_ref[:, spot]
         both = jnp.concatenate([project(env_c, unit, 1.0), project(env_n, unit, -1.0)], axis=0)
-        pre = product(wlat_t_ref[...], latent) + product(wten_t_ref[...], both)
+        pre = early_ref[:, spot] + product(wten_t_ref[...], both)
         hidden, slope = sigmoid_parts(pre)
-        read = jnp.sum(wout * (latent + hidden), axis=0, keepdims=True)
-        direct = wout * envelope
-        grad_pre = direct * slope
-        glat_ref[:, spot] = direct + product(wlat_ref[...], grad_pre)
+        read = first_read_ref[0:1, spot] + jnp.sum(wout * hidden, axis=0, keepdims=True)
+        grad_pre = (wout * envelope) * slope
+        gpre_ref[:, spot] = grad_pre
         grad_both = product(wten_ref[...], grad_pre)
         grad_c, grad_n = grad_both[0:TC], grad_both[TC : 2 * TC]
         found = [read, 0.5 * envelope * read]
@@ -274,19 +328,20 @@
         return four(grad_c, unit, 1.0), four(grad_n, unit, -1.0)
 
     def main(block, carry):
-        spot = pl.ds(pl.multiple_of(block * WIDE, WIDE), WIDE)
+        spot = pl.ds(block * WIDE, WIDE)
         geo = geo_ref[:, spot]
         hot = one_hot(geo[7:8].astype(jnp.int32), 512)
         env_n = fetch(table_ref, slice(0, 512), hot)
-        centre, other = edge_block(spot, geo, jnp.concatenate([own, own], axis=1), env_n)
+        centre, other = edge_block(spot, geo, jnp.concatenate([own] * (WIDE // ATOMS), axis=1), env_n)
         sums = scatter(other, hot)
-        oy_ref[0:128] += sums[:, 0:128] + (centre[:, 0:128] + centre[:, 128:256])
+        oy_ref[0:128] += sums[:, 0:128] + fold(centre)
         xc_ref[0:128] += sums[:, 128:256]
         oy_ref[128:256] += sums[:, 256:384]
         xc_ref[128:256] += sums[:, 384:512]
         return carry
 
-    lax.fori_loop(0, EDGES // WIDE, main, 0)
+    for block in range(EDGES // WIDE):
+        main(block, 0)
 
     def lone(block, carry):
         spot = pl.ds(pl.multiple_of(EDGES + block * LONE, LONE), LONE)
@@ -340,19 +395,20 @@
         return packed, jnp.where(line == 3, packed, -packed)
 
     def main(block, carry):
-        spot = pl.ds(pl.multiple_of(block * WIDE, WIDE), WIDE)
+        spot = pl.ds(block * WIDE, WIDE)
         geo = geo_ref[:, spot]
         hot = one_hot(geo[7:8].astype(jnp.int32), 512)
         grad_n = fetch(table_ref, slice(0, 512), hot)
-        other, centre = edge_block(spot, geo, jnp.concatenate([own, own], axis=1), grad_n)
+        other, centre = edge_block(spot, geo, jnp.concatenate([own] * (WIDE // ATOMS), axis=1), grad_n)
         sums = scatter(other, hot)
-        ox_ref[0:8] += sums[:, 0:128] + (centre[:, 0:128] + centre[:, 128:256])
+        ox_ref[0:8] += sums[:, 0:128] + fold(centre)
         ox_ref[8:16] += sums[:, 128:256]
         yc_ref[0:8] += sums[:, 256:384]
         yc_ref[8:16] += sums[:, 384:512]
         return carry
 
-    lax.fori_loop(0, EDGES // WIDE, main, 0)
+    for block in range(EDGES // WIDE):
+        main(block, 0)
 
     def lone(block, carry):
         spot = pl.ds(pl.multiple_of(EDGES + block * LONE, LONE), LONE)
@@ -369,14 +425,14 @@
     lax.fori_loop(0, blocks, lone, 0)
 
 
-def call(kernel, out_shape, in_specs, out_specs, scratch, cost):
+def call(kernel, out_shape, in_specs, out_specs, scratch, cost, limit=VMEM_LIMIT):
     return pl.pallas_call(
         kernel,
         out_shape=out_shape,
         in_specs=in_specs,
         out_specs=out_specs,
         scratch_shapes=scratch,
-        compiler_params=pltpu.CompilerParams(vmem_limit_bytes=VMEM_LIMIT),
+        compiler_params=pltpu.CompilerParams(vmem_limit_bytes=limit),
         cost_estimate=pl.CostEstimate(flops=cost, bytes_accessed=1 << 20, transcendentals=1 << 18),
     )
 
@@ -433,8 +489,8 @@
 def butterfly(xc, oy, odd_p, odd_q):
     far = jnp.where(odd_p, xc, oy)
     near = jnp.where(odd_p, oy, xc)
+    near_in = trade(near, 0, 0)
     far_in = trade(far, 0, 1)
-    near_in = trade(near, 0, 0)
     far, near = far + far_in, near + near_in
     here = jnp.where(odd_p, near, far)
     beside = jnp.where(odd_p, far, near)
@@ -448,20 +504,33 @@
 def local(
     positions, species, neighbours, counts, image_z, send_lists, w_basis, w_center, w_neigh, w_env, w_latent, w_tensor, w_out
 ):
-    base = jnp.concatenate(
+    base, own = call(
+        pack_kernel,
+        (shape(8, ATOMS), shape(24, ATOMS)),
+        [pl.BlockSpec(memory_space=pl.ANY)] * 6,
+        (IN_VMEM,) * 2,
         [
-            positions[0, 0],
-            species[0].astype(F32),
-            send_lists[0, 0].reshape(2, ATOMS).astype(F32),
-            counts[0].astype(F32),
-            jnp.zeros((1, ATOMS), F32),
+            pltpu.VMEM((3, 1, ATOMS), F32),
+            pltpu.VMEM((1, 1, ATOMS), jnp.int32),
+            pltpu.VMEM((1, 1, ATOMS), jnp.int32),
+            pltpu.VMEM((1, 1, 2 * ATOMS), jnp.int32),
+            pltpu.VMEM((SLOTS, ATOMS), jnp.int32),
+            pltpu.VMEM((SLOTS, ATOMS), jnp.int32),
+            pltpu.SemaphoreType.DMA((6,)),
         ],
-        axis=0,
+        1000,
+        60 * 1024 * 1024,
+    )(
+        positions.transpose(0, 2, 1, 3).reshape(3, 1, ATOMS),
+        species,
+        counts,
+        send_lists,
+        neighbours.transpose(0, 1, 3, 2).reshape(SLOTS, ATOMS),
+        image_z.transpose(0, 1, 3, 2).reshape(SLOTS, ATOMS),
     )
     odd_p, odd_q = odd_box()
     odd = odd_q.astype(jnp.int32).reshape(1)
     in_x = move(base, at_home, at_work, (1, 0))
-    own = jnp.concatenate([base, neighbours[0, 0].T.astype(F32), image_z[0, 0].T.astype(F32)], axis=0)
     own = move(own, at_home, at_work, (0, 0))
     in_yc = move(jnp.concatenate([own, in_x], axis=0), at_work, at_work, (0, 1))
 
@@ -480,14 +549,31 @@
     )(own, in_x, in_yc, wfeat, w_env.T)
     one, two, one_in, two_in = butterfly(xc, oy, odd_p, odd_q)
     wten = w_tensor.reshape(2 * TC, 128)
-    xc, oy, glat, rows = call(
+    wout = w_out[:, None]
+    early, first_read = call(
+        early_kernel,
+        (shape(128, 2 * EDGES), shape(8, 2 * EDGES)),
+        [IN_SMEM] + [IN_VMEM] * 3,
+        (IN_VMEM,) * 2,
+        [],
+        200_000_000,
+    )(count, lat, w_latent.T, wout)
+    xc, oy, gpre, rows = call(
         second_kernel,
         (shape(256, 128), shape(256, 128), shape(128, 2 * EDGES), shape(8, 2 * EDGES)),
-        [IN_SMEM] * 2 + [IN_VMEM] * 11,
+        [IN_SMEM] * 2 + [IN_VMEM] * 10,
         (IN_VMEM,) * 4,
         [pltpu.VMEM((256, 512), BF16)],
         1_000_000_000,
-    )(count, odd, one, two, one_in, two_in, lat, geo, w_latent.T, w_latent, wten.T, wten, w_out[:, None])
+    )(count, odd, one, two, one_in, two_in, early, first_read, geo, wten.T, wten, wout)
+    glat = call(
+        late_kernel,
+        shape(128, 2 * EDGES),
+        [IN_SMEM] + [IN_VMEM] * 4,
+        IN_VMEM,
+        [],
+        200_000_000,
+    )(count, gpre, geo, w_latent, wout)
     one, two, one_in, two_in = butterfly(xc, oy, odd_p, odd_q)
     yc, ox = call(
         third_kernel,

time: 111 us -> 103 us (0.928)
  local copies, waits for them, and re-layouts: 6.28 us -> 3 us
  waiting for transfers between devices: 38.4 us -> 36.8 us
  other arithmetic: 1.54 us -> 0.19 us
  Pallas kernels: 14.6 us -> 13.4 us
    pallas_call x0 -> x3, Pallas kernels: none -> 3.82 us  [the longest x1 1.42 us: local(): call(pack_kernel, (shape(8, ATOMS), shape(24, ATOMS)), [pl.BlockSpec(memo...]
    unnamed x28 -> x17, local copies, waits for them, and re-layouts: 5.33 us -> 2.11 us
    pallas_call x1, Pallas kernels: 5.5 us -> 3.47 us  [local(): call(second_kernel, (shape(256, 128), shape(256, 128), shape(128, 2 * EDG...]
    pallas_call x1, Pallas kernels: 4.9 us -> 3.01 us  [local(): call(third_kernel, (shape(16, 128), shape(16, 128)), [IN_SMEM] * 2 + [IN_...]
    ppermute x8, waiting for transfers between devices: 16.2 us -> 14.5 us  [trade(): return lax.ppermute(block, ('gx', 'gy'), pairs)]
    convert_element_type x3 -> x0, other arithmetic: 1.35 us -> none  [the longest x1 0.69 us: local(): image_z[0, 0].T.astype(F32)]
    pallas_call x1, Pallas kernels: 4.24 us -> 3.06 us  [local(): call(first_kernel, (shape(256, 128), shape(256, 128), shape(128, 2 * EDGE...]
  transfers between devices with their start and end apart: 14 -> 14, of which waited for: 10 -> 10; matrix products, arithmetic and copies ran while one was open for 0% -> 1% of each run, Pallas kernels for 0% -> 2%
where the time goes in v3:
time: 103 us
  starting transfers between devices  48.1 us (47%)
  waiting for transfers between devices  36.8 us (36%)
  Pallas kernels  13.4 us (13%)
  local copies, waits for them, and re-layouts  3 us (3%)
  between operations  1.06 us (1%)
    ppermute x6, starting transfers between devices, move(): return lax.ppermute(block, ('gx', 'gy'), pairs)  24.9 us
    ppermute x8, starting transfers between devices, trade(): return lax.ppermute(block, ('gx', 'gy'), pairs)  23.2 us
    ppermute x6, waiting for transfers between devices, move(): return lax.ppermute(block, ('gx', 'gy'), pairs)  22.3 us
    ppermute x8, waiting for transfers between devices, trade(): return lax.ppermute(block, ('gx', 'gy'), pairs)  14.5 us
    pallas_call x1, Pallas kernels, local(): call(second_kernel, (shape(256, 128), shape(256, 128), shape(128, 2 * EDG...  3.47 us
    pallas_call x1, Pallas kernels, local(): call(first_kernel, (shape(256, 128), shape(256, 128), shape(128, 2 * EDGE...  3.06 us
    pallas_call x1, Pallas kernels, local(): call(third_kernel, (shape(16, 128), shape(16, 128)), [IN_SMEM] * 2 + [IN_...  3.01 us
    unnamed x17, local copies, waits for them, and re-layouts  2.11 us
  transfers between devices with their start and end apart: 14, of which 10 were waited for; matrix products, arithmetic and copies ran while one was open for 1% of the time, Pallas kernels for 2%

profile of v3, /device:TPU:96, one launch (start us, length us, event | category | flops | bytes accessed | tf_op | source)
XLA Modules:
  0.0 102.5 jit_solution(5075396159129941609)
XLA Ops:
  0.6 1.4 %shard_map.140 = (f32[8,128]{1,0:T(8,128)}, f32[24,128]{1,0:T(8,128)}) custom-call(f32[3,1,128]{2,1,0:T(1,128)} %bitcast.27, s32[1,1,128]{2,1,0:T(1,128)} %refs_1_.1, s32[1,1,128]{2,1,0:T(1,128)} %refs_2_.1, s32[1,1,256]{2,1,0:T(1,128)} %refs_3_.1, s32[8,128]{1,0:T(8,128)} %bitcast.25, s32[8,128]{1,0:T(8,128)} %bitcast.26), custom_call_target="tpu_custom_call" | custom-call | flops 1000 | bytes 1048576 | tf_op jit(solution)/shard_map/pallas_call | solution.py:507
  2.1 12.0 %collective-permute-start = (f32[24,128]{1,0:T(8,128)}, f32[24,128]{1,0:T(8,128)S(1)}, u32[]{:S(2)}, u32[]{:S(2)}) collective-permute-start(f32[24,128]{1,0:T(8,128)} %get-tuple-element.19), channel_id=1, source_target_pairs={{0,8},{1,9},{2,13},{3,12},{4,256},{5,257},{6,261},{7,260},{8,264},... | collective-permute-start | bytes 36872 | tf_op jit(solution)/shard_map/ppermute | solution.py:477
  14.1 0.0 copy-start.4
  14.1 0.0 copy-start.5
  14.1 4.2 %collective-permute-start.1 = (f32[8,128]{1,0:T(8,128)}, f32[8,128]{1,0:T(8,128)S(1)}, u32[]{:S(2)}, u32[]{:S(2)}) collective-permute-start(f32[8,128]{1,0:T(8,128)} %get-tuple-element.20), channel_id=1, source_target_pairs={{16,8},{17,9},{18,13},{19,12},{20,256},{21,257},{22,261},{23,260},... | collective-permute-start | bytes 12296 | tf_op jit(solution)/shard_map/ppermute | solution.py:477
  18.3 3.9 %collective-permute-done.1.x_ref = f32[8,128]{1,0:T(8,128)S(1)} collective-permute-done((f32[8,128]{1,0:T(8,128)}, f32[8,128]{1,0:T(8,128)S(1)}, u32[]{:S(2)}, u32[]{:S(2)}) %collective-permute-start.1) | collective-permute-done | bytes 4128 | tf_op jit(solution)/shard_map/ppermute | solution.py:477
  22.2 0.0 collective-permute-done.own_ref
  22.2 1.9 %collective-permute-start.2 = (f32[32,128]{1,0:T(8,128)S(1)}, f32[32,128]{1,0:T(8,128)S(1)}, u32[]{:S(2)}, u32[]{:S(2)}) collective-permute-start(f32[32,128]{1,0:T(8,128)S(1)} %pad_maximum_fusion.4), channel_id=1, source_target_pairs={{9,8},{13,9},{12,13},{256,12},{257,256},{261,257},{260,261},{264,2... | collective-permute-start | bytes 49160 | tf_op jit(solution)/shard_map/ppermute | solution.py:477
  24.2 0.0 copy-start.2
  24.2 0.7 copy-done.2
  24.9 0.1 copy.29
  25.0 2.8 %collective-permute-done.2.yc_ref = f32[32,128]{1,0:T(8,128)S(1)} collective-permute-done((f32[32,128]{1,0:T(8,128)S(1)}, f32[32,128]{1,0:T(8,128)S(1)}, u32[]{:S(2)}, u32[]{:S(2)}) %collective-permute-start.2) | collective-permute-done | bytes 16416 | tf_op jit(solution)/shard_map/ppermute | solution.py:477
  27.9 3.1 %shard_map.141 = (f32[256,128]{1,0:T(8,128)S(1)}, f32[256,128]{1,0:T(8,128)S(1)}, f32[128,2048]{1,0:T(8,128)S(1)}, f32[128,2048]{1,0:T(8,128)S(1)}, f32[32,2048]...) custom-call(f32[24,128]{1,0:T(8,128)S(1)} %collective-permute-done.own_ref, ...), custom_call_target="tpu_custom_call" | custom-call | flops 500000000 | bytes 1048576 | tf_op jit(solution)/shard_map/pallas_call | solution.py:541
  31.0 1.9 %collective-permute-start.3 = (f32[256,128]{1,0:T(8,128)S(1)}, f32[256,128]{1,0:T(8,128)S(1)}, u32[]{:S(2)}, u32[]{:S(2)}) collective-permute-start(f32[256,128]{1,0:T(8,128)S(1)} %get-tuple-element.50), channel_id=1, source_target_pairs={{24,8},{25,9},{29,13},{28,12},{272,256},{273,257},{277,261},{276,2... | collective-permute-start | bytes 393224 | tf_op jit(solution)/shard_map/ppermute | solution.py:486
  32.9 2.6 %collective-permute-start.4 = (f32[256,128]{1,0:T(8,128)S(1)}, f32[256,128]{1,0:T(8,128)S(1)}, u32[]{:S(2)}, u32[]{:S(2)}) collective-permute-start(f32[256,128]{1,0:T(8,128)S(1)} %get-tuple-element.51), channel_id=1, source_target_pairs={{27,8},{26,9},{30,13},{31,12},{275,256},{274,257},{278,261},{279,2... | collective-permute-start | bytes 393224 | tf_op jit(solution)/shard_map/ppermute | solution.py:486
  35.6 0.0 collective-permute-done.3
  35.6 3.6 %collective-permute-done.4 = f32[256,128]{1,0:T(8,128)S(1)} collective-permute-done((f32[256,128]{1,0:T(8,128)S(1)}, f32[256,128]{1,0:T(8,128)S(1)}, u32[]{:S(2)}, u32[]{:S(2)}) %collective-permute-start.4) | collective-permute-done | bytes 131104 | tf_op jit(solution)/shard_map/ppermute | solution.py:486
  39.2 0.0 copy-start.6
  39.3 0.0 copy-start
  39.3 3.3 %collective-permute-start.5 = (f32[256,128]{1,0:T(8,128)S(1)}, f32[256,128]{1,0:T(8,128)S(1)}, u32[]{:S(2)}, u32[]{:S(2)}) collective-permute-start(f32[256,128]{1,0:T(8,128)S(1)} %get-tuple-element.49.one_ref), channel_id=1, source_target_pairs={{4,8},{13,9},{9,13},{256,12},{12,256},{261,257},{257,261},{264,260... | collective-permute-start | bytes 393224 | tf_op jit(solution)/shard_map/ppermute | solution.py:486
  42.6 5.4 %collective-permute-start.6 = (f32[256,128]{1,0:T(8,128)S(1)}, f32[256,128]{1,0:T(8,128)S(1)}, u32[]{:S(2)}, u32[]{:S(2)}) collective-permute-start(f32[256,128]{1,0:T(8,128)S(1)} %get-tuple-element.48.two_ref), channel_id=1, source_target_pairs={{9,8},{8,9},{12,13},{13,12},{257,256},{256,257},{260,261},{261,260... | collective-permute-start | bytes 393224 | tf_op jit(solution)/shard_map/ppermute | solution.py:486
  48.0 0.1 copy.31.wout_ref
  48.1 0.0 copy-start.1
  48.1 0.1 copy.30
  48.2 0.7 copy-done.1
  48.9 0.1 copy.32.wten_t_ref
  49.0 1.2 %shard_map.142 = (f32[128,2048]{1,0:T(8,128)S(1)}, f32[8,2048]{1,0:T(8,128)S(1)}) custom-call(s32[1]{0:T(128)} %get-tuple-element.21.count_ref, f32[128,2048]{1,0:T(8,128)S(1)} %get-tuple-element.24.lat_ref, f32[128,128]{1,0:T(8,128)S(1)} %bitcast.19, f32[128,1]{1,0:T(8,128)S(1)} %copy.31.wout_ref), custom_call_target="tpu_custom_call" | custom-call | flops 200000000 | bytes 1048576 | tf_op jit(solution)/shard_map/pallas_call | solution.py:553
  50.2 0.0 collective-permute-done.5.one_in_ref
  50.2 1.7 %collective-permute-done.6.two_in_ref = f32[256,128]{1,0:T(8,128)S(1)} collective-permute-done((f32[256,128]{1,0:T(8,128)S(1)}, f32[256,128]{1,0:T(8,128)S(1)}, u32[]{:S(2)}, u32[]{:S(2)}) %collective-permute-start.6) | collective-permute-done | bytes 131104 | tf_op jit(solution)/shard_map/ppermute | solution.py:486
  51.8 3.5 %shard_map.143 = (f32[256,128]{1,0:T(8,128)S(1)}, f32[256,128]{1,0:T(8,128)S(1)}, f32[128,2048]{1,0:T(8,128)S(1)}, f32[8,2048]{1,0:T(8,128)S(1)}) custom-call(s32[1]{0:T(128)} %get-tuple-element.21.count_ref, s32[1]{0:T(128)} %bitcast.7.odd_ref, f32[256,128]{1,0:T(8,128)S(1)} %get-tuple-element.49.one_ref, f32[256,128]{1,0:T(8,128)S(1)} %get-tuple-element.48.two_ref, ...), custom_call_target="tpu_custom_call" | custom-call | flops 1000000000 | bytes 1048576 | tf_op jit(solution)/shard_map/pallas_call | solution.py:561
  55.3 1.9 %collective-permute-start.7 = (f32[256,128]{1,0:T(8,128)S(1)}, f32[256,128]{1,0:T(8,128)S(1)}, u32[]{:S(2)}, u32[]{:S(2)}) collective-permute-start(f32[256,128]{1,0:T(8,128)S(1)} %get-tuple-element.46), channel_id=1, source_target_pairs={{24,8},{25,9},{29,13},{28,12},{272,256},{273,257},{277,261},{276,2... | collective-permute-start | bytes 393224 | tf_op jit(solution)/shard_map/ppermute | solution.py:486
  57.3 2.6 %collective-permute-start.8 = (f32[256,128]{1,0:T(8,128)S(1)}, f32[256,128]{1,0:T(8,128)S(1)}, u32[]{:S(2)}, u32[]{:S(2)}) collective-permute-start(f32[256,128]{1,0:T(8,128)S(1)} %get-tuple-element.47), channel_id=1, source_target_pairs={{27,8},{26,9},{30,13},{31,12},{275,256},{274,257},{278,261},{279,2... | collective-permute-start | bytes 393224 | tf_op jit(solution)/shard_map/ppermute | solution.py:486
  59.9 3.7 %collective-permute-done.8 = f32[256,128]{1,0:T(8,128)S(1)} collective-permute-done((f32[256,128]{1,0:T(8,128)S(1)}, f32[256,128]{1,0:T(8,128)S(1)}, u32[]{:S(2)}, u32[]{:S(2)}) %collective-permute-start.8) | collective-permute-done | bytes 131104 | tf_op jit(solution)/shard_map/ppermute | solution.py:486
  63.7 3.6 %collective-permute-start.10 = (f32[256,128]{1,0:T(8,128)S(1)}, f32[256,128]{1,0:T(8,128)S(1)}, u32[]{:S(2)}, u32[]{:S(2)}) collective-permute-start(f32[256,128]{1,0:T(8,128)S(1)} %get-tuple-element.44.two_ref), channel_id=1, source_target_pairs={{9,8},{8,9},{12,13},{13,12},{257,256},{256,257},{260,261},{261,260... | collective-permute-start | bytes 393224 | tf_op jit(solution)/shard_map/ppermute | solution.py:486
  67.3 1.9 %collective-permute-start.9 = (f32[256,128]{1,0:T(8,128)S(1)}, f32[256,128]{1,0:T(8,128)S(1)}, u32[]{:S(2)}, u32[]{:S(2)}) collective-permute-start(f32[256,128]{1,0:T(8,128)S(1)} %get-tuple-element.45.one_ref), channel_id=1, source_target_pairs={{4,8},{13,9},{9,13},{256,12},{12,256},{261,257},{257,261},{264,260... | collective-permute-start | bytes 393224 | tf_op jit(solution)/shard_map/ppermute | solution.py:486
  69.3 0.1 copy.35.wenv_ref
  69.4 1.2 %shard_map.144.glat_ref = f32[128,2048]{1,0:T(8,128)S(1)} custom-call(s32[1]{0:T(128)} %get-tuple-element.21.count_ref, f32[128,2048]{1,0:T(8,128)S(1)} %get-tuple-element.32.gpre_ref, f32[16,2048]{1,0:T(8,128)S(1)} %get-tuple-element.27.geo_ref, f32[128,128]{1,0:T(8,128)S(1)} %copy-done, f32[128,1]{1,0:T(8,128)S(1)} %copy.31.wout_ref), custom_call_target="tpu_custom_call" | custom-call | flops 200000000 | bytes 1048576 | tf_op jit(solution)/shard_map/pallas_call | solution.py:569
  70.6 0.9 collective-permute-done.10.two_in_ref
  71.5 4.6 %collective-permute-done.9.one_in_ref = f32[256,128]{1,0:T(8,128)S(1)} collective-permute-done((f32[256,128]{1,0:T(8,128)S(1)}, f32[256,128]{1,0:T(8,128)S(1)}, u32[]{:S(2)}, u32[]{:S(2)}) %collective-permute-start.9) | collective-permute-done | bytes 131104 | tf_op jit(solution)/shard_map/ppermute | solution.py:486
  76.1 3.0 %shard_map.145 = (f32[16,128]{1,0:T(8,128)S(1)}, f32[16,128]{1,0:T(8,128)S(1)}) custom-call(s32[1]{0:T(128)} %get-tuple-element.21.count_ref, s32[1]{0:T(128)} %bitcast.7.odd_ref, f32[256,128]{1,0:T(8,128)S(1)} %get-tuple-element.45.one_ref, f32[256,128]{1,0:T(8,128)S(1)} %get-tuple-element.44.two_ref, f32[256,128]{1,0:T(8,128)S(1)} %collective-permute-done.9.one_in_ref, ...), custom_call_target="tpu_custom_call" | custom-call | flops 500000000 | bytes 1048576 | tf_op jit(solution)/shard_map/pallas_call | solution.py:578
  79.1 2.0 %collective-permute-start.11 = (f32[16,128]{1,0:T(8,128)S(1)}, f32[16,128]{1,0:T(8,128)S(1)}, u32[]{:S(2)}, u32[]{:S(2)}) collective-permute-start(f32[16,128]{1,0:T(8,128)S(1)} %get-tuple-element.35), channel_id=1, source_target_pairs={{4,8},{8,9},{9,13},{13,12},{12,256},{256,257},{257,261},{261,260},... | collective-permute-start | bytes 24584 | tf_op jit(solution)/shard_map/ppermute | solution.py:477
  81.0 4.8 %collective-permute-done.11 = f32[16,128]{1,0:T(8,128)S(1)} collective-permute-done((f32[16,128]{1,0:T(8,128)S(1)}, f32[16,128]{1,0:T(8,128)S(1)}, u32[]{:S(2)}, u32[]{:S(2)}) %collective-permute-start.11) | collective-permute-done | bytes 8224 | tf_op jit(solution)/shard_map/ppermute | solution.py:477
  85.9 1.9 %collective-permute-start.12 = (f32[8,128]{1,0:T(8,128)S(1)}, f32[8,128]{1,0:T(8,128)S(1)}, u32[]{:S(2)}, u32[]{:S(2)}) collective-permute-start(f32[8,128]{1,0:T(8,128)S(1)} %get-tuple-element.61), channel_id=1, source_target_pairs={{27,0},{26,1},{30,2},{31,3},{275,4},{274,5},{278,6},{279,7},{283,8... | collective-permute-start | bytes 12296 | tf_op jit(solution)/shard_map/ppermute | solution.py:477
  87.8 2.8 %collective-permute-start.13 = (f32[8,128]{1,0:T(8,128)S(1)}, f32[8,128]{1,0:T(8,128)S(1)}, u32[]{:S(2)}, u32[]{:S(2)}) collective-permute-start(f32[8,128]{1,0:T(8,128)S(1)} %get-tuple-element.60), channel_id=1, source_target_pairs={{8,0},{9,1},{13,2},{12,3},{256,4},{257,5},{261,6},{260,7},{264,8},... | collective-permute-start | bytes 12296 | tf_op jit(solution)/shard_map/ppermute | solution.py:477
  90.6 7.4 %collective-permute-done.12 = f32[8,128]{1,0:T(8,128)S(1)} collective-permute-done((f32[8,128]{1,0:T(8,128)S(1)}, f32[8,128]{1,0:T(8,128)S(1)}, u32[]{:S(2)}, u32[]{:S(2)}) %collective-permute-start.12) | collective-permute-done | bytes 4128 | tf_op jit(solution)/shard_map/ppermute | solution.py:477
  98.0 3.4 %collective-permute-done.13 = f32[8,128]{1,0:T(8,128)S(1)} collective-permute-done((f32[8,128]{1,0:T(8,128)S(1)}, f32[8,128]{1,0:T(8,128)S(1)}, u32[]{:S(2)}, u32[]{:S(2)}) %collective-permute-start.13) | collective-permute-done | bytes 4128 | tf_op jit(solution)/shard_map/ppermute | solution.py:477
  101.4 0.5 slice_bitcast_fusion.1
  101.9 0.6 copy.36
  (24 shorter events, 0.3 us)
Async XLA Ops:
  2.1 20.2 %collective-permute-start = (f32[24,128]{1,0:T(8,128)}, f32[24,128]{1,0:T(8,128)S(1)}, u32[]{:S(2)}, u32[]{:S(2)}) collective-permute-start(f32[24,128]{1,0:T(8,128)} %get-tuple-element.19), channel_id=1, source_target_pairs={{0,8},{1,9},{2,13},{3,12},{4,256},{5,257},{6,261},{7,260},{8,264},... | collective-permute-start | bytes 36872 | tf_op jit(solution)/shard_map/ppermute | solution.py:477
  14.1 10.1 %copy-start.4 = (f32[2,128]{1,0:T(2,128)S(1)}, f32[2,128]{1,0:T(2,128)}, u32[]{:S(2)}) copy-start(f32[2,128]{1,0:T(2,128)} %param.21) | copy-start | bytes 3076
  14.1 10.1 %copy-start.5 = (f32[2,128]{1,0:T(2,128)S(1)}, f32[2,128]{1,0:T(2,128)}, u32[]{:S(2)}) copy-start(f32[2,128]{1,0:T(2,128)} %param.20) | copy-start | bytes 3076
  14.1 8.1 %collective-permute-start.1 = (f32[8,128]{1,0:T(8,128)}, f32[8,128]{1,0:T(8,128)S(1)}, u32[]{:S(2)}, u32[]{:S(2)}) collective-permute-start(f32[8,128]{1,0:T(8,128)} %get-tuple-element.20), channel_id=1, source_target_pairs={{16,8},{17,9},{18,13},{19,12},{20,256},{21,257},{22,261},{23,260},... | collective-permute-start | bytes 12296 | tf_op jit(solution)/shard_map/ppermute | solution.py:477
  22.2 5.6 %collective-permute-start.2 = (f32[32,128]{1,0:T(8,128)S(1)}, f32[32,128]{1,0:T(8,128)S(1)}, u32[]{:S(2)}, u32[]{:S(2)}) collective-permute-start(f32[32,128]{1,0:T(8,128)S(1)} %pad_maximum_fusion.4), channel_id=1, source_target_pairs={{9,8},{13,9},{12,13},{256,12},{257,256},{261,257},{260,261},{264,2... | collective-permute-start | bytes 49160 | tf_op jit(solution)/shard_map/ppermute | solution.py:477
  24.2 0.7 copy-start.2
  24.9 2.9 %copy-start.3 = (f32[128,32]{0,1:T(8,128)S(1)}, f32[128,32]{0,1:T(8,128)}, u32[]{:S(2)}) copy-start(f32[128,32]{0,1:T(8,128)} %param.22) | copy-start | bytes 49156
  31.0 4.6 %collective-permute-start.3 = (f32[256,128]{1,0:T(8,128)S(1)}, f32[256,128]{1,0:T(8,128)S(1)}, u32[]{:S(2)}, u32[]{:S(2)}) collective-permute-start(f32[256,128]{1,0:T(8,128)S(1)} %get-tuple-element.50), channel_id=1, source_target_pairs={{24,8},{25,9},{29,13},{28,12},{272,256},{273,257},{277,261},{276,2... | collective-permute-start | bytes 393224 | tf_op jit(solution)/shard_map/ppermute | solution.py:486
  32.9 6.3 %collective-permute-start.4 = (f32[256,128]{1,0:T(8,128)S(1)}, f32[256,128]{1,0:T(8,128)S(1)}, u32[]{:S(2)}, u32[]{:S(2)}) collective-permute-start(f32[256,128]{1,0:T(8,128)S(1)} %get-tuple-element.51), channel_id=1, source_target_pairs={{27,8},{26,9},{30,13},{31,12},{275,256},{274,257},{278,261},{279,2... | collective-permute-start | bytes 393224 | tf_op jit(solution)/shard_map/ppermute | solution.py:486
  39.2 8.7 %copy-start.6 = (f32[128]{0:T(128)S(1)}, f32[128]{0:T(128)}, u32[]{:S(2)}) copy-start(f32[128]{0:T(128)} %param.25) | copy-start | bytes 1540
  39.3 8.8 %copy-start = (f32[128,128]{1,0:T(8,128)S(1)}, f32[128,128]{1,0:T(8,128)}, u32[]{:S(2)}) copy-start(f32[128,128]{1,0:T(8,128)} %wlat_ref.1) | copy-start | bytes 196612
  39.3 10.9 %collective-permute-start.5 = (f32[256,128]{1,0:T(8,128)S(1)}, f32[256,128]{1,0:T(8,128)S(1)}, u32[]{:S(2)}, u32[]{:S(2)}) collective-permute-start(f32[256,128]{1,0:T(8,128)S(1)} %get-tuple-element.49.one_ref), channel_id=1, source_target_pairs={{4,8},{13,9},{9,13},{256,12},{12,256},{261,257},{257,261},{264,260... | collective-permute-start | bytes 393224 | tf_op jit(solution)/shard_map/ppermute | solution.py:486
  42.6 9.3 %collective-permute-start.6 = (f32[256,128]{1,0:T(8,128)S(1)}, f32[256,128]{1,0:T(8,128)S(1)}, u32[]{:S(2)}, u32[]{:S(2)}) collective-permute-start(f32[256,128]{1,0:T(8,128)S(1)} %get-tuple-element.48.two_ref), channel_id=1, source_target_pairs={{9,8},{8,9},{12,13},{13,12},{257,256},{256,257},{260,261},{261,260... | collective-permute-start | bytes 393224 | tf_op jit(solution)/shard_map/ppermute | solution.py:486
  48.1 0.8 copy-start.1
  55.3 4.5 %collective-permute-start.7 = (f32[256,128]{1,0:T(8,128)S(1)}, f32[256,128]{1,0:T(8,128)S(1)}, u32[]{:S(2)}, u32[]{:S(2)}) collective-permute-start(f32[256,128]{1,0:T(8,128)S(1)} %get-tuple-element.46), channel_id=1, source_target_pairs={{24,8},{25,9},{29,13},{28,12},{272,256},{273,257},{277,261},{276,2... | collective-permute-start | bytes 393224 | tf_op jit(solution)/shard_map/ppermute | solution.py:486
  57.3 6.3 %collective-permute-start.8 = (f32[256,128]{1,0:T(8,128)S(1)}, f32[256,128]{1,0:T(8,128)S(1)}, u32[]{:S(2)}, u32[]{:S(2)}) collective-permute-start(f32[256,128]{1,0:T(8,128)S(1)} %get-tuple-element.47), channel_id=1, source_target_pairs={{27,8},{26,9},{30,13},{31,12},{275,256},{274,257},{278,261},{279,2... | collective-permute-start | bytes 393224 | tf_op jit(solution)/shard_map/ppermute | solution.py:486
  63.7 7.8 %collective-permute-start.10 = (f32[256,128]{1,0:T(8,128)S(1)}, f32[256,128]{1,0:T(8,128)S(1)}, u32[]{:S(2)}, u32[]{:S(2)}) collective-permute-start(f32[256,128]{1,0:T(8,128)S(1)} %get-tuple-element.44.two_ref), channel_id=1, source_target_pairs={{9,8},{8,9},{12,13},{13,12},{257,256},{256,257},{260,261},{261,260... | collective-permute-start | bytes 393224 | tf_op jit(solution)/shard_map/ppermute | solution.py:486
  67.3 8.7 %collective-permute-start.9 = (f32[256,128]{1,0:T(8,128)S(1)}, f32[256,128]{1,0:T(8,128)S(1)}, u32[]{:S(2)}, u32[]{:S(2)}) collective-permute-start(f32[256,128]{1,0:T(8,128)S(1)} %get-tuple-element.45.one_ref), channel_id=1, source_target_pairs={{4,8},{13,9},{9,13},{256,12},{12,256},{261,257},{257,261},{264,260... | collective-permute-start | bytes 393224 | tf_op jit(solution)/shard_map/ppermute | solution.py:486
  79.1 6.8 %collective-permute-start.11 = (f32[16,128]{1,0:T(8,128)S(1)}, f32[16,128]{1,0:T(8,128)S(1)}, u32[]{:S(2)}, u32[]{:S(2)}) collective-permute-start(f32[16,128]{1,0:T(8,128)S(1)} %get-tuple-element.35), channel_id=1, source_target_pairs={{4,8},{8,9},{9,13},{13,12},{12,256},{256,257},{257,261},{261,260},... | collective-permute-start | bytes 24584 | tf_op jit(solution)/shard_map/ppermute | solution.py:477
  85.9 12.1 %collective-permute-start.12 = (f32[8,128]{1,0:T(8,128)S(1)}, f32[8,128]{1,0:T(8,128)S(1)}, u32[]{:S(2)}, u32[]{:S(2)}) collective-permute-start(f32[8,128]{1,0:T(8,128)S(1)} %get-tuple-element.61), channel_id=1, source_target_pairs={{27,0},{26,1},{30,2},{31,3},{275,4},{274,5},{278,6},{279,7},{283,8... | collective-permute-start | bytes 12296 | tf_op jit(solution)/shard_map/ppermute | solution.py:477
  87.8 13.6 %collective-permute-start.13 = (f32[8,128]{1,0:T(8,128)S(1)}, f32[8,128]{1,0:T(8,128)S(1)}, u32[]{:S(2)}, u32[]{:S(2)}) collective-permute-start(f32[8,128]{1,0:T(8,128)S(1)} %get-tuple-element.60), channel_id=1, source_target_pairs={{8,0},{9,1},{13,2},{12,3},{256,4},{257,5},{261,6},{260,7},{264,8},... | collective-permute-start | bytes 12296 | tf_op jit(solution)/shard_map/ppermute | solution.py:477

commit v4 on v3

--- a/solution.py
+++ b/solution.py
@@ -10,8 +10,8 @@
 ATOMS = 128
 SLOTS = 8
 EDGES = ATOMS * SLOTS
-WIDE = 1024
 LONE = 128
+WIDE = EDGES + LONE
 TC = 32
 VMEM_LIMIT = 24 * 1024 * 1024
 
@@ -32,7 +32,9 @@
 def product(left, right):
     a, b = halves(left)
     c, d = halves(right)
-    return dot_nn(a, c) + (dot_nn(a, d) + dot_nn(b, c))
+    rows = left.shape[0]
+    both = dot_nn(jnp.concatenate([a, b], axis=0), c)
+    return both[0:rows] + (both[rows:] + dot_nn(a, d))
 
 
 def one_hot(index_row, rows):
@@ -40,17 +42,14 @@
     return jnp.where(lines == index_row, 1.0, 0.0).astype(BF16)
 
 
-def gather(high, low, hot):
-    return dot_nn(high, hot) + dot_nn(low, hot)
-
-
 def scatter(values, hot):
-    high, low = halves(values)
-    return dot_nt(high, hot) + dot_nt(low, hot)
+    rows = values.shape[0]
+    both = dot_nt(jnp.concatenate(halves(values), axis=0), hot)
+    return both[0:rows] + both[rows:]
 
 
 def fold(values):
-    return sum(values[:, k * ATOMS : (k + 1) * ATOMS] for k in range(WIDE // ATOMS))
+    return sum(values[:, k * ATOMS : (k + 1) * ATOMS] for k in range(SLOTS))
 
 
 def lanes(table, index):
@@ -93,7 +92,7 @@
 
 
 def pack_kernel(*refs):
-    sources, (base_ref, own_ref), held, sems = refs[:6], refs[6:8], refs[8:14], refs[14]
+    sources, own_ref, held, sems = refs[:6], refs[6], refs[7:13], refs[13]
     copies = [pltpu.make_async_copy(source, place, sems.at[i]) for i, (source, place) in enumerate(zip(sources, held))]
     for copy in copies:
         copy.start()
@@ -104,7 +103,6 @@
     rows = [positions[0], positions[1], positions[2], species[0].astype(F32), lists[:, 0:ATOMS], lists[:, ATOMS:]]
     rows += [counts[0].astype(F32), jnp.zeros((1, ATOMS), F32)]
     for line, values in enumerate(rows):
-        base_ref[line : line + 1] = values
         own_ref[line : line + 1] = values
     own_ref[8:16] = neighbours[...].astype(F32)
     own_ref[16:24] = images[...].astype(F32)
@@ -149,7 +147,7 @@
     for line, values in enumerate(rows):
         for k in range(SLOTS):
             geo_ref[line : line + 1, k * ATOMS : (k + 1) * ATOMS] = values[k : k + 1]
-    geo_ref[8:16, 0:EDGES] = jnp.zeros((8, EDGES), F32)
+    geo_ref[8:16, 0:WIDE] = jnp.zeros((8, WIDE), F32)
 
     y_neigh = yc_ref[8:16].astype(jnp.int32)
     wanted = (sub < spread(yc_ref[6:7]).astype(jnp.int32)) & (y_neigh >= 352)
@@ -188,18 +186,17 @@
         ex = other[0:1] + 1.0 - centre[0:1]
         ey = other[1:2] - 1.0 - centre[1:2]
         ez = other[2:3] - centre[2:3] + packed[2:3]
-        found = list(geometry(ex, ey, ez, packed[3:4])) + [centre[3:4], other[3:4], packed[1:2], packed[0:1]]
+        found = list(geometry(ex, ey, ez, packed[3:4])) + [centre[3:4], other[3:4], packed[1:2] + 128.0, packed[0:1]]
         spot = pl.ds(pl.multiple_of(EDGES + block * LONE, LONE), LONE)
         for number, values in enumerate(found):
             geo_ref[number : number + 1, spot] = values
         return carry
 
-    lax.fori_loop(0, blocks, compact, 0)
+    compact(jnp.int32(0), 0)
+    lax.fori_loop(1, blocks, compact, 0)
 
     wfeat = wfeat_ref[...]
     wenv = wenv_ref[...]
-    xc_ref[...] = jnp.zeros_like(xc_ref)
-    oy_ref[...] = jnp.zeros_like(oy_ref)
 
     def edge_block(spot):
         geo = geo_ref[:, spot]
@@ -216,27 +213,22 @@
         unit = unit_rows(geo)
         return geo, four(weight, unit, 1.0), four(weight, unit, -1.0)
 
-    def main(block, carry):
-        spot = pl.ds(block * WIDE, WIDE)
-        geo, centre, other = edge_block(spot)
-        sums = scatter(other, one_hot(geo[7:8].astype(jnp.int32), 512))
-        oy_ref[0:128] += sums[:, 0:128] + fold(centre)
-        xc_ref[0:128] += sums[:, 128:256]
-        oy_ref[128:256] += sums[:, 256:384]
-        xc_ref[128:256] += sums[:, 384:512]
-        return carry
-
-    for block in range(EDGES // WIDE):
-        main(block, 0)
+    spot = pl.ds(0, WIDE)
+    geo, centre, other = edge_block(spot)
+    sums = scatter(other, one_hot(geo[7:8].astype(jnp.int32), 512))
+    oy_ref[0:128] = sums[:, 0:128] + fold(centre)
+    xc_ref[0:128] = sums[:, 128:256]
+    oy_ref[128:256] = sums[:, 256:384] + scatter(centre[:, EDGES:], one_hot(geo[8:9, EDGES:].astype(jnp.int32), 128))
+    xc_ref[128:256] = sums[:, 384:512]
 
     def lone(block, carry):
         spot = pl.ds(pl.multiple_of(EDGES + block * LONE, LONE), LONE)
         geo, centre, other = edge_block(spot)
-        xc_ref[0:128] += scatter(other, one_hot(geo[7:8].astype(jnp.int32), 128))
+        xc_ref[0:128] += scatter(other, one_hot(geo[7:8].astype(jnp.int32) - 128, 128))
         oy_ref[128:256] += scatter(centre, one_hot(geo[8:9].astype(jnp.int32), 128))
         return carry
 
-    lax.fori_loop(0, blocks, lone, 0)
+    lax.fori_loop(1, blocks, lone, 0)
 
 
 def fill_tables(odd_ref, one_ref, two_ref, one_in_ref, two_in_ref, table_ref):
@@ -274,13 +266,13 @@
         pre_ref[:, spot] = product(wlat_t_ref[...], latent)
         read_ref[0:1, spot] = jnp.sum(wout * latent, axis=0, keepdims=True)
 
-    edge_block(pl.ds(0, EDGES))
+    edge_block(pl.ds(0, WIDE))
 
     def lone(block, carry):
         edge_block(pl.ds(pl.multiple_of(EDGES + block * LONE, LONE), LONE))
         return carry
 
-    lax.fori_loop(0, blocks, lone, 0)
+    lax.fori_loop(1, blocks, lone, 0)
 
 
 def late_kernel(count_ref, gpre_ref, geo_ref, wlat_ref, wout_ref, glat_ref):
@@ -289,13 +281,13 @@
     def edge_block(spot):
         glat_ref[:, spot] = wout_ref[...] * geo_ref[3:4, spot] + product(wlat_ref[...], gpre_ref[:, spot])
 
-    edge_block(pl.ds(0, EDGES))
+    edge_block(pl.ds(0, WIDE))
 
     def lone(block, carry):
         edge_block(pl.ds(pl.multiple_of(EDGES + block * LONE, LONE), LONE))
         return carry
 
-    lax.fori_loop(0, blocks, lone, 0)
+    lax.fori_loop(1, blocks, lone, 0)
 
 
 def second_kernel(
@@ -305,8 +297,6 @@
     own = fill_tables(odd_ref, one_ref, two_ref, one_in_ref, two_in_ref, table_ref)
     blocks = (count_ref[0] + (LONE - 1)) // LONE
     wout = wout_ref[...]
-    xc_ref[...] = jnp.zeros_like(xc_ref)
-    oy_ref[...] = jnp.zeros_like(oy_ref)
 
     def edge_block(spot, geo, env_c, env_n):
         unit = unit_rows(geo)
@@ -327,26 +317,23 @@
             rows_ref[number : number + 1, spot] = values
         return four(grad_c, unit, 1.0), four(grad_n, unit, -1.0)
 
-    def main(block, carry):
-        spot = pl.ds(block * WIDE, WIDE)
-        geo = geo_ref[:, spot]
-        hot = one_hot(geo[7:8].astype(jnp.int32), 512)
-        env_n = fetch(table_ref, slice(0, 512), hot)
-        centre, other = edge_block(spot, geo, jnp.concatenate([own] * (WIDE // ATOMS), axis=1), env_n)
-        sums = scatter(other, hot)
-        oy_ref[0:128] += sums[:, 0:128] + fold(centre)
-        xc_ref[0:128] += sums[:, 128:256]
-        oy_ref[128:256] += sums[:, 256:384]
-        xc_ref[128:256] += sums[:, 384:512]
-        return carry
-
-    for block in range(EDGES // WIDE):
-        main(block, 0)
+    spot = pl.ds(0, WIDE)
+    geo = geo_ref[:, spot]
+    hot = one_hot(geo[7:8].astype(jnp.int32), 512)
+    hot_c = one_hot(geo[8:9, EDGES:].astype(jnp.int32), 128)
+    env_n = fetch(table_ref, slice(0, 512), hot)
+    env_c = jnp.concatenate([own] * SLOTS + [fetch(table_ref, slice(256, 384), hot_c)], axis=1)
+    centre, other = edge_block(spot, geo, env_c, env_n)
+    sums = scatter(other, hot)
+    oy_ref[0:128] = sums[:, 0:128] + fold(centre)
+    xc_ref[0:128] = sums[:, 128:256]
+    oy_ref[128:256] = sums[:, 256:384] + scatter(centre[:, EDGES:], hot_c)
+    xc_ref[128:256] = sums[:, 384:512]
 
     def lone(block, carry):
         spot = pl.ds(pl.multiple_of(EDGES + block * LONE, LONE), LONE)
         geo = geo_ref[:, spot]
-        hot_n = one_hot(geo[7:8].astype(jnp.int32), 128)
+        hot_n = one_hot(geo[7:8].astype(jnp.int32) - 128, 128)
         hot_c = one_hot(geo[8:9].astype(jnp.int32), 128)
         env_n = fetch(table_ref, slice(128, 256), hot_n)
         env_c = fetch(table_ref, slice(256, 384), hot_c)
@@ -355,7 +342,7 @@
         oy_ref[128:256] += scatter(centre, hot_c)
         return carry
 
-    lax.fori_loop(0, blocks, lone, 0)
+    lax.fori_loop(1, blocks, lone, 0)
 
 
 def third_kernel(
@@ -364,8 +351,6 @@
 ):
     own = fill_tables(odd_ref, one_ref, two_ref, one_in_ref, two_in_ref, table_ref)
     blocks = (count_ref[0] + (LONE - 1)) // LONE
-    yc_ref[...] = jnp.zeros_like(yc_ref)
-    ox_ref[...] = jnp.zeros_like(ox_ref)
 
     def edge_block(spot, geo, grad_c, grad_n):
         unit = unit_rows(geo)
@@ -394,26 +379,23 @@
             packed = jnp.where(line == comp, force[comp], packed)
         return packed, jnp.where(line == 3, packed, -packed)
 
-    def main(block, carry):
-        spot = pl.ds(block * WIDE, WIDE)
-        geo = geo_ref[:, spot]
-        hot = one_hot(geo[7:8].astype(jnp.int32), 512)
-        grad_n = fetch(table_ref, slice(0, 512), hot)
-        other, centre = edge_block(spot, geo, jnp.concatenate([own] * (WIDE // ATOMS), axis=1), grad_n)
-        sums = scatter(other, hot)
-        ox_ref[0:8] += sums[:, 0:128] + fold(centre)
-        ox_ref[8:16] += sums[:, 128:256]
-        yc_ref[0:8] += sums[:, 256:384]
-        yc_ref[8:16] += sums[:, 384:512]
-        return carry
-
-    for block in range(EDGES // WIDE):
-        main(block, 0)
+    spot = pl.ds(0, WIDE)
+    geo = geo_ref[:, spot]
+    hot = one_hot(geo[7:8].astype(jnp.int32), 512)
+    hot_c = one_hot(geo[8:9, EDGES:].astype(jnp.int32), 128)
+    grad_n = fetch(table_ref, slice(0, 512), hot)
+    grad_c = jnp.concatenate([own] * SLOTS + [fetch(table_ref, slice(256, 384), hot_c)], axis=1)
+    other, centre = edge_block(spot, geo, grad_c, grad_n)
+    sums = scatter(other, hot)
+    ox_ref[0:8] = sums[:, 0:128] + fold(centre)
+    ox_ref[8:16] = sums[:, 128:256]
+    yc_ref[0:8] = sums[:, 256:384] + scatter(centre[:, EDGES:], hot_c)
+    yc_ref[8:16] = sums[:, 384:512]
 
     def lone(block, carry):
         spot = pl.ds(pl.multiple_of(EDGES + block * LONE, LONE), LONE)
         geo = geo_ref[:, spot]
-        hot_n = one_hot(geo[7:8].astype(jnp.int32), 128)
+        hot_n = one_hot(geo[7:8].astype(jnp.int32) - 128, 128)
         hot_c = one_hot(geo[8:9].astype(jnp.int32), 128)
         grad_n = fetch(table_ref, slice(128, 256), hot_n)
         grad_c = fetch(table_ref, slice(256, 384), hot_c)
@@ -422,7 +404,7 @@
         yc_ref[0:8] += scatter(centre, hot_c)
         return carry
 
-    lax.fori_loop(0, blocks, lone, 0)
+    lax.fori_loop(1, blocks, lone, 0)
 
 
 def call(kernel, out_shape, in_specs, out_specs, scratch, cost, limit=VMEM_LIMIT):
@@ -492,8 +474,9 @@
     near_in = trade(near, 0, 0)
     far_in = trade(far, 0, 1)
     far, near = far + far_in, near + near_in
-    here = jnp.where(odd_p, near, far)
-    beside = jnp.where(odd_p, far, near)
+    even_p = jnp.logical_not(odd_p)
+    here = jnp.where(even_p, far, near)
+    beside = jnp.where(even_p, near, far)
     up = jnp.concatenate([here[128:256], beside[128:256]], axis=0)
     down = jnp.concatenate([here[0:128], beside[0:128]], axis=0)
     one = jnp.where(odd_q, up, down)
@@ -504,11 +487,11 @@
 def local(
     positions, species, neighbours, counts, image_z, send_lists, w_basis, w_center, w_neigh, w_env, w_latent, w_tensor, w_out
 ):
-    base, own = call(
+    own = call(
         pack_kernel,
-        (shape(8, ATOMS), shape(24, ATOMS)),
+        shape(24, ATOMS),
         [pl.BlockSpec(memory_space=pl.ANY)] * 6,
-        (IN_VMEM,) * 2,
+        IN_VMEM,
         [
             pltpu.VMEM((3, 1, ATOMS), F32),
             pltpu.VMEM((1, 1, ATOMS), jnp.int32),
@@ -530,8 +513,8 @@
     )
     odd_p, odd_q = odd_box()
     odd = odd_q.astype(jnp.int32).reshape(1)
-    in_x = move(base, at_home, at_work, (1, 0))
     own = move(own, at_home, at_work, (0, 0))
+    in_x = move(own[0:8], at_work, at_work, (1, 0))
     in_yc = move(jnp.concatenate([own, in_x], axis=0), at_work, at_work, (0, 1))
 
     wfeat = jnp.concatenate(

time: 103 us -> 97 us (0.942)
  the two profiles are of different devices: /device:TPU:96 before, /device:TPU:22 now
where the time goes in v4:
time: 97 us; the launch traced here: 96.2 us
  starting transfers between devices  48.8 us (50%)
  waiting for transfers between devices  32.7 us (34%)
  Pallas kernels  10.5 us (11%)
  local copies, waits for them, and re-layouts  3 us (3%)
  between operations  1.03 us (1%)
    ppermute x6, starting transfers between devices, move(): return lax.ppermute(block, ('gx', 'gy'), pairs)  26.8 us
    ppermute x6, waiting for transfers between devices, move(): return lax.ppermute(block, ('gx', 'gy'), pairs)  24.2 us
    ppermute x8, starting transfers between devices, trade(): return lax.ppermute(block, ('gx', 'gy'), pairs)  22 us
    ppermute x8, waiting for transfers between devices, trade(): return lax.ppermute(block, ('gx', 'gy'), pairs)  8.55 us
    pallas_call x1, Pallas kernels, local(): call(second_kernel, (shape(256, 128), shape(256, 128), shape(128, 2 * EDG...  2.6 us
    pallas_call x1, Pallas kernels, local(): call(first_kernel, (shape(256, 128), shape(256, 128), shape(128, 2 * EDGE...  2.22 us
    pallas_call x1, Pallas kernels, local(): call(third_kernel, (shape(16, 128), shape(16, 128)), [IN_SMEM] * 2 + [IN_...  2.18 us
    unnamed x17, local copies, waits for them, and re-layouts  2.1 us
  transfers between devices with their start and end apart: 14, of which 13 were waited for; matrix products, arithmetic and copies ran while one was open for 1% of the time, Pallas kernels for 2%

profile of v4, /device:TPU:22, one launch (start us, length us, event | category | flops | bytes accessed | tf_op | source)
XLA Modules:
  0.0 96.2 jit_solution(11961261328929066113)
XLA Ops:
  0.6 1.4 %shard_map.140 = f32[24,128]{1,0:T(8,128)} custom-call(f32[3,1,128]{2,1,0:T(1,128)} %bitcast.27, s32[1,1,128]{2,1,0:T(1,128)} %refs_1_.1, s32[1,1,128]{2,1,0:T(1,128)} %refs_2_.1, s32[1,1,256]{2,1,0:T(1,128)} %refs_3_.1, s32[8,128]{1,0:T(8,128)} %bitcast.25, s32[8,128]{1,0:T(8,128)} %bitcast.26), custom_call_target="tpu_custom_call" | custom-call | flops 1000 | bytes 1048576 | tf_op jit(solution)/shard_map/pallas_call | solution.py:490
  2.1 5.1 %collective-permute-start = (f32[24,128]{1,0:T(8,128)}, f32[24,128]{1,0:T(8,128)S(1)}, u32[]{:S(2)}, u32[]{:S(2)}) collective-permute-start(f32[24,128]{1,0:T(8,128)} %shard_map.140), channel_id=1, source_target_pairs={{0,8},{1,9},{2,13},{3,12},{4,256},{5,257},{6,261},{7,260},{8,264},... | collective-permute-start | bytes 36872 | tf_op jit(solution)/shard_map/ppermute | solution.py:459
  7.1 11.0 %collective-permute-done.own_ref = f32[24,128]{1,0:T(8,128)S(1)} collective-permute-done((f32[24,128]{1,0:T(8,128)}, f32[24,128]{1,0:T(8,128)S(1)}, u32[]{:S(2)}, u32[]{:S(2)}) %collective-permute-start) | collective-permute-done | bytes 12320 | tf_op jit(solution)/shard_map/ppermute | solution.py:459
  18.2 2.0 %collective-permute-start.1 = (f32[8,128]{1,0:T(8,128)S(1)}, f32[8,128]{1,0:T(8,128)S(1)}, u32[]{:S(2)}, u32[]{:S(2)}) collective-permute-start(f32[8,128]{1,0:T(8,128)S(1)} %slice.70), channel_id=1, source_target_pairs={{24,8},{25,9},{29,13},{28,12},{272,256},{273,257},{277,261},{276,2... | collective-permute-start | bytes 12296 | tf_op jit(solution)/shard_map/ppermute | solution.py:459
  20.2 1.3 %collective-permute-done.1.x_ref = f32[8,128]{1,0:T(8,128)S(1)} collective-permute-done((f32[8,128]{1,0:T(8,128)S(1)}, f32[8,128]{1,0:T(8,128)S(1)}, u32[]{:S(2)}, u32[]{:S(2)}) %collective-permute-start.1) | collective-permute-done | bytes 4128 | tf_op jit(solution)/shard_map/ppermute | solution.py:459
  21.5 2.0 %collective-permute-start.2 = (f32[32,128]{1,0:T(8,128)S(1)}, f32[32,128]{1,0:T(8,128)S(1)}, u32[]{:S(2)}, u32[]{:S(2)}) collective-permute-start(f32[32,128]{1,0:T(8,128)S(1)} %pad_maximum_fusion.4), channel_id=1, source_target_pairs={{9,8},{13,9},{12,13},{256,12},{257,256},{261,257},{260,261},{264,2... | collective-permute-start | bytes 49160 | tf_op jit(solution)/shard_map/ppermute | solution.py:459
  23.5 0.0 copy-done.4
  23.6 0.0 copy-start.2
  23.6 0.7 copy-done.2
  24.3 0.1 copy.29
  24.4 2.8 %collective-permute-done.2.yc_ref = f32[32,128]{1,0:T(8,128)S(1)} collective-permute-done((f32[32,128]{1,0:T(8,128)S(1)}, f32[32,128]{1,0:T(8,128)S(1)}, u32[]{:S(2)}, u32[]{:S(2)}) %collective-permute-start.2) | collective-permute-done | bytes 16416 | tf_op jit(solution)/shard_map/ppermute | solution.py:459
  27.2 2.2 %shard_map.141 = (f32[256,128]{1,0:T(8,128)S(1)}, f32[256,128]{1,0:T(8,128)S(1)}, f32[128,2048]{1,0:T(8,128)S(1)}, f32[128,2048]{1,0:T(8,128)S(1)}, f32[32,2048]...) custom-call(f32[24,128]{1,0:T(8,128)S(1)} %collective-permute-done.own_ref, ...), custom_call_target="tpu_custom_call" | custom-call | flops 500000000 | bytes 1048576 | tf_op jit(solution)/shard_map/pallas_call | solution.py:524
  29.4 2.5 %collective-permute-start.3 = (f32[256,128]{1,0:T(8,128)S(1)}, f32[256,128]{1,0:T(8,128)S(1)}, u32[]{:S(2)}, u32[]{:S(2)}) collective-permute-start(f32[256,128]{1,0:T(8,128)S(1)} %get-tuple-element.46), channel_id=1, source_target_pairs={{27,8},{26,9},{30,13},{31,12},{275,256},{274,257},{278,261},{279,2... | collective-permute-start | bytes 393224 | tf_op jit(solution)/shard_map/ppermute | solution.py:468
  31.9 3.3 %collective-permute-start.4 = (f32[256,128]{1,0:T(8,128)S(1)}, f32[256,128]{1,0:T(8,128)S(1)}, u32[]{:S(2)}, u32[]{:S(2)}) collective-permute-start(f32[256,128]{1,0:T(8,128)S(1)} %get-tuple-element.47), channel_id=1, source_target_pairs={{24,8},{25,9},{29,13},{28,12},{272,256},{273,257},{277,261},{276,2... | collective-permute-start | bytes 393224 | tf_op jit(solution)/shard_map/ppermute | solution.py:468
  35.2 0.5 collective-permute-done.3
  35.7 0.4 collective-permute-done.4
  36.2 0.0 copy-start.6
  36.2 0.0 copy-start
  36.2 2.1 %collective-permute-start.5 = (f32[256,128]{1,0:T(8,128)S(1)}, f32[256,128]{1,0:T(8,128)S(1)}, u32[]{:S(2)}, u32[]{:S(2)}) collective-permute-start(f32[256,128]{1,0:T(8,128)S(1)} %get-tuple-element.45.one_ref), channel_id=1, source_target_pairs={{4,8},{13,9},{9,13},{256,12},{12,256},{261,257},{257,261},{264,260... | collective-permute-start | bytes 393224 | tf_op jit(solution)/shard_map/ppermute | solution.py:468
  38.4 2.9 %collective-permute-start.6 = (f32[256,128]{1,0:T(8,128)S(1)}, f32[256,128]{1,0:T(8,128)S(1)}, u32[]{:S(2)}, u32[]{:S(2)}) collective-permute-start(f32[256,128]{1,0:T(8,128)S(1)} %get-tuple-element.44.two_ref), channel_id=1, source_target_pairs={{9,8},{8,9},{12,13},{13,12},{257,256},{256,257},{260,261},{261,260... | collective-permute-start | bytes 393224 | tf_op jit(solution)/shard_map/ppermute | solution.py:468
  41.3 0.1 copy.31.wout_ref
  41.4 0.0 copy-start.1
  41.4 0.1 copy.30
  41.5 0.7 copy-done.1
  42.2 0.1 copy.32.wten_t_ref
  42.3 1.0 %shard_map.142 = (f32[128,2048]{1,0:T(8,128)S(1)}, f32[8,2048]{1,0:T(8,128)S(1)}) custom-call(s32[1]{0:T(128)} %get-tuple-element.17.count_ref, f32[128,2048]{1,0:T(8,128)S(1)} %get-tuple-element.20.lat_ref, f32[128,128]{1,0:T(8,128)S(1)} %bitcast.19, f32[128,1]{1,0:T(8,128)S(1)} %copy.31.wout_ref), custom_call_target="tpu_custom_call" | custom-call | flops 200000000 | bytes 1048576 | tf_op jit(solution)/shard_map/pallas_call | solution.py:536
  43.3 0.9 collective-permute-done.5.one_in_ref
  44.2 2.1 %collective-permute-done.6.two_in_ref = f32[256,128]{1,0:T(8,128)S(1)} collective-permute-done((f32[256,128]{1,0:T(8,128)S(1)}, f32[256,128]{1,0:T(8,128)S(1)}, u32[]{:S(2)}, u32[]{:S(2)}) %collective-permute-start.6) | collective-permute-done | bytes 131104 | tf_op jit(solution)/shard_map/ppermute | solution.py:468
  46.3 2.6 %shard_map.143 = (f32[256,128]{1,0:T(8,128)S(1)}, f32[256,128]{1,0:T(8,128)S(1)}, f32[128,2048]{1,0:T(8,128)S(1)}, f32[8,2048]{1,0:T(8,128)S(1)}) custom-call(s32[1]{0:T(128)} %get-tuple-element.17.count_ref, s32[1]{0:T(128)} %bitcast.7.odd_ref, f32[256,128]{1,0:T(8,128)S(1)} %get-tuple-element.45.one_ref, f32[256,128]{1,0:T(8,128)S(1)} %get-tuple-element.44.two_ref, ...), custom_call_target="tpu_custom_call" | custom-call | flops 1000000000 | bytes 1048576 | tf_op jit(solution)/shard_map/pallas_call | solution.py:544
  48.9 1.9 %collective-permute-start.7 = (f32[256,128]{1,0:T(8,128)S(1)}, f32[256,128]{1,0:T(8,128)S(1)}, u32[]{:S(2)}, u32[]{:S(2)}) collective-permute-start(f32[256,128]{1,0:T(8,128)S(1)} %get-tuple-element.42), channel_id=1, source_target_pairs={{27,8},{26,9},{30,13},{31,12},{275,256},{274,257},{278,261},{279,2... | collective-permute-start | bytes 393224 | tf_op jit(solution)/shard_map/ppermute | solution.py:468
  50.8 3.6 %collective-permute-start.8 = (f32[256,128]{1,0:T(8,128)S(1)}, f32[256,128]{1,0:T(8,128)S(1)}, u32[]{:S(2)}, u32[]{:S(2)}) collective-permute-start(f32[256,128]{1,0:T(8,128)S(1)} %get-tuple-element.43), channel_id=1, source_target_pairs={{24,8},{25,9},{29,13},{28,12},{272,256},{273,257},{277,261},{276,2... | collective-permute-start | bytes 393224 | tf_op jit(solution)/shard_map/ppermute | solution.py:468
  54.4 0.7 collective-permute-done.7
  55.2 0.2 collective-permute-done.8
  55.5 2.8 %collective-permute-start.10 = (f32[256,128]{1,0:T(8,128)S(1)}, f32[256,128]{1,0:T(8,128)S(1)}, u32[]{:S(2)}, u32[]{:S(2)}) collective-permute-start(f32[256,128]{1,0:T(8,128)S(1)} %get-tuple-element.40.two_ref), channel_id=1, source_target_pairs={{9,8},{8,9},{12,13},{13,12},{257,256},{256,257},{260,261},{261,260... | collective-permute-start | bytes 393224 | tf_op jit(solution)/shard_map/ppermute | solution.py:468
  58.4 2.9 %collective-permute-start.9 = (f32[256,128]{1,0:T(8,128)S(1)}, f32[256,128]{1,0:T(8,128)S(1)}, u32[]{:S(2)}, u32[]{:S(2)}) collective-permute-start(f32[256,128]{1,0:T(8,128)S(1)} %get-tuple-element.41.one_ref), channel_id=1, source_target_pairs={{4,8},{13,9},{9,13},{256,12},{12,256},{261,257},{257,261},{264,260... | collective-permute-start | bytes 393224 | tf_op jit(solution)/shard_map/ppermute | solution.py:468
  61.3 0.1 copy.35.wenv_ref
  61.4 1.0 %shard_map.144.glat_ref = f32[128,2048]{1,0:T(8,128)S(1)} custom-call(s32[1]{0:T(128)} %get-tuple-element.17.count_ref, f32[128,2048]{1,0:T(8,128)S(1)} %get-tuple-element.28.gpre_ref, f32[16,2048]{1,0:T(8,128)S(1)} %get-tuple-element.23.geo_ref, f32[128,128]{1,0:T(8,128)S(1)} %copy-done, f32[128,1]{1,0:T(8,128)S(1)} %copy.31.wout_ref), custom_call_target="tpu_custom_call" | custom-call | flops 200000000 | bytes 1048576 | tf_op jit(solution)/shard_map/pallas_call | solution.py:552
  62.4 1.1 %collective-permute-done.10.two_in_ref = f32[256,128]{1,0:T(8,128)S(1)} collective-permute-done((f32[256,128]{1,0:T(8,128)S(1)}, f32[256,128]{1,0:T(8,128)S(1)}, u32[]{:S(2)}, u32[]{:S(2)}) %collective-permute-start.10) | collective-permute-done | bytes 131104 | tf_op jit(solution)/shard_map/ppermute | solution.py:468
  63.5 2.7 %collective-permute-done.9.one_in_ref = f32[256,128]{1,0:T(8,128)S(1)} collective-permute-done((f32[256,128]{1,0:T(8,128)S(1)}, f32[256,128]{1,0:T(8,128)S(1)}, u32[]{:S(2)}, u32[]{:S(2)}) %collective-permute-start.9) | collective-permute-done | bytes 131104 | tf_op jit(solution)/shard_map/ppermute | solution.py:468
  66.2 2.2 %shard_map.145 = (f32[16,128]{1,0:T(8,128)S(1)}, f32[16,128]{1,0:T(8,128)S(1)}) custom-call(s32[1]{0:T(128)} %get-tuple-element.17.count_ref, s32[1]{0:T(128)} %bitcast.7.odd_ref, f32[256,128]{1,0:T(8,128)S(1)} %get-tuple-element.41.one_ref, f32[256,128]{1,0:T(8,128)S(1)} %get-tuple-element.40.two_ref, f32[256,128]{1,0:T(8,128)S(1)} %collective-permute-done.9.one_in_ref, ...), custom_call_target="tpu_custom_call" | custom-call | flops 500000000 | bytes 1048576 | tf_op jit(solution)/shard_map/pallas_call | solution.py:561
  68.4 3.5 %collective-permute-start.11 = (f32[16,128]{1,0:T(8,128)S(1)}, f32[16,128]{1,0:T(8,128)S(1)}, u32[]{:S(2)}, u32[]{:S(2)}) collective-permute-start(f32[16,128]{1,0:T(8,128)S(1)} %get-tuple-element.31), channel_id=1, source_target_pairs={{4,8},{8,9},{9,13},{13,12},{12,256},{256,257},{257,261},{261,260},... | collective-permute-start | bytes 24584 | tf_op jit(solution)/shard_map/ppermute | solution.py:459
  71.9 2.1 %collective-permute-done.11 = f32[16,128]{1,0:T(8,128)S(1)} collective-permute-done((f32[16,128]{1,0:T(8,128)S(1)}, f32[16,128]{1,0:T(8,128)S(1)}, u32[]{:S(2)}, u32[]{:S(2)}) %collective-permute-start.11) | collective-permute-done | bytes 8224 | tf_op jit(solution)/shard_map/ppermute | solution.py:459
  73.9 10.6 %collective-permute-start.12 = (f32[8,128]{1,0:T(8,128)S(1)}, f32[8,128]{1,0:T(8,128)S(1)}, u32[]{:S(2)}, u32[]{:S(2)}) collective-permute-start(f32[8,128]{1,0:T(8,128)S(1)} %get-tuple-element.57), channel_id=1, source_target_pairs={{27,0},{26,1},{30,2},{31,3},{275,4},{274,5},{278,6},{279,7},{283,8... | collective-permute-start | bytes 12296 | tf_op jit(solution)/shard_map/ppermute | solution.py:459
  84.5 3.6 %collective-permute-start.13 = (f32[8,128]{1,0:T(8,128)S(1)}, f32[8,128]{1,0:T(8,128)S(1)}, u32[]{:S(2)}, u32[]{:S(2)}) collective-permute-start(f32[8,128]{1,0:T(8,128)S(1)} %get-tuple-element.56), channel_id=1, source_target_pairs={{8,0},{9,1},{13,2},{12,3},{256,4},{257,5},{261,6},{260,7},{264,8},... | collective-permute-start | bytes 12296 | tf_op jit(solution)/shard_map/ppermute | solution.py:459
  88.2 0.0 collective-permute-done.12
  88.2 7.0 %collective-permute-done.13 = f32[8,128]{1,0:T(8,128)S(1)} collective-permute-done((f32[8,128]{1,0:T(8,128)S(1)}, f32[8,128]{1,0:T(8,128)S(1)}, u32[]{:S(2)}, u32[]{:S(2)}) %collective-permute-start.13) | collective-permute-done | bytes 4128 | tf_op jit(solution)/shard_map/ppermute | solution.py:459
  95.2 0.5 slice_bitcast_fusion.1
  95.7 0.6 copy.36
  (25 shorter events, 0.3 us)
Async XLA Ops:
  2.1 16.1 %collective-permute-start = (f32[24,128]{1,0:T(8,128)}, f32[24,128]{1,0:T(8,128)S(1)}, u32[]{:S(2)}, u32[]{:S(2)}) collective-permute-start(f32[24,128]{1,0:T(8,128)} %shard_map.140), channel_id=1, source_target_pairs={{0,8},{1,9},{2,13},{3,12},{4,256},{5,257},{6,261},{7,260},{8,264},... | collective-permute-start | bytes 36872 | tf_op jit(solution)/shard_map/ppermute | solution.py:459
  18.2 5.4 %copy-start.4 = (f32[2,128]{1,0:T(2,128)S(1)}, f32[2,128]{1,0:T(2,128)}, u32[]{:S(2)}) copy-start(f32[2,128]{1,0:T(2,128)} %param.21) | copy-start | bytes 3076
  18.2 5.4 %copy-start.5 = (f32[2,128]{1,0:T(2,128)S(1)}, f32[2,128]{1,0:T(2,128)}, u32[]{:S(2)}) copy-start(f32[2,128]{1,0:T(2,128)} %param.20) | copy-start | bytes 3076
  18.2 3.4 %collective-permute-start.1 = (f32[8,128]{1,0:T(8,128)S(1)}, f32[8,128]{1,0:T(8,128)S(1)}, u32[]{:S(2)}, u32[]{:S(2)}) collective-permute-start(f32[8,128]{1,0:T(8,128)S(1)} %slice.70), channel_id=1, source_target_pairs={{24,8},{25,9},{29,13},{28,12},{272,256},{273,257},{277,261},{276,2... | collective-permute-start | bytes 12296 | tf_op jit(solution)/shard_map/ppermute | solution.py:459
  21.5 5.6 %collective-permute-start.2 = (f32[32,128]{1,0:T(8,128)S(1)}, f32[32,128]{1,0:T(8,128)S(1)}, u32[]{:S(2)}, u32[]{:S(2)}) collective-permute-start(f32[32,128]{1,0:T(8,128)S(1)} %pad_maximum_fusion.4), channel_id=1, source_target_pairs={{9,8},{13,9},{12,13},{256,12},{257,256},{261,257},{260,261},{264,2... | collective-permute-start | bytes 49160 | tf_op jit(solution)/shard_map/ppermute | solution.py:459
  23.6 0.7 copy-start.2
  24.3 2.9 %copy-start.3 = (f32[128,32]{0,1:T(8,128)S(1)}, f32[128,32]{0,1:T(8,128)}, u32[]{:S(2)}) copy-start(f32[128,32]{0,1:T(8,128)} %param.22) | copy-start | bytes 49156
  29.4 6.3 %collective-permute-start.3 = (f32[256,128]{1,0:T(8,128)S(1)}, f32[256,128]{1,0:T(8,128)S(1)}, u32[]{:S(2)}, u32[]{:S(2)}) collective-permute-start(f32[256,128]{1,0:T(8,128)S(1)} %get-tuple-element.46), channel_id=1, source_target_pairs={{27,8},{26,9},{30,13},{31,12},{275,256},{274,257},{278,261},{279,2... | collective-permute-start | bytes 393224 | tf_op jit(solution)/shard_map/ppermute | solution.py:468
  31.9 4.2 %collective-permute-start.4 = (f32[256,128]{1,0:T(8,128)S(1)}, f32[256,128]{1,0:T(8,128)S(1)}, u32[]{:S(2)}, u32[]{:S(2)}) collective-permute-start(f32[256,128]{1,0:T(8,128)S(1)} %get-tuple-element.47), channel_id=1, source_target_pairs={{24,8},{25,9},{29,13},{28,12},{272,256},{273,257},{277,261},{276,2... | collective-permute-start | bytes 393224 | tf_op jit(solution)/shard_map/ppermute | solution.py:468
  36.2 5.1 %copy-start.6 = (f32[128]{0:T(128)S(1)}, f32[128]{0:T(128)}, u32[]{:S(2)}) copy-start(f32[128]{0:T(128)} %param.25) | copy-start | bytes 1540
  36.2 5.2 %copy-start = (f32[128,128]{1,0:T(8,128)S(1)}, f32[128,128]{1,0:T(8,128)}, u32[]{:S(2)}) copy-start(f32[128,128]{1,0:T(8,128)} %wlat_ref.1) | copy-start | bytes 196612
  36.2 7.9 %collective-permute-start.5 = (f32[256,128]{1,0:T(8,128)S(1)}, f32[256,128]{1,0:T(8,128)S(1)}, u32[]{:S(2)}, u32[]{:S(2)}) collective-permute-start(f32[256,128]{1,0:T(8,128)S(1)} %get-tuple-element.45.one_ref), channel_id=1, source_target_pairs={{4,8},{13,9},{9,13},{256,12},{12,256},{261,257},{257,261},{264,260... | collective-permute-start | bytes 393224 | tf_op jit(solution)/shard_map/ppermute | solution.py:468
  38.4 7.9 %collective-permute-start.6 = (f32[256,128]{1,0:T(8,128)S(1)}, f32[256,128]{1,0:T(8,128)S(1)}, u32[]{:S(2)}, u32[]{:S(2)}) collective-permute-start(f32[256,128]{1,0:T(8,128)S(1)} %get-tuple-element.44.two_ref), channel_id=1, source_target_pairs={{9,8},{8,9},{12,13},{13,12},{257,256},{256,257},{260,261},{261,260... | collective-permute-start | bytes 393224 | tf_op jit(solution)/shard_map/ppermute | solution.py:468
  41.4 0.8 copy-start.1
  48.9 6.3 %collective-permute-start.7 = (f32[256,128]{1,0:T(8,128)S(1)}, f32[256,128]{1,0:T(8,128)S(1)}, u32[]{:S(2)}, u32[]{:S(2)}) collective-permute-start(f32[256,128]{1,0:T(8,128)S(1)} %get-tuple-element.42), channel_id=1, source_target_pairs={{27,8},{26,9},{30,13},{31,12},{275,256},{274,257},{278,261},{279,2... | collective-permute-start | bytes 393224 | tf_op jit(solution)/shard_map/ppermute | solution.py:468
  50.8 4.6 %collective-permute-start.8 = (f32[256,128]{1,0:T(8,128)S(1)}, f32[256,128]{1,0:T(8,128)S(1)}, u32[]{:S(2)}, u32[]{:S(2)}) collective-permute-start(f32[256,128]{1,0:T(8,128)S(1)} %get-tuple-element.43), channel_id=1, source_target_pairs={{24,8},{25,9},{29,13},{28,12},{272,256},{273,257},{277,261},{276,2... | collective-permute-start | bytes 393224 | tf_op jit(solution)/shard_map/ppermute | solution.py:468
  55.5 8.0 %collective-permute-start.10 = (f32[256,128]{1,0:T(8,128)S(1)}, f32[256,128]{1,0:T(8,128)S(1)}, u32[]{:S(2)}, u32[]{:S(2)}) collective-permute-start(f32[256,128]{1,0:T(8,128)S(1)} %get-tuple-element.40.two_ref), channel_id=1, source_target_pairs={{9,8},{8,9},{12,13},{13,12},{257,256},{256,257},{260,261},{261,260... | collective-permute-start | bytes 393224 | tf_op jit(solution)/shard_map/ppermute | solution.py:468
  58.4 7.8 %collective-permute-start.9 = (f32[256,128]{1,0:T(8,128)S(1)}, f32[256,128]{1,0:T(8,128)S(1)}, u32[]{:S(2)}, u32[]{:S(2)}) collective-permute-start(f32[256,128]{1,0:T(8,128)S(1)} %get-tuple-element.41.one_ref), channel_id=1, source_target_pairs={{4,8},{13,9},{9,13},{256,12},{12,256},{261,257},{257,261},{264,260... | collective-permute-start | bytes 393224 | tf_op jit(solution)/shard_map/ppermute | solution.py:468
  68.4 5.6 %collective-permute-start.11 = (f32[16,128]{1,0:T(8,128)S(1)}, f32[16,128]{1,0:T(8,128)S(1)}, u32[]{:S(2)}, u32[]{:S(2)}) collective-permute-start(f32[16,128]{1,0:T(8,128)S(1)} %get-tuple-element.31), channel_id=1, source_target_pairs={{4,8},{8,9},{9,13},{13,12},{12,256},{256,257},{257,261},{261,260},... | collective-permute-start | bytes 24584 | tf_op jit(solution)/shard_map/ppermute | solution.py:459
  73.9 14.2 %collective-permute-start.12 = (f32[8,128]{1,0:T(8,128)S(1)}, f32[8,128]{1,0:T(8,128)S(1)}, u32[]{:S(2)}, u32[]{:S(2)}) collective-permute-start(f32[8,128]{1,0:T(8,128)S(1)} %get-tuple-element.57), channel_id=1, source_target_pairs={{27,0},{26,1},{30,2},{31,3},{275,4},{274,5},{278,6},{279,7},{283,8... | collective-permute-start | bytes 12296 | tf_op jit(solution)/shard_map/ppermute | solution.py:459
  84.5 10.6 %collective-permute-start.13 = (f32[8,128]{1,0:T(8,128)S(1)}, f32[8,128]{1,0:T(8,128)S(1)}, u32[]{:S(2)}, u32[]{:S(2)}) collective-permute-start(f32[8,128]{1,0:T(8,128)S(1)} %get-tuple-element.56), channel_id=1, source_target_pairs={{8,0},{9,1},{13,2},{12,3},{256,4},{257,5},{261,6},{260,7},{264,8},... | collective-permute-start | bytes 12296 | tf_op jit(solution)/shard_map/ppermute | solution.py:459

commit v5 on v4

--- a/solution.py
+++ b/solution.py
@@ -32,9 +32,7 @@
 def product(left, right):
     a, b = halves(left)
     c, d = halves(right)
-    rows = left.shape[0]
-    both = dot_nn(jnp.concatenate([a, b], axis=0), c)
-    return both[0:rows] + (both[rows:] + dot_nn(a, d))
+    return dot_nn(jnp.concatenate([a, a, b], axis=1), jnp.concatenate([c, d, c], axis=0))
 
 
 def one_hot(index_row, rows):
@@ -91,14 +89,7 @@
     return dx * inverse, dy * inverse, dz * inverse, envelope, radius
 
 
-def pack_kernel(*refs):
-    sources, own_ref, held, sems = refs[:6], refs[6], refs[7:13], refs[13]
-    copies = [pltpu.make_async_copy(source, place, sems.at[i]) for i, (source, place) in enumerate(zip(sources, held))]
-    for copy in copies:
-        copy.start()
-    for copy in copies:
-        copy.wait()
-    positions, species, counts, sends, neighbours, images = held
+def pack_kernel(positions, species, counts, sends, neighbours, images, own_ref):
     lists = sends[0].astype(F32)
     rows = [positions[0], positions[1], positions[2], species[0].astype(F32), lists[:, 0:ATOMS], lists[:, ATOMS:]]
     rows += [counts[0].astype(F32), jnp.zeros((1, ATOMS), F32)]
@@ -490,17 +481,9 @@
     own = call(
         pack_kernel,
         shape(24, ATOMS),
-        [pl.BlockSpec(memory_space=pl.ANY)] * 6,
+        [IN_VMEM] * 6,
         IN_VMEM,
-        [
-            pltpu.VMEM((3, 1, ATOMS), F32),
-            pltpu.VMEM((1, 1, ATOMS), jnp.int32),
-            pltpu.VMEM((1, 1, ATOMS), jnp.int32),
-            pltpu.VMEM((1, 1, 2 * ATOMS), jnp.int32),
-            pltpu.VMEM((SLOTS, ATOMS), jnp.int32),
-            pltpu.VMEM((SLOTS, ATOMS), jnp.int32),
-            pltpu.SemaphoreType.DMA((6,)),
-        ],
+        [],
         1000,
         60 * 1024 * 1024,
     )(

time: 97 us -> 96.5 us (level)
  no operation moved by 1% of the time
where the time goes in v5:
time: 96.5 us; the launch traced here: 95.8 us
  starting transfers between devices  48.8 us (51%)
  waiting for transfers between devices  32.8 us (34%)
  Pallas kernels  9.93 us (10%)
  local copies, waits for them, and re-layouts  3 us (3%)
  between operations  1.03 us (1%)
    ppermute x6, starting transfers between devices, move(): return lax.ppermute(block, ('gx', 'gy'), pairs)  26.8 us
    ppermute x6, waiting for transfers between devices, move(): return lax.ppermute(block, ('gx', 'gy'), pairs)  24.2 us
    ppermute x8, starting transfers between devices, trade(): return lax.ppermute(block, ('gx', 'gy'), pairs)  22 us
    ppermute x8, waiting for transfers between devices, trade(): return lax.ppermute(block, ('gx', 'gy'), pairs)  8.65 us
    pallas_call x1, Pallas kernels, local(): call(second_kernel, (shape(256, 128), shape(256, 128), shape(128, 2 * EDG...  2.45 us
    pallas_call x1, Pallas kernels, local(): call(first_kernel, (shape(256, 128), shape(256, 128), shape(128, 2 * EDGE...  2.12 us
    unnamed x17, local copies, waits for them, and re-layouts  2.1 us
    pallas_call x1, Pallas kernels, local(): call(third_kernel, (shape(16, 128), shape(16, 128)), [IN_SMEM] * 2 + [IN_...  2.01 us
  transfers between devices with their start and end apart: 14, of which 13 were waited for; matrix products, arithmetic and copies ran while one was open for 1% of the time, Pallas kernels for 2%

profile of v5, /device:TPU:22, one launch (start us, length us, event | category | flops | bytes accessed | tf_op | source)
XLA Modules:
  0.0 95.8 jit_solution(4569177230080880397)
XLA Ops:
  0.6 1.4 %shard_map.140 = f32[24,128]{1,0:T(8,128)} custom-call(f32[3,1,128]{2,1,0:T(1,128)} %bitcast.27, s32[1,1,128]{2,1,0:T(1,128)} %species.1, s32[1,1,128]{2,1,0:T(1,128)} %counts.1, s32[1,1,256]{2,1,0:T(1,128)} %sends.1, s32[8,128]{1,0:T(8,128)} %bitcast.25, s32[8,128]{1,0:T(8,128)} %bitcast.26), custom_call_target="tpu_custom_call" | custom-call | flops 1000 | bytes 1048576 | tf_op jit(solution)/shard_map/pallas_call | solution.py:481
  2.0 5.1 %collective-permute-start = (f32[24,128]{1,0:T(8,128)}, f32[24,128]{1,0:T(8,128)S(1)}, u32[]{:S(2)}, u32[]{:S(2)}) collective-permute-start(f32[24,128]{1,0:T(8,128)} %shard_map.140), channel_id=1, source_target_pairs={{0,8},{1,9},{2,13},{3,12},{4,256},{5,257},{6,261},{7,260},{8,264},... | collective-permute-start | bytes 36872 | tf_op jit(solution)/shard_map/ppermute | solution.py:450
  7.1 11.0 %collective-permute-done.own_ref = f32[24,128]{1,0:T(8,128)S(1)} collective-permute-done((f32[24,128]{1,0:T(8,128)}, f32[24,128]{1,0:T(8,128)S(1)}, u32[]{:S(2)}, u32[]{:S(2)}) %collective-permute-start) | collective-permute-done | bytes 12320 | tf_op jit(solution)/shard_map/ppermute | solution.py:450
  18.1 2.0 %collective-permute-start.1 = (f32[8,128]{1,0:T(8,128)S(1)}, f32[8,128]{1,0:T(8,128)S(1)}, u32[]{:S(2)}, u32[]{:S(2)}) collective-permute-start(f32[8,128]{1,0:T(8,128)S(1)} %slice.70), channel_id=1, source_target_pairs={{24,8},{25,9},{29,13},{28,12},{272,256},{273,257},{277,261},{276,2... | collective-permute-start | bytes 12296 | tf_op jit(solution)/shard_map/ppermute | solution.py:450
  20.1 1.3 %collective-permute-done.1.x_ref = f32[8,128]{1,0:T(8,128)S(1)} collective-permute-done((f32[8,128]{1,0:T(8,128)S(1)}, f32[8,128]{1,0:T(8,128)S(1)}, u32[]{:S(2)}, u32[]{:S(2)}) %collective-permute-start.1) | collective-permute-done | bytes 4128 | tf_op jit(solution)/shard_map/ppermute | solution.py:450
  21.5 2.0 %collective-permute-start.2 = (f32[32,128]{1,0:T(8,128)S(1)}, f32[32,128]{1,0:T(8,128)S(1)}, u32[]{:S(2)}, u32[]{:S(2)}) collective-permute-start(f32[32,128]{1,0:T(8,128)S(1)} %pad_maximum_fusion.4), channel_id=1, source_target_pairs={{9,8},{13,9},{12,13},{256,12},{257,256},{261,257},{260,261},{264,2... | collective-permute-start | bytes 49160 | tf_op jit(solution)/shard_map/ppermute | solution.py:450
  23.5 0.0 copy-start.2
  23.5 0.7 copy-done.2
  24.2 0.1 copy.29
  24.3 2.8 %collective-permute-done.2.yc_ref = f32[32,128]{1,0:T(8,128)S(1)} collective-permute-done((f32[32,128]{1,0:T(8,128)S(1)}, f32[32,128]{1,0:T(8,128)S(1)}, u32[]{:S(2)}, u32[]{:S(2)}) %collective-permute-start.2) | collective-permute-done | bytes 16416 | tf_op jit(solution)/shard_map/ppermute | solution.py:450
  27.1 2.1 %shard_map.141 = (f32[256,128]{1,0:T(8,128)S(1)}, f32[256,128]{1,0:T(8,128)S(1)}, f32[128,2048]{1,0:T(8,128)S(1)}, f32[128,2048]{1,0:T(8,128)S(1)}, f32[32,2048]...) custom-call(f32[24,128]{1,0:T(8,128)S(1)} %collective-permute-done.own_ref, ...), custom_call_target="tpu_custom_call" | custom-call | flops 500000000 | bytes 1048576 | tf_op jit(solution)/shard_map/pallas_call | solution.py:507
  29.2 2.5 %collective-permute-start.3 = (f32[256,128]{1,0:T(8,128)S(1)}, f32[256,128]{1,0:T(8,128)S(1)}, u32[]{:S(2)}, u32[]{:S(2)}) collective-permute-start(f32[256,128]{1,0:T(8,128)S(1)} %get-tuple-element.46), channel_id=1, source_target_pairs={{27,8},{26,9},{30,13},{31,12},{275,256},{274,257},{278,261},{279,2... | collective-permute-start | bytes 393224 | tf_op jit(solution)/shard_map/ppermute | solution.py:459
  31.7 3.3 %collective-permute-start.4 = (f32[256,128]{1,0:T(8,128)S(1)}, f32[256,128]{1,0:T(8,128)S(1)}, u32[]{:S(2)}, u32[]{:S(2)}) collective-permute-start(f32[256,128]{1,0:T(8,128)S(1)} %get-tuple-element.47), channel_id=1, source_target_pairs={{24,8},{25,9},{29,13},{28,12},{272,256},{273,257},{277,261},{276,2... | collective-permute-start | bytes 393224 | tf_op jit(solution)/shard_map/ppermute | solution.py:459
  35.1 0.5 collective-permute-done.3
  35.5 0.4 collective-permute-done.4
  36.0 0.0 copy-start.6
  36.0 0.0 copy-start
  36.1 2.1 %collective-permute-start.5 = (f32[256,128]{1,0:T(8,128)S(1)}, f32[256,128]{1,0:T(8,128)S(1)}, u32[]{:S(2)}, u32[]{:S(2)}) collective-permute-start(f32[256,128]{1,0:T(8,128)S(1)} %get-tuple-element.45.one_ref), channel_id=1, source_target_pairs={{4,8},{13,9},{9,13},{256,12},{12,256},{261,257},{257,261},{264,260... | collective-permute-start | bytes 393224 | tf_op jit(solution)/shard_map/ppermute | solution.py:459
  38.2 2.9 %collective-permute-start.6 = (f32[256,128]{1,0:T(8,128)S(1)}, f32[256,128]{1,0:T(8,128)S(1)}, u32[]{:S(2)}, u32[]{:S(2)}) collective-permute-start(f32[256,128]{1,0:T(8,128)S(1)} %get-tuple-element.44.two_ref), channel_id=1, source_target_pairs={{9,8},{8,9},{12,13},{13,12},{257,256},{256,257},{260,261},{261,260... | collective-permute-start | bytes 393224 | tf_op jit(solution)/shard_map/ppermute | solution.py:459
  41.1 0.0 copy-done.6
  41.1 0.1 copy.31.wout_ref
  41.2 0.0 copy-start.1
  41.2 0.1 copy.30
  41.3 0.7 copy-done.1
  42.0 0.1 copy.32.wten_t_ref
  42.1 1.0 %shard_map.142 = (f32[128,2048]{1,0:T(8,128)S(1)}, f32[8,2048]{1,0:T(8,128)S(1)}) custom-call(s32[1]{0:T(128)} %get-tuple-element.17.count_ref, f32[128,2048]{1,0:T(8,128)S(1)} %get-tuple-element.20.lat_ref, f32[128,128]{1,0:T(8,128)S(1)} %bitcast.19, f32[128,1]{1,0:T(8,128)S(1)} %copy.31.wout_ref), custom_call_target="tpu_custom_call" | custom-call | flops 200000000 | bytes 1048576 | tf_op jit(solution)/shard_map/pallas_call | solution.py:519
  43.1 0.9 collective-permute-done.5.one_in_ref
  44.0 2.1 %collective-permute-done.6.two_in_ref = f32[256,128]{1,0:T(8,128)S(1)} collective-permute-done((f32[256,128]{1,0:T(8,128)S(1)}, f32[256,128]{1,0:T(8,128)S(1)}, u32[]{:S(2)}, u32[]{:S(2)}) %collective-permute-start.6) | collective-permute-done | bytes 131104 | tf_op jit(solution)/shard_map/ppermute | solution.py:459
  46.1 2.5 %shard_map.143 = (f32[256,128]{1,0:T(8,128)S(1)}, f32[256,128]{1,0:T(8,128)S(1)}, f32[128,2048]{1,0:T(8,128)S(1)}, f32[8,2048]{1,0:T(8,128)S(1)}) custom-call(s32[1]{0:T(128)} %get-tuple-element.17.count_ref, s32[1]{0:T(128)} %bitcast.7.odd_ref, f32[256,128]{1,0:T(8,128)S(1)} %get-tuple-element.45.one_ref, f32[256,128]{1,0:T(8,128)S(1)} %get-tuple-element.44.two_ref, ...), custom_call_target="tpu_custom_call" | custom-call | flops 1000000000 | bytes 1048576 | tf_op jit(solution)/shard_map/pallas_call | solution.py:527
  48.6 1.9 %collective-permute-start.7 = (f32[256,128]{1,0:T(8,128)S(1)}, f32[256,128]{1,0:T(8,128)S(1)}, u32[]{:S(2)}, u32[]{:S(2)}) collective-permute-start(f32[256,128]{1,0:T(8,128)S(1)} %get-tuple-element.42), channel_id=1, source_target_pairs={{27,8},{26,9},{30,13},{31,12},{275,256},{274,257},{278,261},{279,2... | collective-permute-start | bytes 393224 | tf_op jit(solution)/shard_map/ppermute | solution.py:459
  50.5 3.6 %collective-permute-start.8 = (f32[256,128]{1,0:T(8,128)S(1)}, f32[256,128]{1,0:T(8,128)S(1)}, u32[]{:S(2)}, u32[]{:S(2)}) collective-permute-start(f32[256,128]{1,0:T(8,128)S(1)} %get-tuple-element.43), channel_id=1, source_target_pairs={{24,8},{25,9},{29,13},{28,12},{272,256},{273,257},{277,261},{276,2... | collective-permute-start | bytes 393224 | tf_op jit(solution)/shard_map/ppermute | solution.py:459
  54.1 0.8 collective-permute-done.7
  54.8 0.2 collective-permute-done.8
  55.2 2.9 %collective-permute-start.10 = (f32[256,128]{1,0:T(8,128)S(1)}, f32[256,128]{1,0:T(8,128)S(1)}, u32[]{:S(2)}, u32[]{:S(2)}) collective-permute-start(f32[256,128]{1,0:T(8,128)S(1)} %get-tuple-element.40.two_ref), channel_id=1, source_target_pairs={{9,8},{8,9},{12,13},{13,12},{257,256},{256,257},{260,261},{261,260... | collective-permute-start | bytes 393224 | tf_op jit(solution)/shard_map/ppermute | solution.py:459
  58.0 2.9 %collective-permute-start.9 = (f32[256,128]{1,0:T(8,128)S(1)}, f32[256,128]{1,0:T(8,128)S(1)}, u32[]{:S(2)}, u32[]{:S(2)}) collective-permute-start(f32[256,128]{1,0:T(8,128)S(1)} %get-tuple-element.41.one_ref), channel_id=1, source_target_pairs={{4,8},{13,9},{9,13},{256,12},{12,256},{261,257},{257,261},{264,260... | collective-permute-start | bytes 393224 | tf_op jit(solution)/shard_map/ppermute | solution.py:459
  60.9 0.1 copy.35.wenv_ref
  61.0 1.0 %shard_map.144.glat_ref = f32[128,2048]{1,0:T(8,128)S(1)} custom-call(s32[1]{0:T(128)} %get-tuple-element.17.count_ref, f32[128,2048]{1,0:T(8,128)S(1)} %get-tuple-element.28.gpre_ref, f32[16,2048]{1,0:T(8,128)S(1)} %get-tuple-element.23.geo_ref, f32[128,128]{1,0:T(8,128)S(1)} %copy-done, f32[128,1]{1,0:T(8,128)S(1)} %copy.31.wout_ref), custom_call_target="tpu_custom_call" | custom-call | flops 200000000 | bytes 1048576 | tf_op jit(solution)/shard_map/pallas_call | solution.py:535
  62.0 1.1 %collective-permute-done.10.two_in_ref = f32[256,128]{1,0:T(8,128)S(1)} collective-permute-done((f32[256,128]{1,0:T(8,128)S(1)}, f32[256,128]{1,0:T(8,128)S(1)}, u32[]{:S(2)}, u32[]{:S(2)}) %collective-permute-start.10) | collective-permute-done | bytes 131104 | tf_op jit(solution)/shard_map/ppermute | solution.py:459
  63.2 2.7 %collective-permute-done.9.one_in_ref = f32[256,128]{1,0:T(8,128)S(1)} collective-permute-done((f32[256,128]{1,0:T(8,128)S(1)}, f32[256,128]{1,0:T(8,128)S(1)}, u32[]{:S(2)}, u32[]{:S(2)}) %collective-permute-start.9) | collective-permute-done | bytes 131104 | tf_op jit(solution)/shard_map/ppermute | solution.py:459
  65.9 2.0 %shard_map.145 = (f32[16,128]{1,0:T(8,128)S(1)}, f32[16,128]{1,0:T(8,128)S(1)}) custom-call(s32[1]{0:T(128)} %get-tuple-element.17.count_ref, s32[1]{0:T(128)} %bitcast.7.odd_ref, f32[256,128]{1,0:T(8,128)S(1)} %get-tuple-element.41.one_ref, f32[256,128]{1,0:T(8,128)S(1)} %get-tuple-element.40.two_ref, f32[256,128]{1,0:T(8,128)S(1)} %collective-permute-done.9.one_in_ref, ...), custom_call_target="tpu_custom_call" | custom-call | flops 500000000 | bytes 1048576 | tf_op jit(solution)/shard_map/pallas_call | solution.py:544
  67.9 3.5 %collective-permute-start.11 = (f32[16,128]{1,0:T(8,128)S(1)}, f32[16,128]{1,0:T(8,128)S(1)}, u32[]{:S(2)}, u32[]{:S(2)}) collective-permute-start(f32[16,128]{1,0:T(8,128)S(1)} %get-tuple-element.31), channel_id=1, source_target_pairs={{4,8},{8,9},{9,13},{13,12},{12,256},{256,257},{257,261},{261,260},... | collective-permute-start | bytes 24584 | tf_op jit(solution)/shard_map/ppermute | solution.py:450
  71.3 2.1 %collective-permute-done.11 = f32[16,128]{1,0:T(8,128)S(1)} collective-permute-done((f32[16,128]{1,0:T(8,128)S(1)}, f32[16,128]{1,0:T(8,128)S(1)}, u32[]{:S(2)}, u32[]{:S(2)}) %collective-permute-start.11) | collective-permute-done | bytes 8224 | tf_op jit(solution)/shard_map/ppermute | solution.py:450
  73.4 10.6 %collective-permute-start.12 = (f32[8,128]{1,0:T(8,128)S(1)}, f32[8,128]{1,0:T(8,128)S(1)}, u32[]{:S(2)}, u32[]{:S(2)}) collective-permute-start(f32[8,128]{1,0:T(8,128)S(1)} %get-tuple-element.57), channel_id=1, source_target_pairs={{27,0},{26,1},{30,2},{31,3},{275,4},{274,5},{278,6},{279,7},{283,8... | collective-permute-start | bytes 12296 | tf_op jit(solution)/shard_map/ppermute | solution.py:450
  84.1 3.6 %collective-permute-start.13 = (f32[8,128]{1,0:T(8,128)S(1)}, f32[8,128]{1,0:T(8,128)S(1)}, u32[]{:S(2)}, u32[]{:S(2)}) collective-permute-start(f32[8,128]{1,0:T(8,128)S(1)} %get-tuple-element.56), channel_id=1, source_target_pairs={{8,0},{9,1},{13,2},{12,3},{256,4},{257,5},{261,6},{260,7},{264,8},... | collective-permute-start | bytes 12296 | tf_op jit(solution)/shard_map/ppermute | solution.py:450
  87.7 0.0 collective-permute-done.12
  87.7 7.0 %collective-permute-done.13 = f32[8,128]{1,0:T(8,128)S(1)} collective-permute-done((f32[8,128]{1,0:T(8,128)S(1)}, f32[8,128]{1,0:T(8,128)S(1)}, u32[]{:S(2)}, u32[]{:S(2)}) %collective-permute-start.13) | collective-permute-done | bytes 4128 | tf_op jit(solution)/shard_map/ppermute | solution.py:450
  94.7 0.5 slice_bitcast_fusion.1
  95.2 0.6 copy.36
  (25 shorter events, 0.3 us)
Async XLA Ops:
  2.0 16.1 %collective-permute-start = (f32[24,128]{1,0:T(8,128)}, f32[24,128]{1,0:T(8,128)S(1)}, u32[]{:S(2)}, u32[]{:S(2)}) collective-permute-start(f32[24,128]{1,0:T(8,128)} %shard_map.140), channel_id=1, source_target_pairs={{0,8},{1,9},{2,13},{3,12},{4,256},{5,257},{6,261},{7,260},{8,264},... | collective-permute-start | bytes 36872 | tf_op jit(solution)/shard_map/ppermute | solution.py:450
  18.1 5.4 %copy-start.4 = (f32[2,128]{1,0:T(2,128)S(1)}, f32[2,128]{1,0:T(2,128)}, u32[]{:S(2)}) copy-start(f32[2,128]{1,0:T(2,128)} %param.21) | copy-start | bytes 3076
  18.1 5.4 %copy-start.5 = (f32[2,128]{1,0:T(2,128)S(1)}, f32[2,128]{1,0:T(2,128)}, u32[]{:S(2)}) copy-start(f32[2,128]{1,0:T(2,128)} %param.20) | copy-start | bytes 3076
  18.1 3.4 %collective-permute-start.1 = (f32[8,128]{1,0:T(8,128)S(1)}, f32[8,128]{1,0:T(8,128)S(1)}, u32[]{:S(2)}, u32[]{:S(2)}) collective-permute-start(f32[8,128]{1,0:T(8,128)S(1)} %slice.70), channel_id=1, source_target_pairs={{24,8},{25,9},{29,13},{28,12},{272,256},{273,257},{277,261},{276,2... | collective-permute-start | bytes 12296 | tf_op jit(solution)/shard_map/ppermute | solution.py:450
  21.5 5.6 %collective-permute-start.2 = (f32[32,128]{1,0:T(8,128)S(1)}, f32[32,128]{1,0:T(8,128)S(1)}, u32[]{:S(2)}, u32[]{:S(2)}) collective-permute-start(f32[32,128]{1,0:T(8,128)S(1)} %pad_maximum_fusion.4), channel_id=1, source_target_pairs={{9,8},{13,9},{12,13},{256,12},{257,256},{261,257},{260,261},{264,2... | collective-permute-start | bytes 49160 | tf_op jit(solution)/shard_map/ppermute | solution.py:450
  23.5 0.7 copy-start.2
  24.2 2.9 %copy-start.3 = (f32[128,32]{0,1:T(8,128)S(1)}, f32[128,32]{0,1:T(8,128)}, u32[]{:S(2)}) copy-start(f32[128,32]{0,1:T(8,128)} %param.22) | copy-start | bytes 49156
  29.2 6.3 %collective-permute-start.3 = (f32[256,128]{1,0:T(8,128)S(1)}, f32[256,128]{1,0:T(8,128)S(1)}, u32[]{:S(2)}, u32[]{:S(2)}) collective-permute-start(f32[256,128]{1,0:T(8,128)S(1)} %get-tuple-element.46), channel_id=1, source_target_pairs={{27,8},{26,9},{30,13},{31,12},{275,256},{274,257},{278,261},{279,2... | collective-permute-start | bytes 393224 | tf_op jit(solution)/shard_map/ppermute | solution.py:459
  31.7 4.2 %collective-permute-start.4 = (f32[256,128]{1,0:T(8,128)S(1)}, f32[256,128]{1,0:T(8,128)S(1)}, u32[]{:S(2)}, u32[]{:S(2)}) collective-permute-start(f32[256,128]{1,0:T(8,128)S(1)} %get-tuple-element.47), channel_id=1, source_target_pairs={{24,8},{25,9},{29,13},{28,12},{272,256},{273,257},{277,261},{276,2... | collective-permute-start | bytes 393224 | tf_op jit(solution)/shard_map/ppermute | solution.py:459
  36.0 5.1 %copy-start.6 = (f32[128]{0:T(128)S(1)}, f32[128]{0:T(128)}, u32[]{:S(2)}) copy-start(f32[128]{0:T(128)} %param.25) | copy-start | bytes 1540
  36.0 5.2 %copy-start = (f32[128,128]{1,0:T(8,128)S(1)}, f32[128,128]{1,0:T(8,128)}, u32[]{:S(2)}) copy-start(f32[128,128]{1,0:T(8,128)} %wlat_ref.1) | copy-start | bytes 196612
  36.1 7.9 %collective-permute-start.5 = (f32[256,128]{1,0:T(8,128)S(1)}, f32[256,128]{1,0:T(8,128)S(1)}, u32[]{:S(2)}, u32[]{:S(2)}) collective-permute-start(f32[256,128]{1,0:T(8,128)S(1)} %get-tuple-element.45.one_ref), channel_id=1, source_target_pairs={{4,8},{13,9},{9,13},{256,12},{12,256},{261,257},{257,261},{264,260... | collective-permute-start | bytes 393224 | tf_op jit(solution)/shard_map/ppermute | solution.py:459
  38.2 7.9 %collective-permute-start.6 = (f32[256,128]{1,0:T(8,128)S(1)}, f32[256,128]{1,0:T(8,128)S(1)}, u32[]{:S(2)}, u32[]{:S(2)}) collective-permute-start(f32[256,128]{1,0:T(8,128)S(1)} %get-tuple-element.44.two_ref), channel_id=1, source_target_pairs={{9,8},{8,9},{12,13},{13,12},{257,256},{256,257},{260,261},{261,260... | collective-permute-start | bytes 393224 | tf_op jit(solution)/shard_map/ppermute | solution.py:459
  41.2 0.8 copy-start.1
  48.6 6.3 %collective-permute-start.7 = (f32[256,128]{1,0:T(8,128)S(1)}, f32[256,128]{1,0:T(8,128)S(1)}, u32[]{:S(2)}, u32[]{:S(2)}) collective-permute-start(f32[256,128]{1,0:T(8,128)S(1)} %get-tuple-element.42), channel_id=1, source_target_pairs={{27,8},{26,9},{30,13},{31,12},{275,256},{274,257},{278,261},{279,2... | collective-permute-start | bytes 393224 | tf_op jit(solution)/shard_map/ppermute | solution.py:459
  50.5 4.6 %collective-permute-start.8 = (f32[256,128]{1,0:T(8,128)S(1)}, f32[256,128]{1,0:T(8,128)S(1)}, u32[]{:S(2)}, u32[]{:S(2)}) collective-permute-start(f32[256,128]{1,0:T(8,128)S(1)} %get-tuple-element.43), channel_id=1, source_target_pairs={{24,8},{25,9},{29,13},{28,12},{272,256},{273,257},{277,261},{276,2... | collective-permute-start | bytes 393224 | tf_op jit(solution)/shard_map/ppermute | solution.py:459
  55.2 8.0 %collective-permute-start.10 = (f32[256,128]{1,0:T(8,128)S(1)}, f32[256,128]{1,0:T(8,128)S(1)}, u32[]{:S(2)}, u32[]{:S(2)}) collective-permute-start(f32[256,128]{1,0:T(8,128)S(1)} %get-tuple-element.40.two_ref), channel_id=1, source_target_pairs={{9,8},{8,9},{12,13},{13,12},{257,256},{256,257},{260,261},{261,260... | collective-permute-start | bytes 393224 | tf_op jit(solution)/shard_map/ppermute | solution.py:459
  58.0 7.8 %collective-permute-start.9 = (f32[256,128]{1,0:T(8,128)S(1)}, f32[256,128]{1,0:T(8,128)S(1)}, u32[]{:S(2)}, u32[]{:S(2)}) collective-permute-start(f32[256,128]{1,0:T(8,128)S(1)} %get-tuple-element.41.one_ref), channel_id=1, source_target_pairs={{4,8},{13,9},{9,13},{256,12},{12,256},{261,257},{257,261},{264,260... | collective-permute-start | bytes 393224 | tf_op jit(solution)/shard_map/ppermute | solution.py:459
  67.9 5.6 %collective-permute-start.11 = (f32[16,128]{1,0:T(8,128)S(1)}, f32[16,128]{1,0:T(8,128)S(1)}, u32[]{:S(2)}, u32[]{:S(2)}) collective-permute-start(f32[16,128]{1,0:T(8,128)S(1)} %get-tuple-element.31), channel_id=1, source_target_pairs={{4,8},{8,9},{9,13},{13,12},{12,256},{256,257},{257,261},{261,260},... | collective-permute-start | bytes 24584 | tf_op jit(solution)/shard_map/ppermute | solution.py:450
  73.4 14.2 %collective-permute-start.12 = (f32[8,128]{1,0:T(8,128)S(1)}, f32[8,128]{1,0:T(8,128)S(1)}, u32[]{:S(2)}, u32[]{:S(2)}) collective-permute-start(f32[8,128]{1,0:T(8,128)S(1)} %get-tuple-element.57), channel_id=1, source_target_pairs={{27,0},{26,1},{30,2},{31,3},{275,4},{274,5},{278,6},{279,7},{283,8... | collective-permute-start | bytes 12296 | tf_op jit(solution)/shard_map/ppermute | solution.py:450
  84.1 10.6 %collective-permute-start.13 = (f32[8,128]{1,0:T(8,128)S(1)}, f32[8,128]{1,0:T(8,128)S(1)}, u32[]{:S(2)}, u32[]{:S(2)}) collective-permute-start(f32[8,128]{1,0:T(8,128)S(1)} %get-tuple-element.56), channel_id=1, source_target_pairs={{8,0},{9,1},{13,2},{12,3},{256,4},{257,5},{261,6},{260,7},{264,8},... | collective-permute-start | bytes 12296 | tf_op jit(solution)/shard_map/ppermute | solution.py:450

commit v6 on v5

--- a/solution.py
+++ b/solution.py
@@ -396,6 +396,21 @@
         return carry
 
     lax.fori_loop(1, blocks, lone, 0)
+
+
+def unpack_kernel(one_ref, two_ref, forces_ref, energy_ref, three, single, sems):
+    total = one_ref[...] + two_ref[...]
+    for comp in range(3):
+        three[comp] = total[comp : comp + 1]
+    single[0] = total[3:4]
+    copies = [
+        pltpu.make_async_copy(three, forces_ref, sems.at[0]),
+        pltpu.make_async_copy(single, energy_ref, sems.at[1]),
+    ]
+    for copy in copies:
+        copy.start()
+    for copy in copies:
+        copy.wait()
 
 
 def call(kernel, out_shape, in_specs, out_specs, scratch, cost, limit=VMEM_LIMIT):
@@ -550,8 +565,17 @@
         500_000_000,
     )(count, odd, one, two, one_in, two_in, dlat, wl, glat, geo, rows, w_env, w_basis)
     ox = ox + move(yc, at_work, at_work, (0, -1))
-    total = move(ox[8:16], at_work, at_home, (-1, 0)) + move(ox[0:8], at_work, at_home, (0, 0))
-    return (total[0:3][None, None], total[3][None, None])
+    from_left = move(ox[8:16], at_work, at_home, (-1, 0))
+    kept = move(ox[0:8], at_work, at_home, (0, 0))
+    forces, energy = call(
+        unpack_kernel,
+        (shape(3, 1, ATOMS), shape(1, 1, ATOMS)),
+        [IN_VMEM] * 2,
+        (pl.BlockSpec(memory_space=pl.ANY),) * 2,
+        [pltpu.VMEM((3, 1, ATOMS), F32), pltpu.VMEM((1, 1, ATOMS), F32), pltpu.SemaphoreType.DMA((2,))],
+        1000,
+    )(from_left, kept)
+    return (forces.reshape(1, 3, 1, ATOMS).transpose(0, 2, 1, 3), energy)
 
 
 def solution(mesh):

time: 96.5 us -> 96 us (level)
  local copies, waits for them, and re-layouts: 3 us -> 1.91 us
    unnamed x17 -> x16, local copies, waits for them, and re-layouts: 2.1 us -> 1.54 us
where the time goes in v6:
time: 96 us; the launch traced here: 95.3 us
  starting transfers between devices  48.8 us (51%)
  waiting for transfers between devices  32.8 us (34%)
  Pallas kernels  10.5 us (11%)
  local copies, waits for them, and re-layouts  1.91 us (2%)
  between operations  1.03 us (1%)
    ppermute x6, starting transfers between devices, move(): return lax.ppermute(block, ('gx', 'gy'), pairs)  26.8 us
    ppermute x6, waiting for transfers between devices, move(): return lax.ppermute(block, ('gx', 'gy'), pairs)  24.2 us
    ppermute x8, starting transfers between devices, trade(): return lax.ppermute(block, ('gx', 'gy'), pairs)  22 us
    ppermute x8, waiting for transfers between devices, trade(): return lax.ppermute(block, ('gx', 'gy'), pairs)  8.64 us
    pallas_call x1, Pallas kernels, local(): call(second_kernel, (shape(256, 128), shape(256, 128), shape(128, 2 * EDG...  2.45 us
    pallas_call x1, Pallas kernels, local(): call(first_kernel, (shape(256, 128), shape(256, 128), shape(128, 2 * EDGE...  2.12 us
    pallas_call x1, Pallas kernels, local(): call(third_kernel, (shape(16, 128), shape(16, 128)), [IN_SMEM] * 2 + [IN_...  2.01 us
  transfers between devices with their start and end apart: 14, of which 13 were waited for; matrix products, arithmetic and copies ran while one was open for 1% of the time, Pallas kernels for 2%

profile of v6, /device:TPU:22, one launch (start us, length us, event | category | flops | bytes accessed | tf_op | source)
XLA Modules:
  0.0 95.3 jit_solution(14634663747721317363)
XLA Ops:
  0.6 1.4 %shard_map.140 = f32[24,128]{1,0:T(8,128)} custom-call(f32[3,1,128]{2,1,0:T(1,128)} %bitcast.26, s32[1,1,128]{2,1,0:T(1,128)} %species.1, s32[1,1,128]{2,1,0:T(1,128)} %counts.1, s32[1,1,256]{2,1,0:T(1,128)} %sends.1, s32[8,128]{1,0:T(8,128)} %bitcast.24, s32[8,128]{1,0:T(8,128)} %bitcast.25), custom_call_target="tpu_custom_call" | custom-call | flops 1000 | bytes 1048576 | tf_op jit(solution)/shard_map/pallas_call | solution.py:496
  2.0 5.1 %collective-permute-start = (f32[24,128]{1,0:T(8,128)}, f32[24,128]{1,0:T(8,128)S(1)}, u32[]{:S(2)}, u32[]{:S(2)}) collective-permute-start(f32[24,128]{1,0:T(8,128)} %shard_map.140), channel_id=1, source_target_pairs={{0,8},{1,9},{2,13},{3,12},{4,256},{5,257},{6,261},{7,260},{8,264},... | collective-permute-start | bytes 36872 | tf_op jit(solution)/shard_map/ppermute | solution.py:465
  7.1 11.0 %collective-permute-done.own_ref = f32[24,128]{1,0:T(8,128)S(1)} collective-permute-done((f32[24,128]{1,0:T(8,128)}, f32[24,128]{1,0:T(8,128)S(1)}, u32[]{:S(2)}, u32[]{:S(2)}) %collective-permute-start) | collective-permute-done | bytes 12320 | tf_op jit(solution)/shard_map/ppermute | solution.py:465
  18.1 2.0 %collective-permute-start.1 = (f32[8,128]{1,0:T(8,128)S(1)}, f32[8,128]{1,0:T(8,128)S(1)}, u32[]{:S(2)}, u32[]{:S(2)}) collective-permute-start(f32[8,128]{1,0:T(8,128)S(1)} %slice.62), channel_id=1, source_target_pairs={{24,8},{25,9},{29,13},{28,12},{272,256},{273,257},{277,261},{276,2... | collective-permute-start | bytes 12296 | tf_op jit(solution)/shard_map/ppermute | solution.py:465
  20.1 1.3 %collective-permute-done.1.x_ref = f32[8,128]{1,0:T(8,128)S(1)} collective-permute-done((f32[8,128]{1,0:T(8,128)S(1)}, f32[8,128]{1,0:T(8,128)S(1)}, u32[]{:S(2)}, u32[]{:S(2)}) %collective-permute-start.1) | collective-permute-done | bytes 4128 | tf_op jit(solution)/shard_map/ppermute | solution.py:465
  21.5 2.0 %collective-permute-start.2 = (f32[32,128]{1,0:T(8,128)S(1)}, f32[32,128]{1,0:T(8,128)S(1)}, u32[]{:S(2)}, u32[]{:S(2)}) collective-permute-start(f32[32,128]{1,0:T(8,128)S(1)} %pad_maximum_fusion.4), channel_id=1, source_target_pairs={{9,8},{13,9},{12,13},{256,12},{257,256},{261,257},{260,261},{264,2... | collective-permute-start | bytes 49160 | tf_op jit(solution)/shard_map/ppermute | solution.py:465
  23.5 0.0 copy-done.4
  23.5 0.0 copy-done.5
  23.5 0.0 copy-start.2
  23.5 0.7 copy-done.2
  24.2 0.1 copy.29
  24.3 2.8 %collective-permute-done.2.yc_ref = f32[32,128]{1,0:T(8,128)S(1)} collective-permute-done((f32[32,128]{1,0:T(8,128)S(1)}, f32[32,128]{1,0:T(8,128)S(1)}, u32[]{:S(2)}, u32[]{:S(2)}) %collective-permute-start.2) | collective-permute-done | bytes 16416 | tf_op jit(solution)/shard_map/ppermute | solution.py:465
  27.1 2.1 %shard_map.141 = (f32[256,128]{1,0:T(8,128)S(1)}, f32[256,128]{1,0:T(8,128)S(1)}, f32[128,2048]{1,0:T(8,128)S(1)}, f32[128,2048]{1,0:T(8,128)S(1)}, f32[32,2048]...) custom-call(f32[24,128]{1,0:T(8,128)S(1)} %collective-permute-done.own_ref, ...), custom_call_target="tpu_custom_call" | custom-call | flops 500000000 | bytes 1048576 | tf_op jit(solution)/shard_map/pallas_call | solution.py:522
  29.2 2.5 %collective-permute-start.3 = (f32[256,128]{1,0:T(8,128)S(1)}, f32[256,128]{1,0:T(8,128)S(1)}, u32[]{:S(2)}, u32[]{:S(2)}) collective-permute-start(f32[256,128]{1,0:T(8,128)S(1)} %get-tuple-element.50), channel_id=1, source_target_pairs={{27,8},{26,9},{30,13},{31,12},{275,256},{274,257},{278,261},{279,2... | collective-permute-start | bytes 393224 | tf_op jit(solution)/shard_map/ppermute | solution.py:474
  31.7 3.3 %collective-permute-start.4 = (f32[256,128]{1,0:T(8,128)S(1)}, f32[256,128]{1,0:T(8,128)S(1)}, u32[]{:S(2)}, u32[]{:S(2)}) collective-permute-start(f32[256,128]{1,0:T(8,128)S(1)} %get-tuple-element.51), channel_id=1, source_target_pairs={{24,8},{25,9},{29,13},{28,12},{272,256},{273,257},{277,261},{276,2... | collective-permute-start | bytes 393224 | tf_op jit(solution)/shard_map/ppermute | solution.py:474
  35.0 0.5 collective-permute-done.3
  35.5 0.4 collective-permute-done.4
  36.0 0.0 copy-start.6
  36.0 0.0 copy-start
  36.1 2.1 %collective-permute-start.5 = (f32[256,128]{1,0:T(8,128)S(1)}, f32[256,128]{1,0:T(8,128)S(1)}, u32[]{:S(2)}, u32[]{:S(2)}) collective-permute-start(f32[256,128]{1,0:T(8,128)S(1)} %get-tuple-element.49.one_ref), channel_id=1, source_target_pairs={{4,8},{13,9},{9,13},{256,12},{12,256},{261,257},{257,261},{264,260... | collective-permute-start | bytes 393224 | tf_op jit(solution)/shard_map/ppermute | solution.py:474
  38.2 2.9 %collective-permute-start.6 = (f32[256,128]{1,0:T(8,128)S(1)}, f32[256,128]{1,0:T(8,128)S(1)}, u32[]{:S(2)}, u32[]{:S(2)}) collective-permute-start(f32[256,128]{1,0:T(8,128)S(1)} %get-tuple-element.48.two_ref), channel_id=1, source_target_pairs={{9,8},{8,9},{12,13},{13,12},{257,256},{256,257},{260,261},{261,260... | collective-permute-start | bytes 393224 | tf_op jit(solution)/shard_map/ppermute | solution.py:474
  41.1 0.1 copy.31.wout_ref
  41.2 0.0 copy-start.1
  41.2 0.1 copy.30
  41.3 0.7 copy-done.1
  42.0 0.1 copy.32.wten_t_ref
  42.1 1.0 %shard_map.142 = (f32[128,2048]{1,0:T(8,128)S(1)}, f32[8,2048]{1,0:T(8,128)S(1)}) custom-call(s32[1]{0:T(128)} %get-tuple-element.19.count_ref, f32[128,2048]{1,0:T(8,128)S(1)} %get-tuple-element.22.lat_ref, f32[128,128]{1,0:T(8,128)S(1)} %bitcast.18, f32[128,1]{1,0:T(8,128)S(1)} %copy.31.wout_ref), custom_call_target="tpu_custom_call" | custom-call | flops 200000000 | bytes 1048576 | tf_op jit(solution)/shard_map/pallas_call | solution.py:534
  43.1 0.9 collective-permute-done.5.one_in_ref
  44.0 2.1 %collective-permute-done.6.two_in_ref = f32[256,128]{1,0:T(8,128)S(1)} collective-permute-done((f32[256,128]{1,0:T(8,128)S(1)}, f32[256,128]{1,0:T(8,128)S(1)}, u32[]{:S(2)}, u32[]{:S(2)}) %collective-permute-start.6) | collective-permute-done | bytes 131104 | tf_op jit(solution)/shard_map/ppermute | solution.py:474
  46.1 2.5 %shard_map.143 = (f32[256,128]{1,0:T(8,128)S(1)}, f32[256,128]{1,0:T(8,128)S(1)}, f32[128,2048]{1,0:T(8,128)S(1)}, f32[8,2048]{1,0:T(8,128)S(1)}) custom-call(s32[1]{0:T(128)} %get-tuple-element.19.count_ref, s32[1]{0:T(128)} %bitcast.7.odd_ref, f32[256,128]{1,0:T(8,128)S(1)} %get-tuple-element.49.one_ref, f32[256,128]{1,0:T(8,128)S(1)} %get-tuple-element.48.two_ref, ...), custom_call_target="tpu_custom_call" | custom-call | flops 1000000000 | bytes 1048576 | tf_op jit(solution)/shard_map/pallas_call | solution.py:542
  48.6 1.9 %collective-permute-start.7 = (f32[256,128]{1,0:T(8,128)S(1)}, f32[256,128]{1,0:T(8,128)S(1)}, u32[]{:S(2)}, u32[]{:S(2)}) collective-permute-start(f32[256,128]{1,0:T(8,128)S(1)} %get-tuple-element.46), channel_id=1, source_target_pairs={{27,8},{26,9},{30,13},{31,12},{275,256},{274,257},{278,261},{279,2... | collective-permute-start | bytes 393224 | tf_op jit(solution)/shard_map/ppermute | solution.py:474
  50.5 3.6 %collective-permute-start.8 = (f32[256,128]{1,0:T(8,128)S(1)}, f32[256,128]{1,0:T(8,128)S(1)}, u32[]{:S(2)}, u32[]{:S(2)}) collective-permute-start(f32[256,128]{1,0:T(8,128)S(1)} %get-tuple-element.47), channel_id=1, source_target_pairs={{24,8},{25,9},{29,13},{28,12},{272,256},{273,257},{277,261},{276,2... | collective-permute-start | bytes 393224 | tf_op jit(solution)/shard_map/ppermute | solution.py:474
  54.1 0.8 collective-permute-done.7
  54.8 0.2 collective-permute-done.8
  55.2 2.9 %collective-permute-start.10 = (f32[256,128]{1,0:T(8,128)S(1)}, f32[256,128]{1,0:T(8,128)S(1)}, u32[]{:S(2)}, u32[]{:S(2)}) collective-permute-start(f32[256,128]{1,0:T(8,128)S(1)} %get-tuple-element.44.two_ref), channel_id=1, source_target_pairs={{9,8},{8,9},{12,13},{13,12},{257,256},{256,257},{260,261},{261,260... | collective-permute-start | bytes 393224 | tf_op jit(solution)/shard_map/ppermute | solution.py:474
  58.0 2.9 %collective-permute-start.9 = (f32[256,128]{1,0:T(8,128)S(1)}, f32[256,128]{1,0:T(8,128)S(1)}, u32[]{:S(2)}, u32[]{:S(2)}) collective-permute-start(f32[256,128]{1,0:T(8,128)S(1)} %get-tuple-element.45.one_ref), channel_id=1, source_target_pairs={{4,8},{13,9},{9,13},{256,12},{12,256},{261,257},{257,261},{264,260... | collective-permute-start | bytes 393224 | tf_op jit(solution)/shard_map/ppermute | solution.py:474
  60.9 0.1 copy.35.wenv_ref
  61.0 1.0 %shard_map.144.glat_ref = f32[128,2048]{1,0:T(8,128)S(1)} custom-call(s32[1]{0:T(128)} %get-tuple-element.19.count_ref, f32[128,2048]{1,0:T(8,128)S(1)} %get-tuple-element.30.gpre_ref, f32[16,2048]{1,0:T(8,128)S(1)} %get-tuple-element.25.geo_ref, f32[128,128]{1,0:T(8,128)S(1)} %copy-done, f32[128,1]{1,0:T(8,128)S(1)} %copy.31.wout_ref), custom_call_target="tpu_custom_call" | custom-call | flops 200000000 | bytes 1048576 | tf_op jit(solution)/shard_map/pallas_call | solution.py:550
  62.0 1.1 %collective-permute-done.10.two_in_ref = f32[256,128]{1,0:T(8,128)S(1)} collective-permute-done((f32[256,128]{1,0:T(8,128)S(1)}, f32[256,128]{1,0:T(8,128)S(1)}, u32[]{:S(2)}, u32[]{:S(2)}) %collective-permute-start.10) | collective-permute-done | bytes 131104 | tf_op jit(solution)/shard_map/ppermute | solution.py:474
  63.2 2.7 %collective-permute-done.9.one_in_ref = f32[256,128]{1,0:T(8,128)S(1)} collective-permute-done((f32[256,128]{1,0:T(8,128)S(1)}, f32[256,128]{1,0:T(8,128)S(1)}, u32[]{:S(2)}, u32[]{:S(2)}) %collective-permute-start.9) | collective-permute-done | bytes 131104 | tf_op jit(solution)/shard_map/ppermute | solution.py:474
  65.8 2.0 %shard_map.145 = (f32[16,128]{1,0:T(8,128)S(1)}, f32[16,128]{1,0:T(8,128)S(1)}) custom-call(s32[1]{0:T(128)} %get-tuple-element.19.count_ref, s32[1]{0:T(128)} %bitcast.7.odd_ref, f32[256,128]{1,0:T(8,128)S(1)} %get-tuple-element.45.one_ref, f32[256,128]{1,0:T(8,128)S(1)} %get-tuple-element.44.two_ref, f32[256,128]{1,0:T(8,128)S(1)} %collective-permute-done.9.one_in_ref, ...), custom_call_target="tpu_custom_call" | custom-call | flops 500000000 | bytes 1048576 | tf_op jit(solution)/shard_map/pallas_call | solution.py:559
  67.9 3.5 %collective-permute-start.11 = (f32[16,128]{1,0:T(8,128)S(1)}, f32[16,128]{1,0:T(8,128)S(1)}, u32[]{:S(2)}, u32[]{:S(2)}) collective-permute-start(f32[16,128]{1,0:T(8,128)S(1)} %get-tuple-element.33), channel_id=1, source_target_pairs={{4,8},{8,9},{9,13},{13,12},{12,256},{256,257},{257,261},{261,260},... | collective-permute-start | bytes 24584 | tf_op jit(solution)/shard_map/ppermute | solution.py:465
  71.3 2.1 %collective-permute-done.11 = f32[16,128]{1,0:T(8,128)S(1)} collective-permute-done((f32[16,128]{1,0:T(8,128)S(1)}, f32[16,128]{1,0:T(8,128)S(1)}, u32[]{:S(2)}, u32[]{:S(2)}) %collective-permute-start.11) | collective-permute-done | bytes 8224 | tf_op jit(solution)/shard_map/ppermute | solution.py:465
  73.4 10.6 %collective-permute-start.12 = (f32[8,128]{1,0:T(8,128)S(1)}, f32[8,128]{1,0:T(8,128)S(1)}, u32[]{:S(2)}, u32[]{:S(2)}) collective-permute-start(f32[8,128]{1,0:T(8,128)S(1)} %get-tuple-element.61), channel_id=1, source_target_pairs={{27,0},{26,1},{30,2},{31,3},{275,4},{274,5},{278,6},{279,7},{283,8... | collective-permute-start | bytes 12296 | tf_op jit(solution)/shard_map/ppermute | solution.py:465
  84.1 3.6 %collective-permute-start.13 = (f32[8,128]{1,0:T(8,128)S(1)}, f32[8,128]{1,0:T(8,128)S(1)}, u32[]{:S(2)}, u32[]{:S(2)}) collective-permute-start(f32[8,128]{1,0:T(8,128)S(1)} %get-tuple-element.60), channel_id=1, source_target_pairs={{8,0},{9,1},{13,2},{12,3},{256,4},{257,5},{261,6},{260,7},{264,8},... | collective-permute-start | bytes 12296 | tf_op jit(solution)/shard_map/ppermute | solution.py:465
  87.7 0.0 collective-permute-done.12.one_ref
  87.7 7.0 %collective-permute-done.13.two_ref = f32[8,128]{1,0:T(8,128)S(1)} collective-permute-done((f32[8,128]{1,0:T(8,128)S(1)}, f32[8,128]{1,0:T(8,128)S(1)}, u32[]{:S(2)}, u32[]{:S(2)}) %collective-permute-start.13) | collective-permute-done | bytes 4128 | tf_op jit(solution)/shard_map/ppermute | solution.py:465
  94.7 0.6 shard_map.146
  (22 shorter events, 0.3 us)
Async XLA Ops:
  2.0 16.1 %collective-permute-start = (f32[24,128]{1,0:T(8,128)}, f32[24,128]{1,0:T(8,128)S(1)}, u32[]{:S(2)}, u32[]{:S(2)}) collective-permute-start(f32[24,128]{1,0:T(8,128)} %shard_map.140), channel_id=1, source_target_pairs={{0,8},{1,9},{2,13},{3,12},{4,256},{5,257},{6,261},{7,260},{8,264},... | collective-permute-start | bytes 36872 | tf_op jit(solution)/shard_map/ppermute | solution.py:465
  18.1 5.4 %copy-start.4 = (f32[2,128]{1,0:T(2,128)S(1)}, f32[2,128]{1,0:T(2,128)}, u32[]{:S(2)}) copy-start(f32[2,128]{1,0:T(2,128)} %param.21) | copy-start | bytes 3076
  18.1 5.4 %copy-start.5 = (f32[2,128]{1,0:T(2,128)S(1)}, f32[2,128]{1,0:T(2,128)}, u32[]{:S(2)}) copy-start(f32[2,128]{1,0:T(2,128)} %param.20) | copy-start | bytes 3076
  18.1 3.4 %collective-permute-start.1 = (f32[8,128]{1,0:T(8,128)S(1)}, f32[8,128]{1,0:T(8,128)S(1)}, u32[]{:S(2)}, u32[]{:S(2)}) collective-permute-start(f32[8,128]{1,0:T(8,128)S(1)} %slice.62), channel_id=1, source_target_pairs={{24,8},{25,9},{29,13},{28,12},{272,256},{273,257},{277,261},{276,2... | collective-permute-start | bytes 12296 | tf_op jit(solution)/shard_map/ppermute | solution.py:465
  21.5 5.6 %collective-permute-start.2 = (f32[32,128]{1,0:T(8,128)S(1)}, f32[32,128]{1,0:T(8,128)S(1)}, u32[]{:S(2)}, u32[]{:S(2)}) collective-permute-start(f32[32,128]{1,0:T(8,128)S(1)} %pad_maximum_fusion.4), channel_id=1, source_target_pairs={{9,8},{13,9},{12,13},{256,12},{257,256},{261,257},{260,261},{264,2... | collective-permute-start | bytes 49160 | tf_op jit(solution)/shard_map/ppermute | solution.py:465
  23.5 0.7 copy-start.2
  24.2 2.9 %copy-start.3 = (f32[128,32]{0,1:T(8,128)S(1)}, f32[128,32]{0,1:T(8,128)}, u32[]{:S(2)}) copy-start(f32[128,32]{0,1:T(8,128)} %param.22) | copy-start | bytes 49156
  29.2 6.3 %collective-permute-start.3 = (f32[256,128]{1,0:T(8,128)S(1)}, f32[256,128]{1,0:T(8,128)S(1)}, u32[]{:S(2)}, u32[]{:S(2)}) collective-permute-start(f32[256,128]{1,0:T(8,128)S(1)} %get-tuple-element.50), channel_id=1, source_target_pairs={{27,8},{26,9},{30,13},{31,12},{275,256},{274,257},{278,261},{279,2... | collective-permute-start | bytes 393224 | tf_op jit(solution)/shard_map/ppermute | solution.py:474
  31.7 4.2 %collective-permute-start.4 = (f32[256,128]{1,0:T(8,128)S(1)}, f32[256,128]{1,0:T(8,128)S(1)}, u32[]{:S(2)}, u32[]{:S(2)}) collective-permute-start(f32[256,128]{1,0:T(8,128)S(1)} %get-tuple-element.51), channel_id=1, source_target_pairs={{24,8},{25,9},{29,13},{28,12},{272,256},{273,257},{277,261},{276,2... | collective-permute-start | bytes 393224 | tf_op jit(solution)/shard_map/ppermute | solution.py:474
  36.0 5.1 %copy-start.6 = (f32[128]{0:T(128)S(1)}, f32[128]{0:T(128)}, u32[]{:S(2)}) copy-start(f32[128]{0:T(128)} %param.25) | copy-start | bytes 1540
  36.0 5.2 %copy-start = (f32[128,128]{1,0:T(8,128)S(1)}, f32[128,128]{1,0:T(8,128)}, u32[]{:S(2)}) copy-start(f32[128,128]{1,0:T(8,128)} %wlat_ref.1) | copy-start | bytes 196612
  36.1 7.9 %collective-permute-start.5 = (f32[256,128]{1,0:T(8,128)S(1)}, f32[256,128]{1,0:T(8,128)S(1)}, u32[]{:S(2)}, u32[]{:S(2)}) collective-permute-start(f32[256,128]{1,0:T(8,128)S(1)} %get-tuple-element.49.one_ref), channel_id=1, source_target_pairs={{4,8},{13,9},{9,13},{256,12},{12,256},{261,257},{257,261},{264,260... | collective-permute-start | bytes 393224 | tf_op jit(solution)/shard_map/ppermute | solution.py:474
  38.2 7.9 %collective-permute-start.6 = (f32[256,128]{1,0:T(8,128)S(1)}, f32[256,128]{1,0:T(8,128)S(1)}, u32[]{:S(2)}, u32[]{:S(2)}) collective-permute-start(f32[256,128]{1,0:T(8,128)S(1)} %get-tuple-element.48.two_ref), channel_id=1, source_target_pairs={{9,8},{8,9},{12,13},{13,12},{257,256},{256,257},{260,261},{261,260... | collective-permute-start | bytes 393224 | tf_op jit(solution)/shard_map/ppermute | solution.py:474
  41.2 0.8 copy-start.1
  48.6 6.3 %collective-permute-start.7 = (f32[256,128]{1,0:T(8,128)S(1)}, f32[256,128]{1,0:T(8,128)S(1)}, u32[]{:S(2)}, u32[]{:S(2)}) collective-permute-start(f32[256,128]{1,0:T(8,128)S(1)} %get-tuple-element.46), channel_id=1, source_target_pairs={{27,8},{26,9},{30,13},{31,12},{275,256},{274,257},{278,261},{279,2... | collective-permute-start | bytes 393224 | tf_op jit(solution)/shard_map/ppermute | solution.py:474
  50.5 4.6 %collective-permute-start.8 = (f32[256,128]{1,0:T(8,128)S(1)}, f32[256,128]{1,0:T(8,128)S(1)}, u32[]{:S(2)}, u32[]{:S(2)}) collective-permute-start(f32[256,128]{1,0:T(8,128)S(1)} %get-tuple-element.47), channel_id=1, source_target_pairs={{24,8},{25,9},{29,13},{28,12},{272,256},{273,257},{277,261},{276,2... | collective-permute-start | bytes 393224 | tf_op jit(solution)/shard_map/ppermute | solution.py:474
  55.2 8.0 %collective-permute-start.10 = (f32[256,128]{1,0:T(8,128)S(1)}, f32[256,128]{1,0:T(8,128)S(1)}, u32[]{:S(2)}, u32[]{:S(2)}) collective-permute-start(f32[256,128]{1,0:T(8,128)S(1)} %get-tuple-element.44.two_ref), channel_id=1, source_target_pairs={{9,8},{8,9},{12,13},{13,12},{257,256},{256,257},{260,261},{261,260... | collective-permute-start | bytes 393224 | tf_op jit(solution)/shard_map/ppermute | solution.py:474
  58.0 7.8 %collective-permute-start.9 = (f32[256,128]{1,0:T(8,128)S(1)}, f32[256,128]{1,0:T(8,128)S(1)}, u32[]{:S(2)}, u32[]{:S(2)}) collective-permute-start(f32[256,128]{1,0:T(8,128)S(1)} %get-tuple-element.45.one_ref), channel_id=1, source_target_pairs={{4,8},{13,9},{9,13},{256,12},{12,256},{261,257},{257,261},{264,260... | collective-permute-start | bytes 393224 | tf_op jit(solution)/shard_map/ppermute | solution.py:474
  67.9 5.6 %collective-permute-start.11 = (f32[16,128]{1,0:T(8,128)S(1)}, f32[16,128]{1,0:T(8,128)S(1)}, u32[]{:S(2)}, u32[]{:S(2)}) collective-permute-start(f32[16,128]{1,0:T(8,128)S(1)} %get-tuple-element.33), channel_id=1, source_target_pairs={{4,8},{8,9},{9,13},{13,12},{12,256},{256,257},{257,261},{261,260},... | collective-permute-start | bytes 24584 | tf_op jit(solution)/shard_map/ppermute | solution.py:465
  73.4 14.2 %collective-permute-start.12 = (f32[8,128]{1,0:T(8,128)S(1)}, f32[8,128]{1,0:T(8,128)S(1)}, u32[]{:S(2)}, u32[]{:S(2)}) collective-permute-start(f32[8,128]{1,0:T(8,128)S(1)} %get-tuple-element.61), channel_id=1, source_target_pairs={{27,0},{26,1},{30,2},{31,3},{275,4},{274,5},{278,6},{279,7},{283,8... | collective-permute-start | bytes 12296 | tf_op jit(solution)/shard_map/ppermute | solution.py:465
  84.1 10.6 %collective-permute-start.13 = (f32[8,128]{1,0:T(8,128)S(1)}, f32[8,128]{1,0:T(8,128)S(1)}, u32[]{:S(2)}, u32[]{:S(2)}) collective-permute-start(f32[8,128]{1,0:T(8,128)S(1)} %get-tuple-element.60), channel_id=1, source_target_pairs={{8,0},{9,1},{13,2},{12,3},{256,4},{257,5},{261,6},{260,7},{264,8},... | collective-permute-start | bytes 12296 | tf_op jit(solution)/shard_map/ppermute | solution.py:465
